TPU v7x, 32 devices: a whole 2x2x4 slice. The times are simulated.
32 devices in a mesh: groups: 2 (over y), dom: 4 (over z), segment: 2 (over x), chan: 2 (over core).
Axes of the slice: x: 2, y: 2, z: 4, core: 2. Of those that a mesh axis runs over, the one named last changes fastest.
Arguments:
- latents: bfloat16 [2, 4096, 256], P(None, ('groups', 'dom')), parts along dimension 1, may hold values from -6 to 6
- neighbors: int32 [6, 4096], P(None, ('groups', 'dom')), parts along dimension 1, may hold values from 0 to 511
- edge_coef: float32 [6, 4096], P(None, ('groups', 'dom')), parts along dimension 1, may hold values from 0.25 to 4
- cross_src: int32 [2, 2, 1024], P(None, None, ('groups', 'dom')), parts along dimension 2, may hold values from 0 to 511
- cross_coef: float32 [2, 2, 1024], P(None, None, ('groups', 'dom')), parts along dimension 2, may hold values from 0.25 to 10
- recv_node: int32 [2, 1024], P(None, ('groups', 'dom')), parts along dimension 1, may hold values from 0 to 511
- w_edge: bfloat16 [4, 256, 256], P('segment'), may hold values from -0.375 to 0.375
- w_node_in: bfloat16 [4, 512, 256], P('segment', None, 'chan'), may hold values from -0.044194174 to 0.044194174
- w_node_out: bfloat16 [4, 256, 256], P('segment', 'chan'), may hold values from -0.0625 to 0.0625
- edge_bias: bfloat16 [4, 256], P('segment'), may hold values from -3 to 3
- edge_gain: bfloat16 [4, 256], P('segment'), may hold values from -6 to 6
- node_bias: bfloat16 [4, 256], P('segment', 'chan'), may hold values from -3 to 3
- norm_gain: bfloat16 [4, 256], P('segment'), may hold values from 0.099609375 to 1.8984375
- norm_bias: bfloat16 [4, 256], P('segment'), may hold values from -3 to 3
Outputs:
- outputs: bfloat16 [2, 4096, 256], P('segment', ('groups', 'dom')), parts along dimension 1
There are 2 independent parts, one for each index of `groups`. A program takes and returns all parts, laid end to end along the dimension named above; an argument that names none is the same for every part. Nothing has to cross between parts.
Inputs may be any that keep to these rules, and one draw needn't show every extreme that they name: `neighbors`: rows of the node's own partition.
All inputs are finite; a program needn't handle non-finite values.
Results may differ from a plain program's by a relative error of at most 0.024.
Values may be sent and summed in bfloat16 or wider, within the bound.
No kernel may reach another device: no remote copies, remote signals or barrier semaphores. Data moves between devices by JAX's collectives and lax.ppermute only.
A program may use at most 64 MiB of HBM per device.

v0:
```python
import jax
import jax.numpy as jnp
from jax import lax
from jax.sharding import PartitionSpec as P


def from_partner(block, axis, bit):
    count = lax.axis_size(axis)
    route = []
    for low in range(count):
        high = low | 1 << bit
        if high != low and high < count:
            route += [(low, high), (high, low)]
    return lax.ppermute(block, axis, route)


def passed_along(value, axis, steps):
    count = lax.axis_size(axis)
    initial, last = (max(0, -steps), min(count, count - steps))
    return lax.ppermute(value, axis, [(source, source + steps) for source in range(initial, last)])


def broadcast(block, axis, source):
    block = jnp.where(lax.axis_index(axis) == source, block, jnp.zeros_like(block))
    return lax.psum(block, axis)


def edge_hidden(table, rows, coefs, gain):
    return jax.nn.relu(table[rows] + coefs[:, None] * gain[None, :])


def finish_norm(latent, mixed, norm_gain, norm_bias):
    mean = jnp.mean(mixed, axis=1, keepdims=True)
    centred = mixed - mean
    spread = jnp.mean(centred * centred, axis=1, keepdims=True)
    normed = centred * lax.rsqrt(spread + 1e-05) * norm_gain.astype(jnp.float32) + norm_bias.astype(
        jnp.float32
    )
    return (latent.astype(jnp.float32) + normed).astype(jnp.bfloat16)


def apply_layer(latent, params, graph):
    w_edge, w_node_in, w_node_out, edge_bias, edge_gain, node_bias, norm_gain, norm_bias = params
    neighbors, edge_coef, cross_src, cross_coef, recv_node = graph
    source = (
        jnp.dot(latent, w_edge, preferred_element_type=jnp.float32) + edge_bias.astype(jnp.float32)
    ).astype(jnp.bfloat16)
    source = lax.optimization_barrier(source).astype(jnp.float32)
    gain = edge_gain.astype(jnp.float32)
    summed = jnp.zeros(source.shape, jnp.float32)
    for k in range(neighbors.shape[0]):
        summed = summed + edge_hidden(source, neighbors[k], edge_coef[k], gain)
    for r in range(cross_src.shape[0]):
        partial_sum = jnp.zeros((cross_src.shape[2], source.shape[1]), jnp.float32)
        for x in range(cross_src.shape[1]):
            partial_sum = partial_sum + edge_hidden(source, cross_src[r, x], cross_coef[r, x], gain)
        arrived = from_partner(partial_sum.astype(jnp.bfloat16), "dom", r).astype(partial_sum.dtype)
        summed = summed.at[recv_node[r]].add(arrived)
    joined = jnp.concatenate([latent, summed.astype(jnp.bfloat16)], axis=1)
    hidden = jax.nn.relu(
        jnp.dot(joined, w_node_in, preferred_element_type=jnp.float32)
        + node_bias.astype(jnp.float32)
    ).astype(jnp.bfloat16)
    term = jnp.dot(hidden, w_node_out, preferred_element_type=jnp.float32)
    mixed = lax.psum(term.astype(jnp.bfloat16), "chan").astype(jnp.float32)
    return finish_norm(latent, mixed, norm_gain, norm_bias)


def run_layers(latent, params, graph):

    def one_layer(carry, layer_params):
        return (apply_layer(carry, layer_params, graph), None)

    result, unused = lax.scan(one_layer, latent, params)
    return result


def per_device(
    latents,
    neighbors,
    edge_coef,
    cross_src,
    cross_coef,
    recv_node,
    w_edge,
    w_node_in,
    w_node_out,
    edge_bias,
    edge_gain,
    node_bias,
    norm_gain,
    norm_bias,
):
    segments = lax.axis_size("segment")
    position = lax.axis_index("segment")
    graph = (neighbors, edge_coef, cross_src, cross_coef, recv_node)
    micro = latents.shape[0]
    share = micro // segments
    params = (w_edge, w_node_in, w_node_out, edge_bias, edge_gain, node_bias, norm_gain, norm_bias)

    def tick(carry, moment):
        previous, finished = carry
        incoming = passed_along(previous, "segment", 1)
        fresh = lax.dynamic_index_in_dim(latents, jnp.minimum(moment, micro - 1), 0, keepdims=False)
        current = jnp.where(position == 0, fresh, incoming)
        produced = run_layers(current, params, graph)
        target = jnp.clip(moment - (segments - 1), 0, micro - 1)
        older = lax.dynamic_index_in_dim(finished, target, 0, keepdims=False)
        keeping = jnp.logical_and(position == segments - 1, moment >= segments - 1)
        finished = lax.dynamic_update_index_in_dim(
            finished, jnp.where(keeping, produced, older), target, 0
        )
        return ((produced, finished), None)

    start = (jnp.zeros_like(latents[0]), jnp.zeros_like(latents))
    final_state, unused = lax.scan(tick, start, jnp.arange(micro + segments - 1, dtype=jnp.int32))
    everyone = broadcast(final_state[1], "segment", segments - 1)
    return lax.dynamic_slice_in_dim(everyone, position * share, share, 0)


def solution(mesh):
    return jax.shard_map(
        per_device,
        mesh=mesh,
        in_specs=(
            P(None, ("groups", "dom"), None),
            P(None, ("groups", "dom")),
            P(None, ("groups", "dom")),
            P(None, None, ("groups", "dom")),
            P(None, None, ("groups", "dom")),
            P(None, ("groups", "dom")),
            P("segment", None, None),
            P("segment", None, "chan"),
            P("segment", "chan", None),
            P("segment", None),
            P("segment", None),
            P("segment", "chan"),
            P("segment", None),
            P("segment", None),
        ),
        out_specs=P("segment", ("groups", "dom"), None),
        check_vma=False,
    )
```

profile of v0, /device:TPU:0, one launch (start us, length us, event | category | flops | bytes accessed | tf_op | source)
XLA Modules:
  0.0 379.2 jit_solution(1979387214330447219)
XLA Ops:
  7.5 330.3 %while.32 = (s32[]{:T(128)}, bf16[512,256]{1,0:T(8,128)(2,1)S(1)}, bf16[2,512,256]{2,1,0:T(8,128)(2,1)}, pred[]{:T(512)}, s32[3]{0:T(128)S(1)}, /*index=5*/bf16[...) while((s32[]{:T(128)}, bf16[512,256]{1,0:T(8,128)(2,1)S(1)}, ...), condition=%wide.region_8.9_spmd, body=%wide.region_0.8_spmd.sunk | while | flops 175463296 | bytes 25562392 | solution.py:116
  7.6 4.9 %collective-permute-start.2 = (bf16[512,256]{1,0:T(8,128)(2,1)S(1)}, bf16[512,256]{1,0:T(8,128)(2,1)S(1)}, u32[]{:S(2)}, u32[]{:S(2)}) collective-permute-start(bf16[512,256]{1,0:T(8,128)(2,1)S(1)} %get-tuple-element.812), channel_id=1, source_target_pairs={{0,2},{1,3},{4,6},{5,7},{8,10},{9,11},{12,14},{13,15},{16,18},{17,... | collective-permute-start | bytes 786440 | tf_op jit(solution)/shard_map/while/body/eval_jaxpr/ppermute | solution.py:20
  18.9 97.1 %while.33 = (s32[]{:T(128)}, bf16[512,256]{1,0:T(8,128)(2,1)S(1)}, bf16[2,256,256]{2,1,0:T(8,128)(2,1)}, bf16[2,256]{1,0:T(2,128)(2,1)S(1)}, s32[6,512]{1,0:T(8,...) while((s32[]{:T(128)}, bf16[512,256]{1,0:T(8,128)(2,1)S(1)}, ...), condition=%wide.region_7.7_spmd, body=%wide.region_1.6_spmd.sunk | while | flops 175201152 | bytes 22415360 | solution.py:74
  25.2 2.6 collective-permute-start.1
  37.0 2.2 gather_fusion
  42.1 1.8 scatter_custom_fusion.10
  44.0 1.8 scatter_custom_fusion.11
  48.7 16.9 %all-reduce.5.cloned.1.call-done = bf16[512,256]{1,0:T(8,128)(2,1)} async-done(((bf16[512,256]{1,0:T(8,128)(2,1)}), bf16[512,256]{1,0:T(8,128)(2,1)}) %all-reduce.5.cloned.1.call-update) | async-done | bytes 262160 | tf_op jit(solution)/shard_map/while/body/eval_jaxpr/while/body/eval_jaxpr/psum | solution.py:65
  74.4 2.4 collective-permute-start.1
  86.1 2.2 gather_fusion
  91.2 1.8 scatter_custom_fusion.10
  97.7 15.9 %all-reduce.5.cloned.1.call-done = bf16[512,256]{1,0:T(8,128)(2,1)} async-done(((bf16[512,256]{1,0:T(8,128)(2,1)}), bf16[512,256]{1,0:T(8,128)(2,1)}) %all-reduce.5.cloned.1.call-update) | async-done | bytes 262160 | tf_op jit(solution)/shard_map/while/body/eval_jaxpr/while/body/eval_jaxpr/psum | solution.py:65
  118.4 3.6 collective-permute-start.2
  129.0 96.8 %while.33 = (s32[]{:T(128)}, bf16[512,256]{1,0:T(8,128)(2,1)S(1)}, bf16[2,256,256]{2,1,0:T(8,128)(2,1)}, bf16[2,256]{1,0:T(2,128)(2,1)S(1)}, s32[6,512]{1,0:T(8,...) while((s32[]{:T(128)}, bf16[512,256]{1,0:T(8,128)(2,1)S(1)}, ...), condition=%wide.region_7.7_spmd, body=%wide.region_1.6_spmd.sunk | while | flops 175201152 | bytes 22415360 | solution.py:74
  135.2 2.4 collective-permute-start.1
  146.8 2.2 gather_fusion
  151.9 1.8 scatter_custom_fusion.10
  158.5 16.9 %all-reduce.5.cloned.1.call-done = bf16[512,256]{1,0:T(8,128)(2,1)} async-done(((bf16[512,256]{1,0:T(8,128)(2,1)}), bf16[512,256]{1,0:T(8,128)(2,1)}) %all-reduce.5.cloned.1.call-update) | async-done | bytes 262160 | tf_op jit(solution)/shard_map/while/body/eval_jaxpr/while/body/eval_jaxpr/psum | solution.py:65
  184.2 2.4 collective-permute-start.1
  195.8 2.2 gather_fusion
  202.8 1.8 scatter_custom_fusion.11
  207.5 15.9 %all-reduce.5.cloned.1.call-done = bf16[512,256]{1,0:T(8,128)(2,1)} async-done(((bf16[512,256]{1,0:T(8,128)(2,1)}), bf16[512,256]{1,0:T(8,128)(2,1)}) %all-reduce.5.cloned.1.call-update) | async-done | bytes 262160 | tf_op jit(solution)/shard_map/while/body/eval_jaxpr/while/body/eval_jaxpr/psum | solution.py:65
  228.1 3.6 collective-permute-start.2
  238.7 96.8 %while.33 = (s32[]{:T(128)}, bf16[512,256]{1,0:T(8,128)(2,1)S(1)}, bf16[2,256,256]{2,1,0:T(8,128)(2,1)}, bf16[2,256]{1,0:T(2,128)(2,1)S(1)}, s32[6,512]{1,0:T(8,...) while((s32[]{:T(128)}, bf16[512,256]{1,0:T(8,128)(2,1)S(1)}, ...), condition=%wide.region_7.7_spmd, body=%wide.region_1.6_spmd.sunk | while | flops 175201152 | bytes 22415360 | solution.py:74
  244.9 2.4 collective-permute-start.1
  256.5 2.2 gather_fusion
  261.6 1.8 scatter_custom_fusion.10
  268.2 16.9 %all-reduce.5.cloned.1.call-done = bf16[512,256]{1,0:T(8,128)(2,1)} async-done(((bf16[512,256]{1,0:T(8,128)(2,1)}), bf16[512,256]{1,0:T(8,128)(2,1)}) %all-reduce.5.cloned.1.call-update) | async-done | bytes 262160 | tf_op jit(solution)/shard_map/while/body/eval_jaxpr/while/body/eval_jaxpr/psum | solution.py:65
  293.9 2.4 collective-permute-start.1
  305.5 2.2 gather_fusion
  317.2 15.9 %all-reduce.5.cloned.1.call-done = bf16[512,256]{1,0:T(8,128)(2,1)} async-done(((bf16[512,256]{1,0:T(8,128)(2,1)}), bf16[512,256]{1,0:T(8,128)(2,1)}) %all-reduce.5.cloned.1.call-update) | async-done | bytes 262160 | tf_op jit(solution)/shard_map/while/body/eval_jaxpr/while/body/eval_jaxpr/psum | solution.py:65
  338.7 32.0 %all-reduce.3.cloned.1.call-done = bf16[2,512,256]{2,1,0:T(8,128)(2,1)} async-done(((bf16[2,512,256]{2,1,0:T(8,128)(2,1)}), bf16[2,512,256]{2,1,0:T(8,128)(2,1)}) %all-reduce.3.cloned.1.call-update) | async-done | bytes 524304 | tf_op jit(solution)/shard_map/psum | solution.py:25
  (480 shorter events, 176.3 us)
Async XLA Ops:
  7.5 4.9 %copy-start.22 = (s32[3]{0:T(128)}, s32[3]{0:T(128)S(1)}, u32[]{:S(2)}) copy-start(s32[3]{0:T(128)S(1)} %get-tuple-element.842) | copy-start | bytes 40 | tf_op jit(solution)/shard_map/while
  7.6 10.4 %collective-permute-start.2 = (bf16[512,256]{1,0:T(8,128)(2,1)S(1)}, bf16[512,256]{1,0:T(8,128)(2,1)S(1)}, u32[]{:S(2)}, u32[]{:S(2)}) collective-permute-start(bf16[512,256]{1,0:T(8,128)(2,1)S(1)} %get-tuple-element.812), channel_id=1, source_target_pairs={{0,2},{1,3},{4,6},{5,7},{8,10},{9,11},{12,14},{13,15},{16,18},{17,... | collective-permute-start | bytes 786440 | tf_op jit(solution)/shard_map/while/body/eval_jaxpr/ppermute | solution.py:20
  18.9 46.7 %all-reduce.5.cloned.1.call-start = ((), (), s32[]{:S(2)}) async-start(), calls=%async_computation.1 | async-start | bytes 524288 | tf_op jit(solution)/shard_map/while/body/eval_jaxpr/while/body/eval_jaxpr/psum | solution.py:65
  23.6 18.6 %collective-permute-start = (bf16[128,256]{1,0:T(8,128)(2,1)S(1)}, bf16[128,256]{1,0:T(8,128)(2,1)}, u32[]{:S(2)}, u32[]{:S(2)}) collective-permute-start(bf16[128,256]{1,0:T(8,128)(2,1)S(1)} %get-tuple-element.731), channel_id=1, source_target_pairs={{0,4},{4,0},{8,12},{12,8},{1,5},{5,1},{9,13},{13,9},{2,6},{6,2},{1... | collective-permute-start | bytes 196616 | tf_op jit(solution)/shard_map/while/body/eval_jaxpr/while/body/eval_jaxpr/ppermute | solution.py:14
  25.2 18.8 %collective-permute-start.1 = (bf16[128,256]{1,0:T(8,128)(2,1)S(1)}, bf16[128,256]{1,0:T(8,128)(2,1)}, u32[]{:S(2)}, u32[]{:S(2)}) collective-permute-start(bf16[128,256]{1,0:T(8,128)(2,1)S(1)} %get-tuple-element.733), channel_id=1, source_target_pairs={{0,8},{8,0},{4,12},{12,4},{1,9},{9,1},{5,13},{13,5},{2,10},{10,2},... | collective-permute-start | bytes 196616 | tf_op jit(solution)/shard_map/while/body/eval_jaxpr/while/body/eval_jaxpr/ppermute | solution.py:14
  46.8 1.2 copy-start.18
  65.6 1.2 copy-start
  68.1 45.5 %all-reduce.5.cloned.1.call-start = ((), (), s32[]{:S(2)}) async-start(), calls=%async_computation.1 | async-start | bytes 524288 | tf_op jit(solution)/shard_map/while/body/eval_jaxpr/while/body/eval_jaxpr/psum | solution.py:65
  72.6 18.6 %collective-permute-start = (bf16[128,256]{1,0:T(8,128)(2,1)S(1)}, bf16[128,256]{1,0:T(8,128)(2,1)}, u32[]{:S(2)}, u32[]{:S(2)}) collective-permute-start(bf16[128,256]{1,0:T(8,128)(2,1)S(1)} %get-tuple-element.731), channel_id=1, source_target_pairs={{0,4},{4,0},{8,12},{12,8},{1,5},{5,1},{9,13},{13,9},{2,6},{6,2},{1... | collective-permute-start | bytes 196616 | tf_op jit(solution)/shard_map/while/body/eval_jaxpr/while/body/eval_jaxpr/ppermute | solution.py:14
  74.4 18.6 %collective-permute-start.1 = (bf16[128,256]{1,0:T(8,128)(2,1)S(1)}, bf16[128,256]{1,0:T(8,128)(2,1)}, u32[]{:S(2)}, u32[]{:S(2)}) collective-permute-start(bf16[128,256]{1,0:T(8,128)(2,1)S(1)} %get-tuple-element.733), channel_id=1, source_target_pairs={{0,8},{8,0},{4,12},{12,4},{1,9},{9,1},{5,13},{13,5},{2,10},{10,2},... | collective-permute-start | bytes 196616 | tf_op jit(solution)/shard_map/while/body/eval_jaxpr/while/body/eval_jaxpr/ppermute | solution.py:14
  95.8 1.2 copy-start.18
  118.4 3.6 copy-start.22
  118.4 9.6 %collective-permute-start.2 = (bf16[512,256]{1,0:T(8,128)(2,1)S(1)}, bf16[512,256]{1,0:T(8,128)(2,1)S(1)}, u32[]{:S(2)}, u32[]{:S(2)}) collective-permute-start(bf16[512,256]{1,0:T(8,128)(2,1)S(1)} %get-tuple-element.812), channel_id=1, source_target_pairs={{0,2},{1,3},{4,6},{5,7},{8,10},{9,11},{12,14},{13,15},{16,18},{17,... | collective-permute-start | bytes 786440 | tf_op jit(solution)/shard_map/while/body/eval_jaxpr/ppermute | solution.py:20
  129.0 46.4 %all-reduce.5.cloned.1.call-start = ((), (), s32[]{:S(2)}) async-start(), calls=%async_computation.1 | async-start | bytes 524288 | tf_op jit(solution)/shard_map/while/body/eval_jaxpr/while/body/eval_jaxpr/psum | solution.py:65
  133.6 18.3 %collective-permute-start = (bf16[128,256]{1,0:T(8,128)(2,1)S(1)}, bf16[128,256]{1,0:T(8,128)(2,1)}, u32[]{:S(2)}, u32[]{:S(2)}) collective-permute-start(bf16[128,256]{1,0:T(8,128)(2,1)S(1)} %get-tuple-element.731), channel_id=1, source_target_pairs={{0,4},{4,0},{8,12},{12,8},{1,5},{5,1},{9,13},{13,9},{2,6},{6,2},{1... | collective-permute-start | bytes 196616 | tf_op jit(solution)/shard_map/while/body/eval_jaxpr/while/body/eval_jaxpr/ppermute | solution.py:14
  135.2 18.6 %collective-permute-start.1 = (bf16[128,256]{1,0:T(8,128)(2,1)S(1)}, bf16[128,256]{1,0:T(8,128)(2,1)}, u32[]{:S(2)}, u32[]{:S(2)}) collective-permute-start(bf16[128,256]{1,0:T(8,128)(2,1)S(1)} %get-tuple-element.733), channel_id=1, source_target_pairs={{0,8},{8,0},{4,12},{12,4},{1,9},{9,1},{5,13},{13,5},{2,10},{10,2},... | collective-permute-start | bytes 196616 | tf_op jit(solution)/shard_map/while/body/eval_jaxpr/while/body/eval_jaxpr/ppermute | solution.py:14
  156.6 1.2 copy-start.18
  177.8 45.5 %all-reduce.5.cloned.1.call-start = ((), (), s32[]{:S(2)}) async-start(), calls=%async_computation.1 | async-start | bytes 524288 | tf_op jit(solution)/shard_map/while/body/eval_jaxpr/while/body/eval_jaxpr/psum | solution.py:65
  182.4 18.6 %collective-permute-start = (bf16[128,256]{1,0:T(8,128)(2,1)S(1)}, bf16[128,256]{1,0:T(8,128)(2,1)}, u32[]{:S(2)}, u32[]{:S(2)}) collective-permute-start(bf16[128,256]{1,0:T(8,128)(2,1)S(1)} %get-tuple-element.731), channel_id=1, source_target_pairs={{0,4},{4,0},{8,12},{12,8},{1,5},{5,1},{9,13},{13,9},{2,6},{6,2},{1... | collective-permute-start | bytes 196616 | tf_op jit(solution)/shard_map/while/body/eval_jaxpr/while/body/eval_jaxpr/ppermute | solution.py:14
  184.2 18.6 %collective-permute-start.1 = (bf16[128,256]{1,0:T(8,128)(2,1)S(1)}, bf16[128,256]{1,0:T(8,128)(2,1)}, u32[]{:S(2)}, u32[]{:S(2)}) collective-permute-start(bf16[128,256]{1,0:T(8,128)(2,1)S(1)} %get-tuple-element.733), channel_id=1, source_target_pairs={{0,8},{8,0},{4,12},{12,4},{1,9},{9,1},{5,13},{13,5},{2,10},{10,2},... | collective-permute-start | bytes 196616 | tf_op jit(solution)/shard_map/while/body/eval_jaxpr/while/body/eval_jaxpr/ppermute | solution.py:14
  205.6 1.2 copy-start.18
  228.1 3.6 copy-start.22
  228.1 9.6 %collective-permute-start.2 = (bf16[512,256]{1,0:T(8,128)(2,1)S(1)}, bf16[512,256]{1,0:T(8,128)(2,1)S(1)}, u32[]{:S(2)}, u32[]{:S(2)}) collective-permute-start(bf16[512,256]{1,0:T(8,128)(2,1)S(1)} %get-tuple-element.812), channel_id=1, source_target_pairs={{0,2},{1,3},{4,6},{5,7},{8,10},{9,11},{12,14},{13,15},{16,18},{17,... | collective-permute-start | bytes 786440 | tf_op jit(solution)/shard_map/while/body/eval_jaxpr/ppermute | solution.py:20
  238.7 46.4 %all-reduce.5.cloned.1.call-start = ((), (), s32[]{:S(2)}) async-start(), calls=%async_computation.1 | async-start | bytes 524288 | tf_op jit(solution)/shard_map/while/body/eval_jaxpr/while/body/eval_jaxpr/psum | solution.py:65
  243.3 18.3 %collective-permute-start = (bf16[128,256]{1,0:T(8,128)(2,1)S(1)}, bf16[128,256]{1,0:T(8,128)(2,1)}, u32[]{:S(2)}, u32[]{:S(2)}) collective-permute-start(bf16[128,256]{1,0:T(8,128)(2,1)S(1)} %get-tuple-element.731), channel_id=1, source_target_pairs={{0,4},{4,0},{8,12},{12,8},{1,5},{5,1},{9,13},{13,9},{2,6},{6,2},{1... | collective-permute-start | bytes 196616 | tf_op jit(solution)/shard_map/while/body/eval_jaxpr/while/body/eval_jaxpr/ppermute | solution.py:14
  244.9 18.6 %collective-permute-start.1 = (bf16[128,256]{1,0:T(8,128)(2,1)S(1)}, bf16[128,256]{1,0:T(8,128)(2,1)}, u32[]{:S(2)}, u32[]{:S(2)}) collective-permute-start(bf16[128,256]{1,0:T(8,128)(2,1)S(1)} %get-tuple-element.733), channel_id=1, source_target_pairs={{0,8},{8,0},{4,12},{12,4},{1,9},{9,1},{5,13},{13,5},{2,10},{10,2},... | collective-permute-start | bytes 196616 | tf_op jit(solution)/shard_map/while/body/eval_jaxpr/while/body/eval_jaxpr/ppermute | solution.py:14
  266.3 1.2 copy-start.18
  287.5 45.5 %all-reduce.5.cloned.1.call-start = ((), (), s32[]{:S(2)}) async-start(), calls=%async_computation.1 | async-start | bytes 524288 | tf_op jit(solution)/shard_map/while/body/eval_jaxpr/while/body/eval_jaxpr/psum | solution.py:65
  292.1 18.6 %collective-permute-start = (bf16[128,256]{1,0:T(8,128)(2,1)S(1)}, bf16[128,256]{1,0:T(8,128)(2,1)}, u32[]{:S(2)}, u32[]{:S(2)}) collective-permute-start(bf16[128,256]{1,0:T(8,128)(2,1)S(1)} %get-tuple-element.731), channel_id=1, source_target_pairs={{0,4},{4,0},{8,12},{12,8},{1,5},{5,1},{9,13},{13,9},{2,6},{6,2},{1... | collective-permute-start | bytes 196616 | tf_op jit(solution)/shard_map/while/body/eval_jaxpr/while/body/eval_jaxpr/ppermute | solution.py:14
  293.9 18.6 %collective-permute-start.1 = (bf16[128,256]{1,0:T(8,128)(2,1)S(1)}, bf16[128,256]{1,0:T(8,128)(2,1)}, u32[]{:S(2)}, u32[]{:S(2)}) collective-permute-start(bf16[128,256]{1,0:T(8,128)(2,1)S(1)} %get-tuple-element.733), channel_id=1, source_target_pairs={{0,8},{8,0},{4,12},{12,4},{1,9},{9,1},{5,13},{13,5},{2,10},{10,2},... | collective-permute-start | bytes 196616 | tf_op jit(solution)/shard_map/while/body/eval_jaxpr/while/body/eval_jaxpr/ppermute | solution.py:14
  315.3 1.2 copy-start.18
  337.8 32.9 %all-reduce.3.cloned.1.call-start = ((), (), s32[]{:S(2)}) async-start(), calls=%async_computation | async-start | bytes 1048576 | tf_op jit(solution)/shard_map/psum | solution.py:25
  (93 other events, 71.7 us)
Sparse Core Ops, SparseCore 0:
  48.1 17.4 all-reduce.4
  97.2 16.3 all-reduce.4
  157.9 17.4 all-reduce.4
  206.9 16.3 all-reduce.4
  267.6 17.4 all-reduce.4
  316.6 16.3 all-reduce.4
  340.9 29.7 all-reduce.2
where the time goes:
time: 382 us; the launch traced here: 379 us
  waiting for transfers between devices  135 us (35%)
  local copies, waits for them, and re-layouts  116 us (30%)
  other arithmetic  54.9 us (14%)
  starting transfers between devices  37.1 us (10%)
  matrix products  14.3 us (4%)
  between operations  13.5 us (4%)
  loops' own time  8.11 us (2%)
    psum x6, waiting for transfers between devices, apply_layer(): mixed = lax.psum(term.astype(jnp.bfloat16), 'chan').astype(jnp.float32)  98.3 us
    gather x60, local copies, waits for them, and re-layouts, edge_hidden(): return jax.nn.relu(table[rows] + coefs[:, None] * gain[None, :])  78.7 us
    psum x1, waiting for transfers between devices, broadcast(): return lax.psum(block, axis)  32 us
    ppermute x12, starting transfers between devices, from_partner(): return lax.ppermute(block, axis, route)  24.8 us
    while x192, local copies, waits for them, and re-layouts  23.6 us
    scatter-add x12, other arithmetic, apply_layer(): summed = summed.at[recv_node[r]].add(arrived)  21.7 us
    ppermute x3, starting transfers between devices, passed_along(): lax.ppermute(value, axis, [(source, source + steps) for source in range(i...  12.1 us
    add x6, other arithmetic, apply_layer(): summed = summed + edge_hidden(source, neighbors[k], edge_coef[k], gain)  9.16 us
  transfers between devices with their start and end apart: 22, of which 10 were waited for; matrix products, arithmetic and copies ran while one was open for 25% of the time, Pallas kernels for 0%

commit v1 on v0

v1 whole, which is shorter than its diff:
```python
import functools

import jax
import jax.numpy as jnp
from jax import lax
from jax.experimental import pallas as pl
from jax.experimental.pallas import tpu as pltpu
from jax.sharding import PartitionSpec as P

F32 = jnp.float32
BF16 = jnp.bfloat16
VMEM = pl.BlockSpec(memory_space=pltpu.VMEM)
SMEM = pl.BlockSpec(memory_space=pltpu.SMEM)
LANES = 128


def dot(a, b):
    return jnp.dot(a, b, preferred_element_type=F32)


def kernel_call(body, outs, operands, flops, smem=1, limit=24):
    return pl.pallas_call(
        body,
        out_shape=outs,
        in_specs=[SMEM] * smem + [VMEM] * (len(operands) - smem),
        out_specs=jax.tree.map(lambda _: VMEM, outs),
        cost_estimate=pl.CostEstimate(flops=flops, bytes_accessed=1 << 16, transcendentals=0),
        compiler_params=pltpu.CompilerParams(vmem_limit_bytes=limit * 1024 * 1024),
    )(*operands)


def shape(dims, dtype):
    return jax.ShapeDtypeStruct(dims, dtype)


def pack_rows(width):
    half = width // 2
    edge, inner, outer, vecs = 0, half, half + width, 2 * half + width
    return edge, inner, outer, vecs, vecs + 16


def pack_kernel(place, w_edge, w_in, w_out, e_bias, e_gain, n_bias, g_norm, b_norm, out):
    layers, width, _ = w_edge.shape
    half = width // 2
    edge, inner, outer, vecs, _ = pack_rows(width)
    mine = pl.multiple_of(place[1] * half, half)
    for j in range(layers):
        out[j, edge : edge + half, :] = w_edge[j, pl.ds(mine, half), :]
        out[j, inner : inner + width, 0:half] = w_in[j, 0:width, :]
        out[j, inner : inner + width, half:width] = w_in[j, width : 2 * width, :]
        out[j, outer : outer + half, :] = w_out[j]
        spot = lax.broadcasted_iota(jnp.int32, (16, width), 0)
        block = jnp.zeros((16, width), F32)
        bias = n_bias[j : j + 1, :].astype(F32)
        rows = [
            e_bias[j : j + 1, :].astype(F32),
            e_gain[j : j + 1, :].astype(F32),
            jnp.concatenate([bias, bias], axis=1),
            g_norm[j : j + 1, :].astype(F32),
            b_norm[j : j + 1, :].astype(F32),
        ]
        for i, row in enumerate(rows):
            block = jnp.where(spot == i, row, block)
        out[j, vecs : vecs + 16, :] = block.astype(BF16)


def columns(rows):
    rows = rows.astype(F32)
    missing = -rows.shape[0] % 8
    if missing:
        rows = jnp.concatenate([rows, jnp.zeros((missing, rows.shape[1]), F32)], axis=0)
    return rows.T


def one_hot_rows(index_columns, coef_columns, count, nodes, hot, spread):
    rows = index_columns.shape[0]
    lane = lax.broadcasted_iota(jnp.int32, (rows, nodes), 1).astype(F32)
    for k in range(count):
        hot[k * rows : (k + 1) * rows, :] = jnp.where(
            index_columns[:, k : k + 1] == lane, 1.0, 0.0
        ).astype(BF16)
        spread[k * rows : (k + 1) * rows, :] = jnp.broadcast_to(
            coef_columns[:, k : k + 1], (rows, LANES)
        )


def cross_prep_kernel(src, coef, recv, hot, spread, scatter):
    rounds, slots = recv.shape
    nodes = hot.shape[1]
    one_hot_rows(columns(src[...]), columns(coef[...]), src.shape[0], nodes, hot, spread)
    row = lax.broadcasted_iota(jnp.int32, (nodes, slots), 0)
    for r in range(rounds):
        scatter[:, r * slots : (r + 1) * slots] = jnp.where(
            recv[r : r + 1, :] == row, 1.0, 0.0
        ).astype(BF16)


def inner_prep_kernel(neighbors, coef, hot, spread):
    one_hot_rows(
        columns(neighbors[...]), columns(coef[...]), neighbors.shape[0], neighbors.shape[1], hot, spread
    )


def wide(spread):
    return jnp.concatenate([spread, spread], axis=1)


def cross_sums(source, gain, hot, spread, outs):
    slots = outs[0].shape[0]
    each = hot.shape[0] // (len(outs) * slots)
    for r, out in enumerate(outs):
        total = None
        for x in range(each):
            rows = pl.ds((r * each + x) * slots, slots)
            hidden = jnp.maximum(dot(hot[rows, :], source) + wide(spread[rows, :]) * gain, 0.0)
            total = hidden if total is None else total + hidden
        out[...] = total.astype(BF16)


def first_sums_kernel(rounds, wave, place, latents, w_edge, e_bias, e_gain, hot, spread, *outs):
    micro = jnp.minimum(wave * 2 + place[1], latents.shape[0] - 1)
    source = (dot(latents[micro], w_edge[0]) + e_bias[0:1, :].astype(F32)).astype(BF16)
    cross_sums(source, e_gain[0:1, :].astype(F32), hot, spread, outs)


def choose(which, refs, j, rows):
    value = refs[0][j, rows, :]
    for r in range(1, len(refs)):
        value = jnp.where(which == r, refs[r][j, rows, :], value)
    return value


def edge_weights(place, which, mine, other, j, width):
    half = width // 2
    edge, _, _, vecs, _ = pack_rows(width)
    a = choose(which, mine, j, slice(edge, edge + half))
    b = choose(which, other, j, slice(edge, edge + half))
    first = place[1] == 0
    weights = jnp.concatenate([jnp.where(first, a, b), jnp.where(first, b, a)], axis=0)
    return weights, choose(which, mine, j, slice(vecs, vecs + 16)).astype(F32)


def inner_kernel(segments, segment, j, first, place, *refs):
    mine, other = refs[:segments], refs[segments : 2 * segments]
    latent, source, hot, spread, sums, before, chosen = refs[2 * segments :]
    nodes, width = sums.shape
    half = width // 2
    _, inner, outer, vecs, _ = pack_rows(width)
    which = lax.rem(place[0] - segment + segments, segments)
    vectors = choose(which, mine, j, slice(vecs, vecs + 16)).astype(F32)
    if first:
        values = latent[place[0]]
        weights, vectors = edge_weights(place, which, mine, other, j, width)
        table = (dot(values, weights) + vectors[0:1, :]).astype(BF16)
    else:
        values = latent[...]
        table = source[...]
    gain = vectors[1:2, :]
    total = None
    for k in range(hot.shape[0] // nodes):
        rows = pl.ds(k * nodes, nodes)
        hidden = jnp.maximum(dot(hot[rows, :], table) + wide(spread[rows, :]) * gain, 0.0)
        total = hidden if total is None else total + hidden
    sums[...] = total
    in_a = choose(which, mine, j, slice(inner, inner + width))
    in_b = choose(which, other, j, slice(inner, inner + width))
    other_vectors = choose(which, other, j, slice(vecs, vecs + 16)).astype(F32)
    bias = jnp.concatenate([vectors[2:3, :half], other_vectors[2:3, :half]], axis=1)
    before[...] = dot(values, jnp.concatenate([in_a[:, :half], in_b[:, :half]], axis=1)) + bias
    chosen[0:width, :] = jnp.concatenate([in_a[:, half:], in_b[:, half:]], axis=1)
    chosen[width : width + half, :] = choose(which, mine, j, slice(outer, outer + half))
    chosen[width + half : 2 * width, :] = choose(which, other, j, slice(outer, outer + half))
    chosen[2 * width : 2 * width + 16, :] = vectors.astype(BF16)


def node_kernel(segments, segment, j, last, many, first, place, *refs):
    arrived, refs = refs[:many], refs[many:]
    latent, sums, before, chosen, scatter = refs[:5]
    nodes, width = sums.shape
    half = width // 2
    rounds = scatter.shape[1] // arrived[0].shape[0]
    per = many // rounds
    blocks = []
    for r in range(rounds):
        block = arrived[r * per][...]
        for i in range(1, per):
            block = block + arrived[r * per + i][...]
        blocks.append(block)
    summed = sums[...] + dot(scatter[...], jnp.concatenate(blocks, axis=0))
    hidden = before[...] + dot(summed.astype(BF16), chosen[0:width, :])
    hidden = jnp.maximum(hidden, 0.0).astype(BF16)
    mixed = dot(hidden[:, :half], chosen[width : width + half, :]).astype(BF16).astype(F32)
    mixed = mixed + dot(hidden[:, half:], chosen[width + half : 2 * width, :]).astype(BF16).astype(F32)
    vectors = chosen[2 * width : 2 * width + 16, :].astype(F32)
    centred = mixed - jnp.mean(mixed, axis=1, keepdims=True)
    spread_of = jnp.mean(centred * centred, axis=1, keepdims=True)
    normed = centred * lax.rsqrt(spread_of + 1e-05) * vectors[3:4, :] + vectors[4:5, :]
    old = latent[place[0]] if first else latent[...]
    fresh = (old.astype(F32) + normed).astype(BF16)
    if last:
        refs[5][0] = fresh
        return
    mine, other = refs[5 : 5 + segments], refs[5 + segments : 5 + 2 * segments]
    hot, spread, result, source = refs[5 + 2 * segments : 9 + 2 * segments]
    outs = refs[9 + 2 * segments :]
    result[...] = fresh
    which = lax.rem(place[0] - segment + segments, segments)
    weights, vectors = edge_weights(place, which, mine, other, j, width)
    table = (dot(fresh, weights) + vectors[0:1, :]).astype(BF16)
    source[...] = table
    cross_sums(table, vectors[1:2, :], hot, spread, outs)


def partner_route(count, r):
    return [(i, i ^ 1 << r) for i in range(count) if i ^ 1 << r < count]


def swap(block):
    return lax.ppermute(block, "chan", [(0, 1), (1, 0)])


def per_device(
    latents,
    neighbors,
    edge_coef,
    cross_src,
    cross_coef,
    recv_node,
    w_edge,
    w_node_in,
    w_node_out,
    edge_bias,
    edge_gain,
    node_bias,
    norm_gain,
    norm_bias,
):
    segments, cores, parts = (lax.axis_size(a) for a in ("segment", "chan", "dom"))
    micro, nodes, width = latents.shape
    held = w_edge.shape[0]
    rounds, slots = recv_node.shape
    degree, edges = neighbors.shape[0], cross_src.shape[0] * cross_src.shape[1]
    assert micro == segments and cores == 2
    place = jnp.stack([lax.axis_index("segment"), lax.axis_index("chan")]).astype(jnp.int32)

    hot_c, spread_c, scatter = kernel_call(
        cross_prep_kernel,
        (shape((edges * slots, nodes), BF16), shape((edges * slots, LANES), F32), shape((nodes, rounds * slots), BF16)),
        (cross_src.reshape(edges, slots), cross_coef.reshape(edges, slots), recv_node),
        1 << 30,
        smem=0,
    )
    packed = kernel_call(
        pack_kernel,
        shape((held, pack_rows(width)[-1], width), BF16),
        (place, w_edge, w_node_in, w_node_out, edge_bias, edge_gain, node_bias, norm_gain, norm_bias),
        1 << 28,
    )

    arrived = [[] for _ in range(rounds)]
    for wave in range(-(-segments // cores)):
        sums = kernel_call(
            functools.partial(first_sums_kernel, rounds, wave),
            [shape((slots, width), BF16)] * rounds,
            (place, latents, w_edge, edge_bias, edge_gain, hot_c, spread_c),
            1 << 29,
        )
        for r in range(rounds):
            route = []
            for here, there in partner_route(parts, r):
                for core in range(cores):
                    goal = wave * cores + core
                    if goal < segments:
                        route.append(
                            (here * segments * cores + core, (there * segments + goal) * cores + core)
                        )
            block = lax.ppermute(sums[r], ("dom", "segment", "chan"), route)
            arrived[r] += [block, swap(block)]

    packs, others = [], []
    for r in range(segments):
        layers = [packed[j : j + 1] for j in range(held)]
        if r:
            route = [(i, (i + r) % segments) for i in range(segments)]
            layers = [lax.ppermute(layer, "segment", route) for layer in layers]
        packs.append(layers)
        others.append([swap(layer) for layer in layers])

    hot, spread = kernel_call(
        inner_prep_kernel,
        (shape((degree * nodes, nodes), BF16), shape((degree * nodes, LANES), F32)),
        (neighbors, edge_coef),
        1 << 31,
        smem=0,
    )

    total = segments * held
    latent, source = latents, None
    for layer in range(total):
        segment, j = divmod(layer, held)
        mine = [packs[r][j] for r in range(segments)]
        other = [others[r][j] for r in range(segments)]
        sums, before, chosen = kernel_call(
            functools.partial(inner_kernel, segments, segment, 0, layer == 0),
            (shape((nodes, width), F32), shape((nodes, width), F32), shape((2 * width + 16, width), BF16)),
            (place, *mine, *other, latent, latent if layer == 0 else source, hot, spread),
            1 << 31,
        )
        blocks = [block for r in range(rounds) for block in arrived[r]]
        last = layer == total - 1
        operands = [place, *blocks, latent, sums, before, chosen, scatter]
        outs = [shape((1, nodes, width), BF16)]
        follow, step = divmod(layer + 1, held)
        if not last:
            operands += [packs[r][step] for r in range(segments)] + [others[r][step] for r in range(segments)]
            operands += [hot_c, spread_c]
            outs = [shape((nodes, width), BF16)] * 2 + [shape((slots, width), BF16)] * rounds
        results = kernel_call(
            functools.partial(node_kernel, segments, follow, 0, last, len(blocks), layer == 0),
            outs,
            operands,
            1 << 30,
        )
        if last:
            return results[0]
        latent, source = results[0], results[1]
        arrived = [
            [lax.ppermute(results[2 + r], "dom", partner_route(parts, r))] for r in range(rounds)
        ]


def solution(mesh):
    return jax.shard_map(
        per_device,
        mesh=mesh,
        in_specs=(
            P(None, ("groups", "dom"), None),
            P(None, ("groups", "dom")),
            P(None, ("groups", "dom")),
            P(None, None, ("groups", "dom")),
            P(None, None, ("groups", "dom")),
            P(None, ("groups", "dom")),
            P("segment", None, None),
            P("segment", None, "chan"),
            P("segment", "chan", None),
            P("segment", None),
            P("segment", None),
            P("segment", "chan"),
            P("segment", None),
            P("segment", None),
        ),
        out_specs=P("segment", ("groups", "dom"), None),
        check_vma=False,
    )
```

time: 382 us -> 65.5 us (0.17)
  waiting for transfers between devices: 135 us -> 11.3 us
  local copies, waits for them, and re-layouts: 116 us -> 8.31 us
  other arithmetic: 54.9 us -> 0.07 us
  Pallas kernels: 0 us -> 17.4 us
  matrix products: 14.3 us -> 0 us
  between operations: 13.5 us -> 0.2 us
  starting transfers between devices: 37.1 us -> 27.8 us
  loops' own time: 8.11 us -> 0 us
    psum x7 -> x0, waiting for transfers between devices: 130 us -> none  [the longest x6 98.3 us: apply_layer(): mixed = lax.psum(term.astype(jnp.bfloat16), 'chan').astype(jnp.float32)]
    gather x60 -> x0, local copies, waits for them, and re-layouts: 78.7 us -> none  [edge_hidden(): return jax.nn.relu(table[rows] + coefs[:, None] * gain[None, :])]
    while x192 -> x0, local copies, waits for them, and re-layouts: 23.6 us -> none
    scatter-add x12 -> x0, other arithmetic: 21.7 us -> none  [apply_layer(): summed = summed.at[recv_node[r]].add(arrived)]
    pallas_call x0 -> x12, Pallas kernels: none -> 17.4 us  [kernel_call(): pl.pallas_call(body, out_shape=outs, in_specs=[SMEM] * smem + [VMEM] * (l...]
    dot_general x12 -> x0, matrix products: 14.3 us -> none  [the longest x6 7.21 us: apply_layer(): term = jnp.dot(hidden, w_node_out, preferred_element_type=jnp.float32)]
    add x24 -> x0, other arithmetic: 9.3 us -> none  [the longest x6 9.16 us: apply_layer(): summed = summed + edge_hidden(source, neighbors[k], edge_coef[k], gain)]
    ppermute x15 -> x16, starting transfers between devices: 36.9 us -> 27.8 us  [the longest x6 12.9 us: per_device(): lax.ppermute(results[2 + r], 'dom', partner_route(parts, r))]
  transfers between devices with their start and end apart: 22 -> 16, of which waited for: 10 -> 6; matrix products, arithmetic and copies ran while one was open for 25% -> 0% of each run, Pallas kernels for 0% -> 15%
where the time goes in v1:
time: 65.5 us; the launch traced here: 65.1 us
  starting transfers between devices  27.8 us (42%)
  Pallas kernels  17.4 us (27%)
  waiting for transfers between devices  11.3 us (17%)
  local copies, waits for them, and re-layouts  8.31 us (13%)
    pallas_call x12, Pallas kernels, kernel_call(): pl.pallas_call(body, out_shape=outs, in_specs=[SMEM] * smem + [VMEM] * (l...  17.4 us
    ppermute x6, starting transfers between devices, per_device(): lax.ppermute(results[2 + r], 'dom', partner_route(parts, r))  12.9 us
    ppermute x2, starting transfers between devices, per_device(): block = lax.ppermute(sums[r], ('dom', 'segment', 'chan'), route)  9.29 us
    unnamed x30, local copies, waits for them, and re-layouts  8.28 us
    ppermute x6, waiting for transfers between devices, per_device(): lax.ppermute(results[2 + r], 'dom', partner_route(parts, r))  4.87 us
    ppermute x2, waiting for transfers between devices, per_device(): layers = [lax.ppermute(layer, 'segment', route) for layer in layers]  4.76 us
    ppermute x2, starting transfers between devices, per_device(): layers = [lax.ppermute(layer, 'segment', route) for layer in layers]  3.08 us
    ppermute x6, starting transfers between devices, swap(): return lax.ppermute(block, 'chan', [(0, 1), (1, 0)])  2.62 us
  transfers between devices with their start and end apart: 16, of which 6 were waited for; matrix products, arithmetic and copies ran while one was open for 0% of the time, Pallas kernels for 15%

profile of v1, /device:TPU:0, one launch (start us, length us, event | category | flops | bytes accessed | tf_op | source)
XLA Modules:
  0.0 65.1 jit_solution(12848917332190301492)
XLA Ops:
  0.1 1.0 %copy-done.1 = bf16[2,512,128]{2,1,0:T(8,128)(2,1)S(1)} copy-done((bf16[2,512,128]{2,1,0:T(8,128)(2,1)S(1)}, bf16[2,512,128]{2,1,0:T(8,128)(2,1)}, u32[]{:S(2)}) %copy-start.1) | copy-done | bytes 262168
  1.1 0.9 %copy-done.2 = bf16[2,256,256]{2,1,0:T(8,128)(2,1)S(1)} copy-done((bf16[2,256,256]{2,1,0:T(8,128)(2,1)S(1)}, bf16[2,256,256]{2,1,0:T(8,128)(2,1)}, u32[]{:S(2)}) %copy-start.2) | copy-done | bytes 262168
  2.0 0.9 %copy-done.4 = bf16[2,128,256]{2,1,0:T(8,128)(2,1)S(1)} copy-done((bf16[2,128,256]{2,1,0:T(8,128)(2,1)S(1)}, bf16[2,128,256]{2,1,0:T(8,128)(2,1)}, u32[]{:S(2)}) %copy-start.4) | copy-done | bytes 131096
  2.9 0.7 %copy-done.5 = bf16[2,256]{1,0:T(2,128)(2,1)S(1)} copy-done((bf16[2,256]{1,0:T(2,128)(2,1)S(1)}, bf16[2,256]{1,0:T(2,128)(2,1)}, u32[]{:S(2)}) %copy-start.5) | copy-done | bytes 1048
  3.6 0.7 %copy-done.6 = bf16[2,256]{1,0:T(2,128)(2,1)S(1)} copy-done((bf16[2,256]{1,0:T(2,128)(2,1)S(1)}, bf16[2,256]{1,0:T(2,128)(2,1)}, u32[]{:S(2)}) %copy-start.6) | copy-done | bytes 1048
  4.3 0.7 %copy-done.7 = bf16[2,256]{1,0:T(2,128)(2,1)S(1)} copy-done((bf16[2,256]{1,0:T(2,128)(2,1)S(1)}, bf16[2,256]{1,0:T(2,128)(2,1)}, u32[]{:S(2)}) %copy-start.7) | copy-done | bytes 1048
  7.0 3.0 %collective-permute-start.4 = (bf16[1,528,256]{2,1,0:T(8,128)(2,1)S(1)}, bf16[1,528,256]{2,1,0:T(8,128)(2,1)S(1)}, u32[]{:S(2)}, u32[]{:S(2)}) collective-permute-start(bf16[1,528,256]{2,1,0:T(8,128)(2,1)S(1)} %get-tuple-element.68.refs_0_.refs_7_), channel_id=1, source_target_pairs={{0,2},{2,0},{1,3},{3,1},{4,6},{6,4},{5,7},{7,5},{8,10},{10,8},{9,1... | collective-permute-start | bytes 811016 | tf_op jit(solution)/shard_map/ppermute | solution.py:285
  10.1 0.7 %copy-done.12 = s32[2,2,128]{2,1,0:T(2,128)S(1)} copy-done((s32[2,2,128]{2,1,0:T(2,128)S(1)}, s32[2,2,128]{2,1,0:T(2,128)}, u32[]{:S(2)}) %copy-start.12) | copy-done | bytes 2072
  10.8 0.7 %copy-done.13 = f32[2,2,128]{2,1,0:T(2,128)S(1)} copy-done((f32[2,2,128]{2,1,0:T(2,128)S(1)}, f32[2,2,128]{2,1,0:T(2,128)}, u32[]{:S(2)}) %copy-start.13) | copy-done | bytes 2072
  12.5 4.8 %collective-permute-done.4.refs_1_.refs_8_ = bf16[1,528,256]{2,1,0:T(8,128)(2,1)S(1)} collective-permute-done((bf16[1,528,256]{2,1,0:T(8,128)(2,1)S(1)}, bf16[1,528,256]{2,1,0:T(8,128)(2,1)S(1)}, u32[]{:S(2)}, u32[]{:S(2)}) %collective-permute-start.4) | collective-permute-done | bytes 270368 | tf_op jit(solution)/shard_map/ppermute | solution.py:285
  17.3 1.1 %shard_map.137 = (bf16[128,256]{1,0:T(8,128)(2,1)S(1)}, bf16[128,256]{1,0:T(8,128)(2,1)S(1)}) custom-call(s32[2]{0:T(128)S(1)} %pad_add_fusion.place, bf16[2,512,256]{2,1,0:T(8,128)(2,1)S(1)} %copy-done, bf16[2,256,256]{2,1,0:T(8,128)(2,1)S(1)} %copy-done.3, bf16[2,256]{1,0:T(2,128)(2,1)S(1)} %copy-done.7, bf16[2,256]{1,0:T(2,128)(2,1)S(1)} %copy-done.8, ...), custom_call_target="tpu_custom_call" | custom-call | flops 536870912 | bytes 65536 | tf_op jit(solution)/shard_map/pallas_call | solution.py:22
  18.5 4.1 %collective-permute-start = (bf16[128,256]{1,0:T(8,128)(2,1)S(1)}, bf16[128,256]{1,0:T(8,128)(2,1)S(1)}, u32[]{:S(2)}, u32[]{:S(2)}) collective-permute-start(bf16[128,256]{1,0:T(8,128)(2,1)S(1)} %get-tuple-element.38), channel_id=1, source_target_pairs={{0,4},{1,7},{4,0},{5,3},{8,12},{9,15},{12,8},{13,11},{16,20},{17,2... | collective-permute-start | bytes 196616 | tf_op jit(solution)/shard_map/ppermute | solution.py:277
  22.5 1.2 %collective-permute-start.8 = (bf16[1,528,256]{2,1,0:T(8,128)(2,1)S(1)}, bf16[1,528,256]{2,1,0:T(8,128)(2,1)S(1)}, u32[]{:S(2)}, u32[]{:S(2)}) collective-permute-start(bf16[1,528,256]{2,1,0:T(8,128)(2,1)S(1)} %get-tuple-element.67.refs_9_.refs_0_.refs_7_), channel_id=1, source_target_pairs={{0,1},{1,0},{2,3},{3,2},{4,5},{5,4},{6,7},{7,6},{8,9},{9,8},{10,11... | collective-permute-start | bytes 811016 | tf_op jit(solution)/shard_map/ppermute | solution.py:219
  23.7 1.0 %collective-permute-done.refs_0_ = bf16[128,256]{1,0:T(8,128)(2,1)S(1)} collective-permute-done((bf16[128,256]{1,0:T(8,128)(2,1)S(1)}, bf16[128,256]{1,0:T(8,128)(2,1)S(1)}, u32[]{:S(2)}, u32[]{:S(2)}) %collective-permute-start) | collective-permute-done | bytes 65568 | tf_op jit(solution)/shard_map/ppermute | solution.py:277
  24.8 5.2 %collective-permute-start.2 = (bf16[128,256]{1,0:T(8,128)(2,1)S(1)}, bf16[128,256]{1,0:T(8,128)(2,1)S(1)}, u32[]{:S(2)}, u32[]{:S(2)}) collective-permute-start(bf16[128,256]{1,0:T(8,128)(2,1)S(1)} %get-tuple-element.39), channel_id=1, source_target_pairs={{0,8},{1,11},{4,12},{5,15},{8,0},{9,3},{12,4},{13,7},{16,24},{17,2... | collective-permute-start | bytes 196616 | tf_op jit(solution)/shard_map/ppermute | solution.py:277
  30.0 0.9 %collective-permute-start.9 = (bf16[1,528,256]{2,1,0:T(8,128)(2,1)S(1)}, bf16[1,528,256]{2,1,0:T(8,128)(2,1)S(1)}, u32[]{:S(2)}, u32[]{:S(2)}) collective-permute-start(bf16[1,528,256]{2,1,0:T(8,128)(2,1)S(1)} %collective-permute-done.7.refs_10_.refs_1_.refs_8_), channel_id=1, source_target_pairs={{0,1},{1,0},{2,3},{3,2},{4,5},{5,4},{6,7},{7,6},{8,9},{9,8},{10,11... | collective-permute-start | bytes 811016 | tf_op jit(solution)/shard_map/ppermute | solution.py:219
  30.9 1.2 %shard_map.139 = (bf16[3072,512]{1,0:T(8,128)(2,1)S(1)}, f32[3072,128]{1,0:T(8,128)S(1)}) custom-call(s32[6,512]{1,0:T(8,128)S(1)} %copy-done.10, f32[6,512]{1,0:T(8,128)S(1)} %copy-done.11), custom_call_target="tpu_custom_call" | custom-call | flops 2147483648 | bytes 65536 | tf_op jit(solution)/shard_map/pallas_call | solution.py:22
  33.2 1.9 %shard_map.140 = (f32[512,256]{1,0:T(8,128)S(1)}, f32[512,256]{1,0:T(8,128)S(1)}, bf16[528,256]{1,0:T(8,128)(2,1)S(1)}) custom-call(s32[2]{0:T(128)S(1)} %pad_add_fusion.place, bf16[1,528,256]{2,1,0:T(8,128)(2,1)S(1)} %get-tuple-element.68.refs_0_.refs_7_, bf16[1,528,256]{2,1,0:T(8,128)(2,1)S(1)} %collective-permute-done.4.refs_1_.refs_8_, ...), custom_call_target="tpu_custom_call" | custom-call | flops 2147483648 | bytes 65536 | tf_op jit(solution)/shard_map/pallas_call | solution.py:22
  35.2 1.8 %shard_map.141 = (bf16[512,256]{1,0:T(8,128)(2,1)S(1)}, bf16[512,256]{1,0:T(8,128)(2,1)S(1)}, bf16[128,256]{1,0:T(8,128)(2,1)S(1)}, bf16[128,256]{1,0:T(8,128)(2,1)S(1)}) custom-call(s32[2]{0:T(128)S(1)} %pad_add_fusion.place, bf16[128,256]{1,0:T(8,128)(2,1)S(1)} %collective-permute-done.refs_0_, bf16[128,256]{1,0:T(8,128)(2,1)S(1)} %collective-permute-done.1.refs_1_, ...), custom_call_target="tpu_custom_call" | custom-call | flops 1073741824 | bytes 65536 | tf_op jit(solution)/shard_map/pallas_call | solution.py:22
  37.0 2.7 %collective-permute-start.10 = (bf16[128,256]{1,0:T(8,128)(2,1)S(1)}, bf16[128,256]{1,0:T(8,128)(2,1)S(1)}, u32[]{:S(2)}, u32[]{:S(2)}) collective-permute-start(bf16[128,256]{1,0:T(8,128)(2,1)S(1)} %get-tuple-element.46), channel_id=1, source_target_pairs={{0,4},{4,0},{8,12},{12,8},{1,5},{5,1},{9,13},{13,9},{2,6},{6,2},{1... | collective-permute-start | bytes 196616 | tf_op jit(solution)/shard_map/ppermute | solution.py:328
  39.6 3.4 %collective-permute-start.11 = (bf16[128,256]{1,0:T(8,128)(2,1)S(1)}, bf16[128,256]{1,0:T(8,128)(2,1)S(1)}, u32[]{:S(2)}, u32[]{:S(2)}) collective-permute-start(bf16[128,256]{1,0:T(8,128)(2,1)S(1)} %get-tuple-element.47), channel_id=1, source_target_pairs={{0,8},{4,12},{8,0},{12,4},{1,9},{5,13},{9,1},{13,5},{2,10},{6,14},... | collective-permute-start | bytes 196616 | tf_op jit(solution)/shard_map/ppermute | solution.py:328
  43.0 1.6 %shard_map.142 = (f32[512,256]{1,0:T(8,128)S(1)}, f32[512,256]{1,0:T(8,128)S(1)}, bf16[528,256]{1,0:T(8,128)(2,1)S(1)}) custom-call(s32[2]{0:T(128)S(1)} %pad_add_fusion.place, bf16[1,528,256]{2,1,0:T(8,128)(2,1)S(1)} %get-tuple-element.67.refs_9_.refs_0_.refs_7_, bf16[1,528,256]{2,1,0:T(8,128)(2,1)S(1)} %collective-permute-done.7.refs_10_.refs_1_.refs_8_, ...), custom_call_target="tpu_custom_call" | custom-call | flops 2147483648 | bytes 65536 | tf_op jit(solution)/shard_map/pallas_call | solution.py:22
  44.7 1.8 %collective-permute-done.11.refs_1_ = bf16[128,256]{1,0:T(8,128)(2,1)S(1)} collective-permute-done((bf16[128,256]{1,0:T(8,128)(2,1)S(1)}, bf16[128,256]{1,0:T(8,128)(2,1)S(1)}, u32[]{:S(2)}, u32[]{:S(2)}) %collective-permute-start.11) | collective-permute-done | bytes 65568 | tf_op jit(solution)/shard_map/ppermute | solution.py:328
  46.4 1.8 %shard_map.143 = (bf16[512,256]{1,0:T(8,128)(2,1)S(1)}, bf16[512,256]{1,0:T(8,128)(2,1)S(1)}, bf16[128,256]{1,0:T(8,128)(2,1)S(1)}, bf16[128,256]{1,0:T(8,128)(2,1)S(1)}) custom-call(s32[2]{0:T(128)S(1)} %pad_add_fusion.place, bf16[128,256]{1,0:T(8,128)(2,1)S(1)} %collective-permute-done.10.refs_0_, bf16[128,256]{1,0:T(8,128)(2,1)S(1)} %collective-permute-done.11.refs_1_, ...), custom_call_target="tpu_custom_call" | custom-call | flops 1073741824 | bytes 65536 | tf_op jit(solution)/shard_map/pallas_call | solution.py:22
  48.6 2.9 %collective-permute-start.13 = (bf16[128,256]{1,0:T(8,128)(2,1)S(1)}, bf16[128,256]{1,0:T(8,128)(2,1)S(1)}, u32[]{:S(2)}, u32[]{:S(2)}) collective-permute-start(bf16[128,256]{1,0:T(8,128)(2,1)S(1)} %get-tuple-element.54), channel_id=1, source_target_pairs={{0,8},{4,12},{8,0},{12,4},{1,9},{5,13},{9,1},{13,5},{2,10},{6,14},... | collective-permute-start | bytes 196616 | tf_op jit(solution)/shard_map/ppermute | solution.py:328
  51.5 1.6 %shard_map.144 = (f32[512,256]{1,0:T(8,128)S(1)}, f32[512,256]{1,0:T(8,128)S(1)}, bf16[528,256]{1,0:T(8,128)(2,1)S(1)}) custom-call(s32[2]{0:T(128)S(1)} %pad_add_fusion.place, bf16[1,528,256]{2,1,0:T(8,128)(2,1)S(1)} %get-tuple-element.68.refs_0_.refs_7_, bf16[1,528,256]{2,1,0:T(8,128)(2,1)S(1)} %collective-permute-done.4.refs_1_.refs_8_, ...), custom_call_target="tpu_custom_call" | custom-call | flops 2147483648 | bytes 65536 | tf_op jit(solution)/shard_map/pallas_call | solution.py:22
  53.8 1.8 %shard_map.145 = (bf16[512,256]{1,0:T(8,128)(2,1)S(1)}, bf16[512,256]{1,0:T(8,128)(2,1)S(1)}, bf16[128,256]{1,0:T(8,128)(2,1)S(1)}, bf16[128,256]{1,0:T(8,128)(2,1)S(1)}) custom-call(s32[2]{0:T(128)S(1)} %pad_add_fusion.place, bf16[128,256]{1,0:T(8,128)(2,1)S(1)} %collective-permute-done.12.refs_0_, bf16[128,256]{1,0:T(8,128)(2,1)S(1)} %collective-permute-done.13.refs_1_, ...), custom_call_target="tpu_custom_call" | custom-call | flops 1073741824 | bytes 65536 | tf_op jit(solution)/shard_map/pallas_call | solution.py:22
  55.6 1.7 %collective-permute-start.14 = (bf16[128,256]{1,0:T(8,128)(2,1)S(1)}, bf16[128,256]{1,0:T(8,128)(2,1)S(1)}, u32[]{:S(2)}, u32[]{:S(2)}) collective-permute-start(bf16[128,256]{1,0:T(8,128)(2,1)S(1)} %get-tuple-element.60), channel_id=1, source_target_pairs={{0,4},{4,0},{8,12},{12,8},{1,5},{5,1},{9,13},{13,9},{2,6},{6,2},{1... | collective-permute-start | bytes 196616 | tf_op jit(solution)/shard_map/ppermute | solution.py:328
  57.3 1.8 %collective-permute-start.15 = (bf16[128,256]{1,0:T(8,128)(2,1)S(1)}, bf16[128,256]{1,0:T(8,128)(2,1)S(1)}, u32[]{:S(2)}, u32[]{:S(2)}) collective-permute-start(bf16[128,256]{1,0:T(8,128)(2,1)S(1)} %get-tuple-element.61), channel_id=1, source_target_pairs={{0,8},{4,12},{8,0},{12,4},{1,9},{5,13},{9,1},{13,5},{2,10},{6,14},... | collective-permute-start | bytes 196616 | tf_op jit(solution)/shard_map/ppermute | solution.py:328
  59.1 1.6 %shard_map.146 = (f32[512,256]{1,0:T(8,128)S(1)}, f32[512,256]{1,0:T(8,128)S(1)}, bf16[528,256]{1,0:T(8,128)(2,1)S(1)}) custom-call(s32[2]{0:T(128)S(1)} %pad_add_fusion.place, bf16[1,528,256]{2,1,0:T(8,128)(2,1)S(1)} %get-tuple-element.67.refs_9_.refs_0_.refs_7_, bf16[1,528,256]{2,1,0:T(8,128)(2,1)S(1)} %collective-permute-done.7.refs_10_.refs_1_.refs_8_, ...), custom_call_target="tpu_custom_call" | custom-call | flops 2147483648 | bytes 65536 | tf_op jit(solution)/shard_map/pallas_call | solution.py:22
  60.7 2.4 %collective-permute-done.15.refs_1_ = bf16[128,256]{1,0:T(8,128)(2,1)S(1)} collective-permute-done((bf16[128,256]{1,0:T(8,128)(2,1)S(1)}, bf16[128,256]{1,0:T(8,128)(2,1)S(1)}, u32[]{:S(2)}, u32[]{:S(2)}) %collective-permute-start.15) | collective-permute-done | bytes 65568 | tf_op jit(solution)/shard_map/ppermute | solution.py:328
  63.2 2.0 %shard_map.147 = bf16[1,512,256]{2,1,0:T(8,128)(2,1)} custom-call(s32[2]{0:T(128)S(1)} %pad_add_fusion.place, bf16[128,256]{1,0:T(8,128)(2,1)S(1)} %collective-permute-done.14.refs_0_, bf16[128,256]{1,0:T(8,128)(2,1)S(1)} %collective-permute-done.15.refs_1_, bf16[512,256]{1,0:T(8,128)(2,1)S(1)} %get-tuple-element.62.refs_4_.refs_2_, ...), custom_call_target="tpu_custom_call" | custom-call | flops 1073741824 | bytes 65536 | tf_op jit(solution)/shard_map/pallas_call | solution.py:22
  (44 shorter events, 5.5 us)
Async XLA Ops:
  0.0 17.3 %copy-start = (bf16[2,512,256]{2,1,0:T(8,128)(2,1)S(1)}, bf16[2,512,256]{2,1,0:T(8,128)(2,1)}, u32[]{:S(2)}) copy-start(bf16[2,512,256]{2,1,0:T(8,128)(2,1)} %refs_4_.3) | copy-start | bytes 1572868
  0.1 1.0 %copy-start.1 = (bf16[2,512,128]{2,1,0:T(8,128)(2,1)S(1)}, bf16[2,512,128]{2,1,0:T(8,128)(2,1)}, u32[]{:S(2)}) copy-start(bf16[2,512,128]{2,1,0:T(8,128)(2,1)} %w_in.1) | copy-start | bytes 786436
  1.1 0.9 %copy-start.2 = (bf16[2,256,256]{2,1,0:T(8,128)(2,1)S(1)}, bf16[2,256,256]{2,1,0:T(8,128)(2,1)}, u32[]{:S(2)}) copy-start(bf16[2,256,256]{2,1,0:T(8,128)(2,1)} %w_edge.3) | copy-start | bytes 786436
  2.0 0.9 %copy-start.4 = (bf16[2,128,256]{2,1,0:T(8,128)(2,1)S(1)}, bf16[2,128,256]{2,1,0:T(8,128)(2,1)}, u32[]{:S(2)}) copy-start(bf16[2,128,256]{2,1,0:T(8,128)(2,1)} %w_out.1) | copy-start | bytes 393220
  2.9 0.7 %copy-start.5 = (bf16[2,256]{1,0:T(2,128)(2,1)S(1)}, bf16[2,256]{1,0:T(2,128)(2,1)}, u32[]{:S(2)}) copy-start(bf16[2,256]{1,0:T(2,128)(2,1)} %g_norm.1) | copy-start | bytes 3076
  3.6 0.7 %copy-start.6 = (bf16[2,256]{1,0:T(2,128)(2,1)S(1)}, bf16[2,256]{1,0:T(2,128)(2,1)}, u32[]{:S(2)}) copy-start(bf16[2,256]{1,0:T(2,128)(2,1)} %b_norm.1) | copy-start | bytes 3076
  4.3 0.7 %copy-start.7 = (bf16[2,256]{1,0:T(2,128)(2,1)S(1)}, bf16[2,256]{1,0:T(2,128)(2,1)}, u32[]{:S(2)}) copy-start(bf16[2,256]{1,0:T(2,128)(2,1)} %e_bias.3) | copy-start | bytes 3076
  5.0 0.7 %copy-start.8 = (bf16[2,256]{1,0:T(2,128)(2,1)S(1)}, bf16[2,256]{1,0:T(2,128)(2,1)}, u32[]{:S(2)}) copy-start(bf16[2,256]{1,0:T(2,128)(2,1)} %e_gain.3) | copy-start | bytes 3076
  5.6 0.7 %copy-start.9 = (bf16[2,128]{1,0:T(2,128)(2,1)S(1)}, bf16[2,128]{1,0:T(2,128)(2,1)}, u32[]{:S(2)}) copy-start(bf16[2,128]{1,0:T(2,128)(2,1)} %n_bias.1) | copy-start | bytes 1540
  6.3 11.0 %copy-start.3 = (bf16[2,256,256]{2,1,0:T(8,128)(2,1)S(1)}, bf16[2,256,256]{2,1,0:T(8,128)(2,1)}, u32[]{:S(2)}) copy-start(bf16[2,256,256]{2,1,0:T(8,128)(2,1)} %w_edge.3) | copy-start | bytes 786436
  7.0 23.9 %copy-start.10 = (s32[6,512]{1,0:T(8,128)S(1)}, s32[6,512]{1,0:T(8,128)}, u32[]{:S(2)}) copy-start(s32[6,512]{1,0:T(8,128)} %neighbors.1) | copy-start | bytes 36868
  7.0 23.9 %copy-start.11 = (f32[6,512]{1,0:T(8,128)S(1)}, f32[6,512]{1,0:T(8,128)}, u32[]{:S(2)}) copy-start(f32[6,512]{1,0:T(8,128)} %coef.1) | copy-start | bytes 36868
  7.0 10.3 %collective-permute-start.4 = (bf16[1,528,256]{2,1,0:T(8,128)(2,1)S(1)}, bf16[1,528,256]{2,1,0:T(8,128)(2,1)S(1)}, u32[]{:S(2)}, u32[]{:S(2)}) collective-permute-start(bf16[1,528,256]{2,1,0:T(8,128)(2,1)S(1)} %get-tuple-element.68.refs_0_.refs_7_), channel_id=1, source_target_pairs={{0,2},{2,0},{1,3},{3,1},{4,6},{6,4},{5,7},{7,5},{8,10},{10,8},{9,1... | collective-permute-start | bytes 811016 | tf_op jit(solution)/shard_map/ppermute | solution.py:285
  10.0 20.0 %collective-permute-start.7 = (bf16[1,528,256]{2,1,0:T(8,128)(2,1)S(1)}, bf16[1,528,256]{2,1,0:T(8,128)(2,1)S(1)}, u32[]{:S(2)}, u32[]{:S(2)}) collective-permute-start(bf16[1,528,256]{2,1,0:T(8,128)(2,1)S(1)} %get-tuple-element.67.refs_9_.refs_0_.refs_7_), channel_id=1, source_target_pairs={{0,2},{2,0},{1,3},{3,1},{4,6},{6,4},{5,7},{7,5},{8,10},{10,8},{9,1... | collective-permute-start | bytes 811016 | tf_op jit(solution)/shard_map/ppermute | solution.py:285
  10.1 22.6 %collective-permute-start.5 = (bf16[1,528,256]{2,1,0:T(8,128)(2,1)S(1)}, bf16[1,528,256]{2,1,0:T(8,128)(2,1)S(1)}, u32[]{:S(2)}, u32[]{:S(2)}) collective-permute-start(bf16[1,528,256]{2,1,0:T(8,128)(2,1)S(1)} %get-tuple-element.68.refs_0_.refs_7_), channel_id=1, source_target_pairs={{0,1},{1,0},{2,3},{3,2},{4,5},{5,4},{6,7},{7,6},{8,9},{9,8},{10,11... | collective-permute-start | bytes 811016 | tf_op jit(solution)/shard_map/ppermute | solution.py:219
  10.1 0.7 %copy-start.12 = (s32[2,2,128]{2,1,0:T(2,128)S(1)}, s32[2,2,128]{2,1,0:T(2,128)}, u32[]{:S(2)}) copy-start(s32[2,2,128]{2,1,0:T(2,128)} %param.17) | copy-start | bytes 6148
  10.8 0.7 %copy-start.13 = (f32[2,2,128]{2,1,0:T(2,128)S(1)}, f32[2,2,128]{2,1,0:T(2,128)}, u32[]{:S(2)}) copy-start(f32[2,2,128]{2,1,0:T(2,128)} %param.18) | copy-start | bytes 6148
  11.4 0.7 %copy-start.14 = (s32[2,128]{1,0:T(2,128)S(1)}, s32[2,128]{1,0:T(2,128)}, u32[]{:S(2)}) copy-start(s32[2,128]{1,0:T(2,128)} %recv.1) | copy-start | bytes 3076
  17.3 15.9 %collective-permute-start.6 = (bf16[1,528,256]{2,1,0:T(8,128)(2,1)S(1)}, bf16[1,528,256]{2,1,0:T(8,128)(2,1)S(1)}, u32[]{:S(2)}, u32[]{:S(2)}) collective-permute-start(bf16[1,528,256]{2,1,0:T(8,128)(2,1)S(1)} %collective-permute-done.4.refs_1_.refs_8_), channel_id=1, source_target_pairs={{0,1},{1,0},{2,3},{3,2},{4,5},{5,4},{6,7},{7,6},{8,9},{9,8},{10,11... | collective-permute-start | bytes 811016 | tf_op jit(solution)/shard_map/ppermute | solution.py:219
  18.5 6.3 %collective-permute-start = (bf16[128,256]{1,0:T(8,128)(2,1)S(1)}, bf16[128,256]{1,0:T(8,128)(2,1)S(1)}, u32[]{:S(2)}, u32[]{:S(2)}) collective-permute-start(bf16[128,256]{1,0:T(8,128)(2,1)S(1)} %get-tuple-element.38), channel_id=1, source_target_pairs={{0,4},{1,7},{4,0},{5,3},{8,12},{9,15},{12,8},{13,11},{16,20},{17,2... | collective-permute-start | bytes 196616 | tf_op jit(solution)/shard_map/ppermute | solution.py:277
  22.5 12.6 %collective-permute-start.8 = (bf16[1,528,256]{2,1,0:T(8,128)(2,1)S(1)}, bf16[1,528,256]{2,1,0:T(8,128)(2,1)S(1)}, u32[]{:S(2)}, u32[]{:S(2)}) collective-permute-start(bf16[1,528,256]{2,1,0:T(8,128)(2,1)S(1)} %get-tuple-element.67.refs_9_.refs_0_.refs_7_), channel_id=1, source_target_pairs={{0,1},{1,0},{2,3},{3,2},{4,5},{5,4},{6,7},{7,6},{8,9},{9,8},{10,11... | collective-permute-start | bytes 811016 | tf_op jit(solution)/shard_map/ppermute | solution.py:219
  24.8 8.0 %collective-permute-start.2 = (bf16[128,256]{1,0:T(8,128)(2,1)S(1)}, bf16[128,256]{1,0:T(8,128)(2,1)S(1)}, u32[]{:S(2)}, u32[]{:S(2)}) collective-permute-start(bf16[128,256]{1,0:T(8,128)(2,1)S(1)} %get-tuple-element.39), channel_id=1, source_target_pairs={{0,8},{1,11},{4,12},{5,15},{8,0},{9,3},{12,4},{13,7},{16,24},{17,2... | collective-permute-start | bytes 196616 | tf_op jit(solution)/shard_map/ppermute | solution.py:277
  30.0 5.1 %collective-permute-start.9 = (bf16[1,528,256]{2,1,0:T(8,128)(2,1)S(1)}, bf16[1,528,256]{2,1,0:T(8,128)(2,1)S(1)}, u32[]{:S(2)}, u32[]{:S(2)}) collective-permute-start(bf16[1,528,256]{2,1,0:T(8,128)(2,1)S(1)} %collective-permute-done.7.refs_10_.refs_1_.refs_8_), channel_id=1, source_target_pairs={{0,1},{1,0},{2,3},{3,2},{4,5},{5,4},{6,7},{7,6},{8,9},{9,8},{10,11... | collective-permute-start | bytes 811016 | tf_op jit(solution)/shard_map/ppermute | solution.py:219
  32.7 2.4 %collective-permute-start.1 = (bf16[128,256]{1,0:T(8,128)(2,1)S(1)}, bf16[128,256]{1,0:T(8,128)(2,1)S(1)}, u32[]{:S(2)}, u32[]{:S(2)}) collective-permute-start(bf16[128,256]{1,0:T(8,128)(2,1)S(1)} %collective-permute-done.refs_0_), channel_id=1, source_target_pairs={{0,1},{1,0},{2,3},{3,2},{4,5},{5,4},{6,7},{7,6},{8,9},{9,8},{10,11... | collective-permute-start | bytes 196616 | tf_op jit(solution)/shard_map/ppermute | solution.py:219
  32.7 2.4 %collective-permute-start.3 = (bf16[128,256]{1,0:T(8,128)(2,1)S(1)}, bf16[128,256]{1,0:T(8,128)(2,1)S(1)}, u32[]{:S(2)}, u32[]{:S(2)}) collective-permute-start(bf16[128,256]{1,0:T(8,128)(2,1)S(1)} %collective-permute-done.2.refs_2_), channel_id=1, source_target_pairs={{0,1},{1,0},{2,3},{3,2},{4,5},{5,4},{6,7},{7,6},{8,9},{9,8},{10,11... | collective-permute-start | bytes 196616 | tf_op jit(solution)/shard_map/ppermute | solution.py:219
  37.0 7.7 %collective-permute-start.10 = (bf16[128,256]{1,0:T(8,128)(2,1)S(1)}, bf16[128,256]{1,0:T(8,128)(2,1)S(1)}, u32[]{:S(2)}, u32[]{:S(2)}) collective-permute-start(bf16[128,256]{1,0:T(8,128)(2,1)S(1)} %get-tuple-element.46), channel_id=1, source_target_pairs={{0,4},{4,0},{8,12},{12,8},{1,5},{5,1},{9,13},{13,9},{2,6},{6,2},{1... | collective-permute-start | bytes 196616 | tf_op jit(solution)/shard_map/ppermute | solution.py:328
  39.6 6.8 %collective-permute-start.11 = (bf16[128,256]{1,0:T(8,128)(2,1)S(1)}, bf16[128,256]{1,0:T(8,128)(2,1)S(1)}, u32[]{:S(2)}, u32[]{:S(2)}) collective-permute-start(bf16[128,256]{1,0:T(8,128)(2,1)S(1)} %get-tuple-element.47), channel_id=1, source_target_pairs={{0,8},{4,12},{8,0},{12,4},{1,9},{5,13},{9,1},{13,5},{2,10},{6,14},... | collective-permute-start | bytes 196616 | tf_op jit(solution)/shard_map/ppermute | solution.py:328
  48.2 4.9 %collective-permute-start.12 = (bf16[128,256]{1,0:T(8,128)(2,1)S(1)}, bf16[128,256]{1,0:T(8,128)(2,1)S(1)}, u32[]{:S(2)}, u32[]{:S(2)}) collective-permute-start(bf16[128,256]{1,0:T(8,128)(2,1)S(1)} %get-tuple-element.53), channel_id=1, source_target_pairs={{0,4},{4,0},{8,12},{12,8},{1,5},{5,1},{9,13},{13,9},{2,6},{6,2},{1... | collective-permute-start | bytes 196616 | tf_op jit(solution)/shard_map/ppermute | solution.py:328
  48.6 5.2 %collective-permute-start.13 = (bf16[128,256]{1,0:T(8,128)(2,1)S(1)}, bf16[128,256]{1,0:T(8,128)(2,1)S(1)}, u32[]{:S(2)}, u32[]{:S(2)}) collective-permute-start(bf16[128,256]{1,0:T(8,128)(2,1)S(1)} %get-tuple-element.54), channel_id=1, source_target_pairs={{0,8},{4,12},{8,0},{12,4},{1,9},{5,13},{9,1},{13,5},{2,10},{6,14},... | collective-permute-start | bytes 196616 | tf_op jit(solution)/shard_map/ppermute | solution.py:328
  55.6 5.1 %collective-permute-start.14 = (bf16[128,256]{1,0:T(8,128)(2,1)S(1)}, bf16[128,256]{1,0:T(8,128)(2,1)S(1)}, u32[]{:S(2)}, u32[]{:S(2)}) collective-permute-start(bf16[128,256]{1,0:T(8,128)(2,1)S(1)} %get-tuple-element.60), channel_id=1, source_target_pairs={{0,4},{4,0},{8,12},{12,8},{1,5},{5,1},{9,13},{13,9},{2,6},{6,2},{1... | collective-permute-start | bytes 196616 | tf_op jit(solution)/shard_map/ppermute | solution.py:328
  57.3 5.9 %collective-permute-start.15 = (bf16[128,256]{1,0:T(8,128)(2,1)S(1)}, bf16[128,256]{1,0:T(8,128)(2,1)S(1)}, u32[]{:S(2)}, u32[]{:S(2)}) collective-permute-start(bf16[128,256]{1,0:T(8,128)(2,1)S(1)} %get-tuple-element.61), channel_id=1, source_target_pairs={{0,8},{4,12},{8,0},{12,4},{1,9},{5,13},{9,1},{13,5},{2,10},{6,14},... | collective-permute-start | bytes 196616 | tf_op jit(solution)/shard_map/ppermute | solution.py:328

commit v2 on v1

v2 whole, which is shorter than its diff:
```python
import functools

import jax
import jax.numpy as jnp
from jax import lax
from jax.experimental import pallas as pl
from jax.experimental.pallas import tpu as pltpu
from jax.sharding import PartitionSpec as P

F32 = jnp.float32
BF16 = jnp.bfloat16
VMEM = pl.BlockSpec(memory_space=pltpu.VMEM)
SMEM = pl.BlockSpec(memory_space=pltpu.SMEM)
HBM = pl.BlockSpec(memory_space=pltpu.HBM)
LANES = 128


def dot(a, b):
    return jnp.dot(a, b, preferred_element_type=F32)


def kernel_call(body, outs, operands, flops, smem=1, space=VMEM, scratch=(), limit=24):
    return pl.pallas_call(
        body,
        out_shape=outs,
        in_specs=[SMEM] * smem + [space] * (len(operands) - smem),
        out_specs=jax.tree.map(lambda _: VMEM, outs),
        scratch_shapes=scratch,
        cost_estimate=pl.CostEstimate(flops=flops, bytes_accessed=1 << 16, transcendentals=0),
        compiler_params=pltpu.CompilerParams(vmem_limit_bytes=limit * 1024 * 1024),
    )(*operands)


def shape(dims, dtype):
    return jax.ShapeDtypeStruct(dims, dtype)


VECTORS = 16


def start_kernel(
    held,
    waves,
    place,
    latents,
    w_edge,
    w_in,
    w_out,
    e_bias,
    e_gain,
    n_bias,
    g_norm,
    b_norm,
    src,
    coef,
    recv,
    *refs,
):
    edge_whole, edge_pack, *refs = refs
    node_packs, refs = refs[:held], refs[held:]
    latent, early, src_here, coef_here, recv_here, *vectors, sem = refs
    half = w_out.shape[1]
    width = w_out.shape[2]
    mine = pl.multiple_of(place[1] * half, half)
    copies = []

    def fetch(source, target):
        copy = pltpu.make_async_copy(source, target, sem.at[len(copies)])
        copy.start()
        copies.append(copy)

    for ref, here in zip((e_bias, e_gain, n_bias, g_norm, b_norm), vectors):
        fetch(ref, here)
    for j in range(held):
        fetch(w_edge.at[j, pl.ds(mine, half)], edge_pack.at[j, pl.ds(0, half)])
    for j in range(held):
        fetch(w_in.at[j, pl.ds(0, width)], node_packs[j].at[pl.ds(0, width), pl.ds(0, half)])
        fetch(w_in.at[j, pl.ds(width, width)], node_packs[j].at[pl.ds(0, width), pl.ds(half, half)])
        fetch(w_out.at[j], node_packs[j].at[pl.ds(width, half)])
    fetch(src, src_here)
    fetch(coef, coef_here)
    fetch(recv, recv_here)
    for wave in range(waves):
        fetch(latents.at[jnp.minimum(wave * 2 + place[1], latents.shape[0] - 1)], early.at[wave])
    fetch(latents.at[place[0]], latent)
    fetch(w_edge, edge_whole)
    for copy in copies[:5]:
        copy.wait()
    spot = lax.broadcasted_iota(jnp.int32, (VECTORS, width), 0)
    for j in range(held):
        block = jnp.zeros((VECTORS, width), F32)
        for i, here in enumerate(vectors):
            row = here[j : j + 1, :].astype(F32)
            if row.shape[1] == half:
                row = jnp.concatenate([row, row], axis=1)
            block = jnp.where(spot == i, row, block)
        edge_pack[j, half : half + VECTORS, :] = block.astype(BF16)
    for copy in copies[5:]:
        copy.wait()


def columns(rows):
    rows = rows.astype(F32)
    missing = -rows.shape[0] % 8
    if missing:
        rows = jnp.concatenate([rows, jnp.zeros((missing, rows.shape[1]), F32)], axis=0)
    return rows.T


def one_hot_rows(index_columns, coef_columns, count, nodes, hot, spread):
    rows = index_columns.shape[0]
    lane = lax.broadcasted_iota(jnp.int32, (rows, nodes), 1).astype(F32)
    for k in range(count):
        hot[k * rows : (k + 1) * rows, :] = jnp.where(
            index_columns[:, k : k + 1] == lane, 1.0, 0.0
        ).astype(BF16)
        spread[k * rows : (k + 1) * rows, :] = jnp.broadcast_to(
            coef_columns[:, k : k + 1], (rows, LANES)
        )


def first_sums_kernel(rounds, waves, src, coef, recv, early, edge_whole, edge_pack, hot, spread, scatter, *outs):
    slots = recv.shape[1]
    nodes, half = hot.shape[1], edge_pack.shape[1] - VECTORS
    whole = [jnp.concatenate([ref[r] for r in range(rounds)], axis=0) for ref in (src, coef)]
    one_hot_rows(columns(whole[0]), columns(whole[1]), whole[0].shape[0], nodes, hot, spread)
    row = lax.broadcasted_iota(jnp.int32, (nodes, slots), 0)
    for r in range(rounds):
        scatter[:, r * slots : (r + 1) * slots] = jnp.where(recv[r : r + 1, :] == row, 1.0, 0.0).astype(BF16)
    vectors = edge_pack[0, half : half + VECTORS, :].astype(F32)
    for wave in range(waves):
        source = (dot(early[wave], edge_whole[0]) + vectors[0:1, :]).astype(BF16)
        cross_sums(source, vectors[1:2, :], hot, spread, outs[wave * rounds : (wave + 1) * rounds])


def inner_prep_kernel(neighbors, coef, hot, spread, neighbors_here, coef_here, sem):
    copies = [
        pltpu.make_async_copy(neighbors, neighbors_here, sem.at[0]),
        pltpu.make_async_copy(coef, coef_here, sem.at[1]),
    ]
    for copy in copies:
        copy.start()
    for copy in copies:
        copy.wait()
    degree, nodes = neighbors.shape
    one_hot_rows(columns(neighbors_here[...]), columns(coef_here[...]), degree, nodes, hot, spread)


def wide(spread):
    return jnp.concatenate([spread, spread], axis=1)


def cross_sums(source, gain, hot, spread, outs):
    slots = outs[0].shape[0]
    each = hot.shape[0] // (len(outs) * slots)
    for r, out in enumerate(outs):
        total = None
        for x in range(each):
            rows = pl.ds((r * each + x) * slots, slots)
            hidden = jnp.maximum(dot(hot[rows, :], source) + wide(spread[rows, :]) * gain, 0.0)
            total = hidden if total is None else total + hidden
        out[...] = total.astype(BF16)


def choose(which, refs, rows):
    value = refs[0][rows, :]
    for r in range(1, len(refs)):
        value = jnp.where(which == r, refs[r][rows, :], value)
    return value


def edge_weights(place, which, j, edge_whole, mine, other):
    half = mine[0].shape[1] - VECTORS
    first = place[1] == 0
    weights = edge_whole[j]
    vectors = mine[0][j, half : half + VECTORS, :]
    for r in range(1, len(mine)):
        a, b = mine[r][j, 0:half, :], other[r - 1][j, 0:half, :]
        halves = jnp.concatenate([jnp.where(first, a, b), jnp.where(first, b, a)], axis=0)
        weights = jnp.where(which == r, halves, weights)
        vectors = jnp.where(which == r, mine[r][j, half : half + VECTORS, :], vectors)
    return weights, vectors.astype(F32)


def place_of(segment, segments, place):
    return lax.rem(place[0] - segment + segments, segments)


def inner_kernel(segments, segment, j, first, place, edge_whole, *refs):
    mine, other = refs[:segments], refs[segments : 2 * segments - 1]
    table, hot, spread, sums = refs[2 * segments - 1 :]
    nodes = sums.shape[0]
    which = place_of(segment, segments, place)
    weights, vectors = edge_weights(place, which, j, edge_whole, mine, other)
    values = table[...]
    if first:
        values = (dot(values, weights) + vectors[0:1, :]).astype(BF16)
    gain = vectors[1:2, :]
    total = None
    for k in range(hot.shape[0] // nodes):
        rows = pl.ds(k * nodes, nodes)
        hidden = jnp.maximum(dot(hot[rows, :], values) + wide(spread[rows, :]) * gain, 0.0)
        total = hidden if total is None else total + hidden
    sums[...] = total


def weights_kernel(segments, segment, j, place, *refs):
    mine, other = refs[:segments], refs[segments : 2 * segments]
    vec_mine, vec_other = refs[2 * segments : 3 * segments], refs[3 * segments : 4 * segments]
    latent, before, chosen = refs[4 * segments :]
    width = before.shape[1]
    half = width // 2
    which = place_of(segment, segments, place)
    in_a, in_b = (choose(which, refs, slice(0, width)) for refs in (mine, other))
    vectors, other_vectors = (
        choose(which, [ref.at[j] for ref in refs], slice(half, half + VECTORS)).astype(F32)
        for refs in (vec_mine, vec_other)
    )
    bias = jnp.concatenate([vectors[2:3, :half], other_vectors[2:3, :half]], axis=1)
    joined = jnp.concatenate([in_a[:, :half], in_b[:, :half]], axis=1)
    before[...] = dot(latent[...], joined) + bias
    chosen[0:width, :] = jnp.concatenate([in_a[:, half:], in_b[:, half:]], axis=1)
    chosen[width : width + half, :] = choose(which, mine, slice(width, width + half))
    chosen[width + half : 2 * width, :] = choose(which, other, slice(width, width + half))
    chosen[2 * width : 2 * width + VECTORS, :] = vectors.astype(BF16)


def node_kernel(segments, segment, j, last, many, place, *refs):
    arrived, refs = refs[:many], refs[many:]
    latent, sums, before, chosen, scatter = refs[:5]
    nodes, width = sums.shape
    half = width // 2
    rounds = scatter.shape[1] // arrived[0].shape[0]
    per = many // rounds
    blocks = []
    for r in range(rounds):
        block = arrived[r * per][...]
        for i in range(1, per):
            block = block + arrived[r * per + i][...]
        blocks.append(block)
    summed = sums[...] + dot(scatter[...], jnp.concatenate(blocks, axis=0))
    hidden = before[...] + dot(summed.astype(BF16), chosen[0:width, :])
    hidden = jnp.maximum(hidden, 0.0).astype(BF16)
    mixed = dot(hidden[:, :half], chosen[width : width + half, :]).astype(BF16).astype(F32)
    mixed = mixed + dot(hidden[:, half:], chosen[width + half : 2 * width, :]).astype(BF16).astype(F32)
    vectors = chosen[2 * width : 2 * width + VECTORS, :].astype(F32)
    centred = mixed - jnp.mean(mixed, axis=1, keepdims=True)
    spread_of = jnp.mean(centred * centred, axis=1, keepdims=True)
    normed = centred * lax.rsqrt(spread_of + 1e-05) * vectors[3:4, :] + vectors[4:5, :]
    fresh = (latent[...].astype(F32) + normed).astype(BF16)
    if last:
        refs[5][0] = fresh
        return
    edge_whole, *refs = refs[5:]
    mine, other, refs = refs[:segments], refs[segments : 2 * segments - 1], refs[2 * segments - 1 :]
    hot, spread, result, source = refs[:4]
    result[...] = fresh
    which = place_of(segment, segments, place)
    weights, vectors = edge_weights(place, which, j, edge_whole, mine, other)
    table = (dot(fresh, weights) + vectors[0:1, :]).astype(BF16)
    source[...] = table
    cross_sums(table, vectors[1:2, :], hot, spread, refs[4:])


def partner_route(count, r):
    return [(i, i ^ 1 << r) for i in range(count) if i ^ 1 << r < count]


def swap(block):
    return lax.ppermute(block, "chan", [(0, 1), (1, 0)])


def per_device(
    latents,
    neighbors,
    edge_coef,
    cross_src,
    cross_coef,
    recv_node,
    w_edge,
    w_node_in,
    w_node_out,
    edge_bias,
    edge_gain,
    node_bias,
    norm_gain,
    norm_bias,
):
    segments, cores, parts = (lax.axis_size(a) for a in ("segment", "chan", "dom"))
    micro, nodes, width = latents.shape
    held = w_edge.shape[0]
    rounds, slots = recv_node.shape
    degree, edges = neighbors.shape[0], cross_src.shape[0] * cross_src.shape[1]
    assert micro == segments and cores == 2
    place = jnp.stack([lax.axis_index("segment"), lax.axis_index("chan")]).astype(jnp.int32)

    waves = -(-segments // cores)
    half = width // 2
    vectors = (edge_bias, edge_gain, node_bias, norm_gain, norm_bias)
    graph = (cross_src, cross_coef, recv_node)
    outs = [shape((held, width, width), BF16), shape((held, half + VECTORS, width), BF16)]
    outs += [shape((width + half, width), BF16)] * held
    outs += [shape((nodes, width), BF16), shape((waves, nodes, width), BF16)]
    outs += [shape(ref.shape, ref.dtype) for ref in graph]
    edge_whole, edge_pack, *rest = kernel_call(
        functools.partial(start_kernel, held, waves),
        outs,
        (place, *map(lambda v: pltpu.with_memory_space_constraint(v, pltpu.HBM), (latents, w_edge, w_node_in, w_node_out, *vectors, *graph))),
        1 << 28,
        space=HBM,
        scratch=[pltpu.VMEM(ref.shape, ref.dtype) for ref in vectors]
        + [pltpu.SemaphoreType.DMA((5 + 4 * held + 3 + waves + 2,))],
    )
    node_packs, (latent, early, *graph) = rest[:held], rest[held:]

    hot_c, spread_c, scatter, *sums = kernel_call(
        functools.partial(first_sums_kernel, rounds, waves),
        [shape((edges * slots, nodes), BF16), shape((edges * slots, LANES), F32), shape((nodes, rounds * slots), BF16)]
        + [shape((slots, width), BF16)] * (waves * rounds),
        (*graph, early, edge_whole, edge_pack),
        1 << 29,
        smem=0,
    )
    arrived = [[] for _ in range(rounds)]
    for wave in range(waves):
        for r in range(rounds):
            route = []
            for here, there in partner_route(parts, r):
                for core in range(cores):
                    goal = wave * cores + core
                    if goal < segments:
                        route.append(
                            (here * segments * cores + core, (there * segments + goal) * cores + core)
                        )
            block = lax.ppermute(sums[wave * rounds + r], ("dom", "segment", "chan"), route)
            arrived[r] += [block, swap(block)]

    edges_mine, nodes_mine = [edge_pack], [node_packs]
    for r in range(1, segments):
        route = [(i, (i + r) % segments) for i in range(segments)]
        edges_mine.append(lax.ppermute(edge_pack, "segment", route))
        nodes_mine.append([lax.ppermute(pack, "segment", route) for pack in node_packs])
    edges_other = [swap(pack) for pack in edges_mine]
    nodes_other = [[swap(pack) for pack in packs] for packs in nodes_mine]

    hot, spread = kernel_call(
        inner_prep_kernel,
        (shape((degree * nodes, nodes), BF16), shape((degree * nodes, LANES), F32)),
        tuple(pltpu.with_memory_space_constraint(v, pltpu.HBM) for v in (neighbors, edge_coef)),
        1 << 31,
        smem=0,
        space=HBM,
        scratch=[
            pltpu.VMEM(neighbors.shape, neighbors.dtype),
            pltpu.VMEM(edge_coef.shape, edge_coef.dtype),
            pltpu.SemaphoreType.DMA((2,)),
        ],
    )

    total = segments * held
    source = latent
    for layer in range(total):
        segment, j = divmod(layer, held)
        edge_operands = (edge_whole, *edges_mine, *edges_other[1:])
        sums = kernel_call(
            functools.partial(inner_kernel, segments, segment, j, layer == 0),
            shape((nodes, width), F32),
            (place, *edge_operands, source, hot, spread),
            1 << 31,
        )
        before, chosen = kernel_call(
            functools.partial(weights_kernel, segments, segment, j),
            (shape((nodes, width), F32), shape((2 * width + VECTORS, width), BF16)),
            (
                place,
                *[packs[j] for packs in nodes_mine],
                *[packs[j] for packs in nodes_other],
                *edges_mine,
                *edges_other,
                latent,
            ),
            1 << 28,
        )
        blocks = [block for r in range(rounds) for block in arrived[r]]
        last = layer == total - 1
        operands = [place, *blocks, latent, sums, before, chosen, scatter]
        outs = [shape((1, nodes, width), BF16)]
        follow, step = divmod(layer + 1, held)
        if not last:
            operands += [*edge_operands, hot_c, spread_c]
            outs = [shape((nodes, width), BF16)] * 2 + [shape((slots, width), BF16)] * rounds
        results = kernel_call(
            functools.partial(node_kernel, segments, follow, step, last, len(blocks)),
            outs,
            operands,
            1 << 30,
        )
        if last:
            return results[0]
        latent, source, *blocks = results
        arrived = [[lax.ppermute(blocks[r], "dom", partner_route(parts, r))] for r in range(rounds)]


def solution(mesh):
    return jax.shard_map(
        per_device,
        mesh=mesh,
        in_specs=(
            P(None, ("groups", "dom"), None),
            P(None, ("groups", "dom")),
            P(None, ("groups", "dom")),
            P(None, None, ("groups", "dom")),
            P(None, None, ("groups", "dom")),
            P(None, ("groups", "dom")),
            P("segment", None, None),
            P("segment", None, "chan"),
            P("segment", "chan", None),
            P("segment", None),
            P("segment", None),
            P("segment", "chan"),
            P("segment", None),
            P("segment", None),
        ),
        out_specs=P("segment", ("groups", "dom"), None),
        check_vma=False,
    )
```

time: 65.5 us -> 53 us (0.81)
  local copies, waits for them, and re-layouts: 8.31 us -> 0 us
  starting transfers between devices: 27.8 us -> 21.1 us
  Pallas kernels: 17.4 us -> 21.6 us
  waiting for transfers between devices: 11.3 us -> 9.7 us
    unnamed x30 -> x0, local copies, waits for them, and re-layouts: 8.28 us -> none
    ppermute x10 -> x11, starting transfers between devices: 25.2 us -> 18.9 us  [the longest x2 8.36 us: per_device(): lax.ppermute(sums[wave * rounds + r], ('dom', 'segment', 'chan'), route)]
    pallas_call x12 -> x15, Pallas kernels: 17.4 us -> 21.6 us  [kernel_call(): pl.pallas_call(body, out_shape=outs, in_specs=[SMEM] * smem + [space] * (...]
    ppermute x10 -> x11, waiting for transfers between devices: 11.3 us -> 9.67 us  [the longest x6 5.53 us: per_device(): lax.ppermute(blocks[r], 'dom', partner_route(parts, r))]
    ppermute x6 -> x8, starting transfers between devices: 2.62 us -> 2.2 us  [swap(): return lax.ppermute(block, 'chan', [(0, 1), (1, 0)])]
  transfers between devices with their start and end apart: 16 -> 19, of which waited for: 6 -> 6; matrix products, arithmetic and copies ran while one was open for 0% -> 0% of each run, Pallas kernels for 15% -> 26%
where the time goes in v2:
time: 53 us; the launch traced here: 52.7 us
  Pallas kernels  21.6 us (41%)
  starting transfers between devices  21.1 us (40%)
  waiting for transfers between devices  9.7 us (18%)
    pallas_call x15, Pallas kernels, kernel_call(): pl.pallas_call(body, out_shape=outs, in_specs=[SMEM] * smem + [space] * (...  21.6 us
    ppermute x2, starting transfers between devices, per_device(): lax.ppermute(sums[wave * rounds + r], ('dom', 'segment', 'chan'), route)  8.36 us
    ppermute x6, starting transfers between devices, per_device(): lax.ppermute(blocks[r], 'dom', partner_route(parts, r))  7.37 us
    ppermute x6, waiting for transfers between devices, per_device(): lax.ppermute(blocks[r], 'dom', partner_route(parts, r))  5.53 us
    ppermute x1, starting transfers between devices, per_device(): edges_mine.append(lax.ppermute(edge_pack, 'segment', route))  3 us
    ppermute x2, waiting for transfers between devices, per_device(): lax.ppermute(pack, 'segment', route)  2.94 us
    ppermute x8, starting transfers between devices, swap(): return lax.ppermute(block, 'chan', [(0, 1), (1, 0)])  2.2 us
    ppermute x2, waiting for transfers between devices, per_device(): lax.ppermute(sums[wave * rounds + r], ('dom', 'segment', 'chan'), route)  1.2 us
  transfers between devices with their start and end apart: 19, of which 6 were waited for; matrix products, arithmetic and copies ran while one was open for 0% of the time, Pallas kernels for 26%

profile of v2, /device:TPU:0, one launch (start us, length us, event | category | flops | bytes accessed | tf_op | source)
XLA Modules:
  0.0 52.7 jit_solution(12342581655989061371)
XLA Ops:
  0.1 2.2 %shard_map.136 = (bf16[2,256,256]{2,1,0:T(8,128)(2,1)S(1)}, bf16[2,144,256]{2,1,0:T(8,128)(2,1)S(1)}, bf16[384,256]{1,0:T(8,128)(2,1)S(1)}, bf16[384,256]{1,0:T(...) custom-call(s32[2]{0:T(128)S(1)} %pad_add_fusion.place, ...), custom_call_target="tpu_custom_call" | custom-call | flops 268435456 | bytes 65536 | tf_op jit(solution)/shard_map/pallas_call | solution.py:23
  2.2 3.0 %collective-permute-start.4 = (bf16[2,144,256]{2,1,0:T(8,128)(2,1)S(1)}, bf16[2,144,256]{2,1,0:T(8,128)(2,1)S(1)}, u32[]{:S(2)}, u32[]{:S(2)}) collective-permute-start(bf16[2,144,256]{2,1,0:T(8,128)(2,1)S(1)} %get-tuple-element.46.edge_pack.refs_0_.refs_4_.refs_10_.refs_8_), channel_id=1, source_target_pairs={{0,2},{2,0},{1,3},{3,1},{4,6},{6,4},{5,7},{7,5},{8,10},{10,8},{9,1... | collective-permute-start | bytes 442376 | tf_op jit(solution)/shard_map/ppermute | solution.py:341
  5.4 0.7 %shard_map.137 = (bf16[512,512]{1,0:T(8,128)(2,1)S(1)}, f32[512,128]{1,0:T(8,128)S(1)}, bf16[512,256]{1,0:T(8,128)(2,1)S(1)}, bf16[128,256]{1,0:T(8,128)(2,1)S(1)}, bf16[128,256]{1,0:T(8,128)(2,1)S(1)}) custom-call(s32[2,2,128]{2,1,0:T(2,128)S(1)} %get-tuple-element.41.src, f32[2,2,128]{2,1,0:T(2,128)S(1)} %get-tuple-element.42.coef, ...), custom_call_target="tpu_custom_call" | custom-call | flops 536870912 | bytes 65536 | tf_op jit(solution)/shard_map/pallas_call | solution.py:23
  6.1 3.9 %collective-permute-start = (bf16[128,256]{1,0:T(8,128)(2,1)S(1)}, bf16[128,256]{1,0:T(8,128)(2,1)S(1)}, u32[]{:S(2)}, u32[]{:S(2)}) collective-permute-start(bf16[128,256]{1,0:T(8,128)(2,1)S(1)} %get-tuple-element.47), channel_id=1, source_target_pairs={{0,4},{1,7},{4,0},{5,3},{8,12},{9,15},{12,8},{13,11},{16,20},{17,2... | collective-permute-start | bytes 196616 | tf_op jit(solution)/shard_map/ppermute | solution.py:335
  10.0 4.5 %collective-permute-start.2 = (bf16[128,256]{1,0:T(8,128)(2,1)S(1)}, bf16[128,256]{1,0:T(8,128)(2,1)S(1)}, u32[]{:S(2)}, u32[]{:S(2)}) collective-permute-start(bf16[128,256]{1,0:T(8,128)(2,1)S(1)} %get-tuple-element.48), channel_id=1, source_target_pairs={{0,8},{1,11},{4,12},{5,15},{8,0},{9,3},{12,4},{13,7},{16,24},{17,2... | collective-permute-start | bytes 196616 | tf_op jit(solution)/shard_map/ppermute | solution.py:335
  14.6 1.9 %shard_map.138 = (bf16[3072,512]{1,0:T(8,128)(2,1)S(1)}, f32[3072,128]{1,0:T(8,128)S(1)}) custom-call(s32[6,512]{1,0:T(8,128)} %neighbors.1, f32[6,512]{1,0:T(8,128)} %coef.3), custom_call_target="tpu_custom_call" | custom-call | flops 2147483648 | bytes 65536 | tf_op jit(solution)/shard_map/pallas_call | solution.py:23
  16.5 0.6 %collective-permute-start.7 = (bf16[384,256]{1,0:T(8,128)(2,1)S(1)}, bf16[384,256]{1,0:T(8,128)(2,1)S(1)}, u32[]{:S(2)}, u32[]{:S(2)}) collective-permute-start(bf16[384,256]{1,0:T(8,128)(2,1)S(1)} %get-tuple-element.52.refs_0_), channel_id=1, source_target_pairs={{0,1},{1,0},{2,3},{3,2},{4,5},{5,4},{6,7},{7,6},{8,9},{9,8},{10,11... | collective-permute-start | bytes 589832 | tf_op jit(solution)/shard_map/ppermute | solution.py:270
  17.1 1.2 %collective-permute-done.2.refs_2_ = bf16[128,256]{1,0:T(8,128)(2,1)S(1)} collective-permute-done((bf16[128,256]{1,0:T(8,128)(2,1)S(1)}, bf16[128,256]{1,0:T(8,128)(2,1)S(1)}, u32[]{:S(2)}, u32[]{:S(2)}) %collective-permute-start.2) | collective-permute-done | bytes 65568 | tf_op jit(solution)/shard_map/ppermute | solution.py:335
  18.3 0.9 %collective-permute-start.1 = (bf16[128,256]{1,0:T(8,128)(2,1)S(1)}, bf16[128,256]{1,0:T(8,128)(2,1)S(1)}, u32[]{:S(2)}, u32[]{:S(2)}) collective-permute-start(bf16[128,256]{1,0:T(8,128)(2,1)S(1)} %collective-permute-done.refs_0_), channel_id=1, source_target_pairs={{0,1},{1,0},{2,3},{3,2},{4,5},{5,4},{6,7},{7,6},{8,9},{9,8},{10,11... | collective-permute-start | bytes 196616 | tf_op jit(solution)/shard_map/ppermute | solution.py:270
  19.3 0.4 collective-permute-start.8
  19.8 1.7 %shard_map.139.refs_5_ = f32[512,256]{1,0:T(8,128)S(1)} custom-call(s32[2]{0:T(128)S(1)} %pad_add_fusion.place, bf16[2,256,256]{2,1,0:T(8,128)(2,1)S(1)} %get-tuple-element.45.edge_whole.refs_9_.refs_7_, bf16[2,144,256]{2,1,0:T(8,128)(2,1)S(1)} %get-tuple-element.46.edge_pack.refs_0_.refs_4_.refs_10_.refs_8_, ...), custom_call_target="tpu_custom_call" | custom-call | flops 2147483648 | bytes 65536 | tf_op jit(solution)/shard_map/pallas_call | solution.py:23
  21.6 2.9 %collective-permute-done.12.refs_1_ = bf16[384,256]{1,0:T(8,128)(2,1)S(1)} collective-permute-done((bf16[384,256]{1,0:T(8,128)(2,1)S(1)}, bf16[384,256]{1,0:T(8,128)(2,1)S(1)}, u32[]{:S(2)}, u32[]{:S(2)}) %collective-permute-start.12) | collective-permute-done | bytes 196640 | tf_op jit(solution)/shard_map/ppermute | solution.py:342
  24.6 0.8 %shard_map.140 = (f32[512,256]{1,0:T(8,128)S(1)}, bf16[528,256]{1,0:T(8,128)(2,1)S(1)}) custom-call(s32[2]{0:T(128)S(1)} %pad_add_fusion.place, bf16[384,256]{1,0:T(8,128)(2,1)S(1)} %get-tuple-element.52.refs_0_, bf16[384,256]{1,0:T(8,128)(2,1)S(1)} %collective-permute-done.6.refs_1_, bf16[384,256]{1,0:T(8,128)(2,1)S(1)} %collective-permute-done.7.refs_2_, ...), custom_call_target="tpu_custom_call" | custom-call | flops 268435456 | bytes 65536 | tf_op jit(solution)/shard_map/pallas_call | solution.py:23
  25.4 1.8 %shard_map.141 = (bf16[512,256]{1,0:T(8,128)(2,1)S(1)}, bf16[512,256]{1,0:T(8,128)(2,1)S(1)}, bf16[128,256]{1,0:T(8,128)(2,1)S(1)}, bf16[128,256]{1,0:T(8,128)(2,1)S(1)}) custom-call(s32[2]{0:T(128)S(1)} %pad_add_fusion.place, bf16[128,256]{1,0:T(8,128)(2,1)S(1)} %collective-permute-done.refs_0_, bf16[128,256]{1,0:T(8,128)(2,1)S(1)} %collective-permute-done.1.refs_1_, ...), custom_call_target="tpu_custom_call" | custom-call | flops 1073741824 | bytes 65536 | tf_op jit(solution)/shard_map/pallas_call | solution.py:23
  27.3 2.0 %collective-permute-start.11 = (bf16[128,256]{1,0:T(8,128)(2,1)S(1)}, bf16[128,256]{1,0:T(8,128)(2,1)S(1)}, u32[]{:S(2)}, u32[]{:S(2)}) collective-permute-start(bf16[128,256]{1,0:T(8,128)(2,1)S(1)} %get-tuple-element.59), channel_id=1, source_target_pairs={{0,8},{4,12},{8,0},{12,4},{1,9},{5,13},{9,1},{13,5},{2,10},{6,14},... | collective-permute-start | bytes 196616 | tf_op jit(solution)/shard_map/ppermute | solution.py:401
  29.3 1.5 %shard_map.142.refs_3_ = f32[512,256]{1,0:T(8,128)S(1)} custom-call(s32[2]{0:T(128)S(1)} %pad_add_fusion.place, bf16[2,256,256]{2,1,0:T(8,128)(2,1)S(1)} %get-tuple-element.45.edge_whole.refs_9_.refs_7_, bf16[2,144,256]{2,1,0:T(8,128)(2,1)S(1)} %get-tuple-element.46.edge_pack.refs_0_.refs_4_.refs_10_.refs_8_, ...), custom_call_target="tpu_custom_call" | custom-call | flops 2147483648 | bytes 65536 | tf_op jit(solution)/shard_map/pallas_call | solution.py:23
  30.8 0.8 %shard_map.143 = (f32[512,256]{1,0:T(8,128)S(1)}, bf16[528,256]{1,0:T(8,128)(2,1)S(1)}) custom-call(s32[2]{0:T(128)S(1)} %pad_add_fusion.place, bf16[384,256]{1,0:T(8,128)(2,1)S(1)} %get-tuple-element.62.refs_0_, bf16[384,256]{1,0:T(8,128)(2,1)S(1)} %collective-permute-done.12.refs_1_, bf16[384,256]{1,0:T(8,128)(2,1)S(1)} %collective-permute-done.13.refs_2_, ...), custom_call_target="tpu_custom_call" | custom-call | flops 268435456 | bytes 65536 | tf_op jit(solution)/shard_map/pallas_call | solution.py:23
  31.6 1.3 %collective-permute-done.10.refs_0_ = bf16[128,256]{1,0:T(8,128)(2,1)S(1)} collective-permute-done((bf16[128,256]{1,0:T(8,128)(2,1)S(1)}, bf16[128,256]{1,0:T(8,128)(2,1)S(1)}, u32[]{:S(2)}, u32[]{:S(2)}) %collective-permute-start.10) | collective-permute-done | bytes 65568 | tf_op jit(solution)/shard_map/ppermute | solution.py:401
  32.9 1.3 %collective-permute-done.11.refs_1_ = bf16[128,256]{1,0:T(8,128)(2,1)S(1)} collective-permute-done((bf16[128,256]{1,0:T(8,128)(2,1)S(1)}, bf16[128,256]{1,0:T(8,128)(2,1)S(1)}, u32[]{:S(2)}, u32[]{:S(2)}) %collective-permute-start.11) | collective-permute-done | bytes 65568 | tf_op jit(solution)/shard_map/ppermute | solution.py:401
  34.2 1.8 %shard_map.144 = (bf16[512,256]{1,0:T(8,128)(2,1)S(1)}, bf16[512,256]{1,0:T(8,128)(2,1)S(1)}, bf16[128,256]{1,0:T(8,128)(2,1)S(1)}, bf16[128,256]{1,0:T(8,128)(2,1)S(1)}) custom-call(s32[2]{0:T(128)S(1)} %pad_add_fusion.place, bf16[128,256]{1,0:T(8,128)(2,1)S(1)} %collective-permute-done.10.refs_0_, bf16[128,256]{1,0:T(8,128)(2,1)S(1)} %collective-permute-done.11.refs_1_, ...), custom_call_target="tpu_custom_call" | custom-call | flops 1073741824 | bytes 65536 | tf_op jit(solution)/shard_map/pallas_call | solution.py:23
  36.0 0.4 collective-permute-start.15
  36.4 2.2 %collective-permute-start.16 = (bf16[128,256]{1,0:T(8,128)(2,1)S(1)}, bf16[128,256]{1,0:T(8,128)(2,1)S(1)}, u32[]{:S(2)}, u32[]{:S(2)}) collective-permute-start(bf16[128,256]{1,0:T(8,128)(2,1)S(1)} %get-tuple-element.66), channel_id=1, source_target_pairs={{0,8},{4,12},{8,0},{12,4},{1,9},{5,13},{9,1},{13,5},{2,10},{6,14},... | collective-permute-start | bytes 196616 | tf_op jit(solution)/shard_map/ppermute | solution.py:401
  38.5 1.5 %shard_map.145.refs_3_ = f32[512,256]{1,0:T(8,128)S(1)} custom-call(s32[2]{0:T(128)S(1)} %pad_add_fusion.place, bf16[2,256,256]{2,1,0:T(8,128)(2,1)S(1)} %get-tuple-element.45.edge_whole.refs_9_.refs_7_, bf16[2,144,256]{2,1,0:T(8,128)(2,1)S(1)} %get-tuple-element.46.edge_pack.refs_0_.refs_4_.refs_10_.refs_8_, ...), custom_call_target="tpu_custom_call" | custom-call | flops 2147483648 | bytes 65536 | tf_op jit(solution)/shard_map/pallas_call | solution.py:23
  40.1 0.8 %shard_map.146 = (f32[512,256]{1,0:T(8,128)S(1)}, bf16[528,256]{1,0:T(8,128)(2,1)S(1)}) custom-call(s32[2]{0:T(128)S(1)} %pad_add_fusion.place, bf16[384,256]{1,0:T(8,128)(2,1)S(1)} %get-tuple-element.52.refs_0_, bf16[384,256]{1,0:T(8,128)(2,1)S(1)} %collective-permute-done.6.refs_1_, bf16[384,256]{1,0:T(8,128)(2,1)S(1)} %collective-permute-done.7.refs_2_, ...), custom_call_target="tpu_custom_call" | custom-call | flops 268435456 | bytes 65536 | tf_op jit(solution)/shard_map/pallas_call | solution.py:23
  40.9 0.7 %collective-permute-done.16.refs_1_ = bf16[128,256]{1,0:T(8,128)(2,1)S(1)} collective-permute-done((bf16[128,256]{1,0:T(8,128)(2,1)S(1)}, bf16[128,256]{1,0:T(8,128)(2,1)S(1)}, u32[]{:S(2)}, u32[]{:S(2)}) %collective-permute-start.16) | collective-permute-done | bytes 65568 | tf_op jit(solution)/shard_map/ppermute | solution.py:401
  41.5 1.8 %shard_map.147 = (bf16[512,256]{1,0:T(8,128)(2,1)S(1)}, bf16[512,256]{1,0:T(8,128)(2,1)S(1)}, bf16[128,256]{1,0:T(8,128)(2,1)S(1)}, bf16[128,256]{1,0:T(8,128)(2,1)S(1)}) custom-call(s32[2]{0:T(128)S(1)} %pad_add_fusion.place, bf16[128,256]{1,0:T(8,128)(2,1)S(1)} %collective-permute-done.15.refs_0_, bf16[128,256]{1,0:T(8,128)(2,1)S(1)} %collective-permute-done.16.refs_1_, ...), custom_call_target="tpu_custom_call" | custom-call | flops 1073741824 | bytes 65536 | tf_op jit(solution)/shard_map/pallas_call | solution.py:23
  43.3 1.8 %collective-permute-start.17 = (bf16[128,256]{1,0:T(8,128)(2,1)S(1)}, bf16[128,256]{1,0:T(8,128)(2,1)S(1)}, u32[]{:S(2)}, u32[]{:S(2)}) collective-permute-start(bf16[128,256]{1,0:T(8,128)(2,1)S(1)} %get-tuple-element.71), channel_id=1, source_target_pairs={{0,4},{4,0},{8,12},{12,8},{1,5},{5,1},{9,13},{13,9},{2,6},{6,2},{1... | collective-permute-start | bytes 196616 | tf_op jit(solution)/shard_map/ppermute | solution.py:401
  45.1 1.0 %collective-permute-start.18 = (bf16[128,256]{1,0:T(8,128)(2,1)S(1)}, bf16[128,256]{1,0:T(8,128)(2,1)S(1)}, u32[]{:S(2)}, u32[]{:S(2)}) collective-permute-start(bf16[128,256]{1,0:T(8,128)(2,1)S(1)} %get-tuple-element.72), channel_id=1, source_target_pairs={{0,8},{4,12},{8,0},{12,4},{1,9},{5,13},{9,1},{13,5},{2,10},{6,14},... | collective-permute-start | bytes 196616 | tf_op jit(solution)/shard_map/ppermute | solution.py:401
  46.1 1.5 %shard_map.148.refs_3_ = f32[512,256]{1,0:T(8,128)S(1)} custom-call(s32[2]{0:T(128)S(1)} %pad_add_fusion.place, bf16[2,256,256]{2,1,0:T(8,128)(2,1)S(1)} %get-tuple-element.45.edge_whole.refs_9_.refs_7_, bf16[2,144,256]{2,1,0:T(8,128)(2,1)S(1)} %get-tuple-element.46.edge_pack.refs_0_.refs_4_.refs_10_.refs_8_, ...), custom_call_target="tpu_custom_call" | custom-call | flops 2147483648 | bytes 65536 | tf_op jit(solution)/shard_map/pallas_call | solution.py:23
  47.6 0.8 %shard_map.149 = (f32[512,256]{1,0:T(8,128)S(1)}, bf16[528,256]{1,0:T(8,128)(2,1)S(1)}) custom-call(s32[2]{0:T(128)S(1)} %pad_add_fusion.place, bf16[384,256]{1,0:T(8,128)(2,1)S(1)} %get-tuple-element.62.refs_0_, bf16[384,256]{1,0:T(8,128)(2,1)S(1)} %collective-permute-done.12.refs_1_, bf16[384,256]{1,0:T(8,128)(2,1)S(1)} %collective-permute-done.13.refs_2_, ...), custom_call_target="tpu_custom_call" | custom-call | flops 268435456 | bytes 65536 | tf_op jit(solution)/shard_map/pallas_call | solution.py:23
  48.4 2.3 %collective-permute-done.18.refs_1_ = bf16[128,256]{1,0:T(8,128)(2,1)S(1)} collective-permute-done((bf16[128,256]{1,0:T(8,128)(2,1)S(1)}, bf16[128,256]{1,0:T(8,128)(2,1)S(1)}, u32[]{:S(2)}, u32[]{:S(2)}) %collective-permute-start.18) | collective-permute-done | bytes 65568 | tf_op jit(solution)/shard_map/ppermute | solution.py:401
  50.7 2.0 %shard_map.150 = bf16[1,512,256]{2,1,0:T(8,128)(2,1)} custom-call(s32[2]{0:T(128)S(1)} %pad_add_fusion.place, bf16[128,256]{1,0:T(8,128)(2,1)S(1)} %collective-permute-done.17.refs_0_, bf16[128,256]{1,0:T(8,128)(2,1)S(1)} %collective-permute-done.18.refs_1_, bf16[512,256]{1,0:T(8,128)(2,1)S(1)} %get-tuple-element.73.refs_8_.refs_2_, ...), custom_call_target="tpu_custom_call" | custom-call | flops 1073741824 | bytes 65536 | tf_op jit(solution)/shard_map/pallas_call | solution.py:23
  (22 shorter events, 0.6 us)
Async XLA Ops:
  2.2 12.3 %collective-permute-start.4 = (bf16[2,144,256]{2,1,0:T(8,128)(2,1)S(1)}, bf16[2,144,256]{2,1,0:T(8,128)(2,1)S(1)}, u32[]{:S(2)}, u32[]{:S(2)}) collective-permute-start(bf16[2,144,256]{2,1,0:T(8,128)(2,1)S(1)} %get-tuple-element.46.edge_pack.refs_0_.refs_4_.refs_10_.refs_8_), channel_id=1, source_target_pairs={{0,2},{2,0},{1,3},{3,1},{4,6},{6,4},{5,7},{7,5},{8,10},{10,8},{9,1... | collective-permute-start | bytes 442376 | tf_op jit(solution)/shard_map/ppermute | solution.py:341
  5.2 13.1 %collective-permute-start.9 = (bf16[2,144,256]{2,1,0:T(8,128)(2,1)S(1)}, bf16[2,144,256]{2,1,0:T(8,128)(2,1)S(1)}, u32[]{:S(2)}, u32[]{:S(2)}) collective-permute-start(bf16[2,144,256]{2,1,0:T(8,128)(2,1)S(1)} %get-tuple-element.46.edge_pack.refs_0_.refs_4_.refs_10_.refs_8_), channel_id=1, source_target_pairs={{0,1},{1,0},{2,3},{3,2},{4,5},{5,4},{6,7},{7,6},{8,9},{9,8},{10,11... | collective-permute-start | bytes 442376 | tf_op jit(solution)/shard_map/ppermute | solution.py:270
  5.3 14.0 %collective-permute-start.6 = (bf16[384,256]{1,0:T(8,128)(2,1)S(1)}, bf16[384,256]{1,0:T(8,128)(2,1)S(1)}, u32[]{:S(2)}, u32[]{:S(2)}) collective-permute-start(bf16[384,256]{1,0:T(8,128)(2,1)S(1)} %get-tuple-element.52.refs_0_), channel_id=1, source_target_pairs={{0,2},{2,0},{1,3},{3,1},{4,6},{6,4},{5,7},{7,5},{8,10},{10,8},{9,1... | collective-permute-start | bytes 589832 | tf_op jit(solution)/shard_map/ppermute | solution.py:342
  6.1 10.4 %collective-permute-start = (bf16[128,256]{1,0:T(8,128)(2,1)S(1)}, bf16[128,256]{1,0:T(8,128)(2,1)S(1)}, u32[]{:S(2)}, u32[]{:S(2)}) collective-permute-start(bf16[128,256]{1,0:T(8,128)(2,1)S(1)} %get-tuple-element.47), channel_id=1, source_target_pairs={{0,4},{1,7},{4,0},{5,3},{8,12},{9,15},{12,8},{13,11},{16,20},{17,2... | collective-permute-start | bytes 196616 | tf_op jit(solution)/shard_map/ppermute | solution.py:335
  10.0 8.3 %collective-permute-start.2 = (bf16[128,256]{1,0:T(8,128)(2,1)S(1)}, bf16[128,256]{1,0:T(8,128)(2,1)S(1)}, u32[]{:S(2)}, u32[]{:S(2)}) collective-permute-start(bf16[128,256]{1,0:T(8,128)(2,1)S(1)} %get-tuple-element.48), channel_id=1, source_target_pairs={{0,8},{1,11},{4,12},{5,15},{8,0},{9,3},{12,4},{13,7},{16,24},{17,2... | collective-permute-start | bytes 196616 | tf_op jit(solution)/shard_map/ppermute | solution.py:335
  14.5 4.8 %collective-permute-start.5 = (bf16[2,144,256]{2,1,0:T(8,128)(2,1)S(1)}, bf16[2,144,256]{2,1,0:T(8,128)(2,1)S(1)}, u32[]{:S(2)}, u32[]{:S(2)}) collective-permute-start(bf16[2,144,256]{2,1,0:T(8,128)(2,1)S(1)} %collective-permute-done.4.refs_1_.refs_5_.refs_11_.refs_9_), channel_id=1, source_target_pairs={{0,1},{1,0},{2,3},{3,2},{4,5},{5,4},{6,7},{7,6},{8,9},{9,8},{10,11... | collective-permute-start | bytes 442376 | tf_op jit(solution)/shard_map/ppermute | solution.py:270
  16.5 5.0 %collective-permute-start.7 = (bf16[384,256]{1,0:T(8,128)(2,1)S(1)}, bf16[384,256]{1,0:T(8,128)(2,1)S(1)}, u32[]{:S(2)}, u32[]{:S(2)}) collective-permute-start(bf16[384,256]{1,0:T(8,128)(2,1)S(1)} %get-tuple-element.52.refs_0_), channel_id=1, source_target_pairs={{0,1},{1,0},{2,3},{3,2},{4,5},{5,4},{6,7},{7,6},{8,9},{9,8},{10,11... | collective-permute-start | bytes 589832 | tf_op jit(solution)/shard_map/ppermute | solution.py:270
  18.3 6.3 %collective-permute-start.12 = (bf16[384,256]{1,0:T(8,128)(2,1)S(1)}, bf16[384,256]{1,0:T(8,128)(2,1)S(1)}, u32[]{:S(2)}, u32[]{:S(2)}) collective-permute-start(bf16[384,256]{1,0:T(8,128)(2,1)S(1)} %get-tuple-element.62.refs_0_), channel_id=1, source_target_pairs={{0,2},{2,0},{1,3},{3,1},{4,6},{6,4},{5,7},{7,5},{8,10},{10,8},{9,1... | collective-permute-start | bytes 589832 | tf_op jit(solution)/shard_map/ppermute | solution.py:342
  18.3 7.1 %collective-permute-start.1 = (bf16[128,256]{1,0:T(8,128)(2,1)S(1)}, bf16[128,256]{1,0:T(8,128)(2,1)S(1)}, u32[]{:S(2)}, u32[]{:S(2)}) collective-permute-start(bf16[128,256]{1,0:T(8,128)(2,1)S(1)} %collective-permute-done.refs_0_), channel_id=1, source_target_pairs={{0,1},{1,0},{2,3},{3,2},{4,5},{5,4},{6,7},{7,6},{8,9},{9,8},{10,11... | collective-permute-start | bytes 196616 | tf_op jit(solution)/shard_map/ppermute | solution.py:270
  19.2 6.1 %collective-permute-start.3 = (bf16[128,256]{1,0:T(8,128)(2,1)S(1)}, bf16[128,256]{1,0:T(8,128)(2,1)S(1)}, u32[]{:S(2)}, u32[]{:S(2)}) collective-permute-start(bf16[128,256]{1,0:T(8,128)(2,1)S(1)} %collective-permute-done.2.refs_2_), channel_id=1, source_target_pairs={{0,1},{1,0},{2,3},{3,2},{4,5},{5,4},{6,7},{7,6},{8,9},{9,8},{10,11... | collective-permute-start | bytes 196616 | tf_op jit(solution)/shard_map/ppermute | solution.py:270
  19.3 5.3 %collective-permute-start.8 = (bf16[384,256]{1,0:T(8,128)(2,1)S(1)}, bf16[384,256]{1,0:T(8,128)(2,1)S(1)}, u32[]{:S(2)}, u32[]{:S(2)}) collective-permute-start(bf16[384,256]{1,0:T(8,128)(2,1)S(1)} %collective-permute-done.6.refs_1_), channel_id=1, source_target_pairs={{0,1},{1,0},{2,3},{3,2},{4,5},{5,4},{6,7},{7,6},{8,9},{9,8},{10,11... | collective-permute-start | bytes 589832 | tf_op jit(solution)/shard_map/ppermute | solution.py:270
  21.5 9.3 %collective-permute-start.13 = (bf16[384,256]{1,0:T(8,128)(2,1)S(1)}, bf16[384,256]{1,0:T(8,128)(2,1)S(1)}, u32[]{:S(2)}, u32[]{:S(2)}) collective-permute-start(bf16[384,256]{1,0:T(8,128)(2,1)S(1)} %get-tuple-element.62.refs_0_), channel_id=1, source_target_pairs={{0,1},{1,0},{2,3},{3,2},{4,5},{5,4},{6,7},{7,6},{8,9},{9,8},{10,11... | collective-permute-start | bytes 589832 | tf_op jit(solution)/shard_map/ppermute | solution.py:270
  24.6 6.2 %collective-permute-start.14 = (bf16[384,256]{1,0:T(8,128)(2,1)S(1)}, bf16[384,256]{1,0:T(8,128)(2,1)S(1)}, u32[]{:S(2)}, u32[]{:S(2)}) collective-permute-start(bf16[384,256]{1,0:T(8,128)(2,1)S(1)} %collective-permute-done.12.refs_1_), channel_id=1, source_target_pairs={{0,1},{1,0},{2,3},{3,2},{4,5},{5,4},{6,7},{7,6},{8,9},{9,8},{10,11... | collective-permute-start | bytes 589832 | tf_op jit(solution)/shard_map/ppermute | solution.py:270
  27.2 5.7 %collective-permute-start.10 = (bf16[128,256]{1,0:T(8,128)(2,1)S(1)}, bf16[128,256]{1,0:T(8,128)(2,1)S(1)}, u32[]{:S(2)}, u32[]{:S(2)}) collective-permute-start(bf16[128,256]{1,0:T(8,128)(2,1)S(1)} %get-tuple-element.58), channel_id=1, source_target_pairs={{0,4},{4,0},{8,12},{12,8},{1,5},{5,1},{9,13},{13,9},{2,6},{6,2},{1... | collective-permute-start | bytes 196616 | tf_op jit(solution)/shard_map/ppermute | solution.py:401
  27.3 6.9 %collective-permute-start.11 = (bf16[128,256]{1,0:T(8,128)(2,1)S(1)}, bf16[128,256]{1,0:T(8,128)(2,1)S(1)}, u32[]{:S(2)}, u32[]{:S(2)}) collective-permute-start(bf16[128,256]{1,0:T(8,128)(2,1)S(1)} %get-tuple-element.59), channel_id=1, source_target_pairs={{0,8},{4,12},{8,0},{12,4},{1,9},{5,13},{9,1},{13,5},{2,10},{6,14},... | collective-permute-start | bytes 196616 | tf_op jit(solution)/shard_map/ppermute | solution.py:401
  36.0 4.9 %collective-permute-start.15 = (bf16[128,256]{1,0:T(8,128)(2,1)S(1)}, bf16[128,256]{1,0:T(8,128)(2,1)S(1)}, u32[]{:S(2)}, u32[]{:S(2)}) collective-permute-start(bf16[128,256]{1,0:T(8,128)(2,1)S(1)} %get-tuple-element.65), channel_id=1, source_target_pairs={{0,4},{4,0},{8,12},{12,8},{1,5},{5,1},{9,13},{13,9},{2,6},{6,2},{1... | collective-permute-start | bytes 196616 | tf_op jit(solution)/shard_map/ppermute | solution.py:401
  36.4 5.2 %collective-permute-start.16 = (bf16[128,256]{1,0:T(8,128)(2,1)S(1)}, bf16[128,256]{1,0:T(8,128)(2,1)S(1)}, u32[]{:S(2)}, u32[]{:S(2)}) collective-permute-start(bf16[128,256]{1,0:T(8,128)(2,1)S(1)} %get-tuple-element.66), channel_id=1, source_target_pairs={{0,8},{4,12},{8,0},{12,4},{1,9},{5,13},{9,1},{13,5},{2,10},{6,14},... | collective-permute-start | bytes 196616 | tf_op jit(solution)/shard_map/ppermute | solution.py:401
  43.3 5.1 %collective-permute-start.17 = (bf16[128,256]{1,0:T(8,128)(2,1)S(1)}, bf16[128,256]{1,0:T(8,128)(2,1)S(1)}, u32[]{:S(2)}, u32[]{:S(2)}) collective-permute-start(bf16[128,256]{1,0:T(8,128)(2,1)S(1)} %get-tuple-element.71), channel_id=1, source_target_pairs={{0,4},{4,0},{8,12},{12,8},{1,5},{5,1},{9,13},{13,9},{2,6},{6,2},{1... | collective-permute-start | bytes 196616 | tf_op jit(solution)/shard_map/ppermute | solution.py:401
  45.1 5.6 %collective-permute-start.18 = (bf16[128,256]{1,0:T(8,128)(2,1)S(1)}, bf16[128,256]{1,0:T(8,128)(2,1)S(1)}, u32[]{:S(2)}, u32[]{:S(2)}) collective-permute-start(bf16[128,256]{1,0:T(8,128)(2,1)S(1)} %get-tuple-element.72), channel_id=1, source_target_pairs={{0,8},{4,12},{8,0},{12,4},{1,9},{5,13},{9,1},{13,5},{2,10},{6,14},... | collective-permute-start | bytes 196616 | tf_op jit(solution)/shard_map/ppermute | solution.py:401

commit v3 on v1

v3 whole, which is shorter than its diff:
```python
import functools

import jax
import jax.numpy as jnp
from jax import lax
from jax.experimental import pallas as pl
from jax.experimental.pallas import tpu as pltpu
from jax.sharding import PartitionSpec as P

F32 = jnp.float32
BF16 = jnp.bfloat16
VMEM = pl.BlockSpec(memory_space=pltpu.VMEM)
SMEM = pl.BlockSpec(memory_space=pltpu.SMEM)
HBM = pl.BlockSpec(memory_space=pltpu.HBM)
ANY = pl.BlockSpec(memory_space=pl.ANY)
LANES = 128


def dot(a, b):
    return jnp.dot(a, b, preferred_element_type=F32)


def kernel_call(body, outs, operands, flops, smem=1, scratch=(), after=0):
    plain = len(operands) - smem - after
    return pl.pallas_call(
        body,
        out_shape=outs,
        in_specs=[SMEM] * smem + [HBM if scratch else VMEM] * plain + [ANY] * after,
        out_specs=jax.tree.map(lambda _: VMEM, outs),
        scratch_shapes=scratch,
        cost_estimate=pl.CostEstimate(flops=flops, bytes_accessed=1 << 16, transcendentals=0),
        compiler_params=pltpu.CompilerParams(vmem_limit_bytes=24 * 1024 * 1024),
    )(*operands)


def shape(dims, dtype):
    return jax.ShapeDtypeStruct(dims, dtype)


VECTORS = 16


def fetch_all(pairs, sem):
    copies = [pltpu.make_async_copy(a, b, sem.at[i]) for i, (a, b) in enumerate(pairs)]
    for copy in copies:
        copy.start()
    return copies


def vector_rows(rows, width):
    spot = lax.broadcasted_iota(jnp.int32, (VECTORS, width), 0)
    block = jnp.zeros((VECTORS, width), F32)
    for i, row in enumerate(rows):
        row = row.astype(F32)
        if row.shape[1] < width:
            row = jnp.concatenate([row] * (width // row.shape[1]), axis=1)
        block = jnp.where(spot == i, row, block)
    return block.astype(BF16)


def edge_rows(width, j):
    half = width // 2
    start = j * (half + VECTORS)
    return slice(start, start + half), slice(start + half, start + half + VECTORS)


def node_rows(width, held, j):
    half = width // 2
    start = 0 if j else edge_rows(width, held)[0].start
    return slice(start, start + width), slice(start + width, start + width + half)


def pack_kernel(place, w_edge, w_in, w_out, e_bias, e_gain, g_norm, b_norm, n_bias, *refs):
    held, half, width = w_out.shape
    packs, vectors, sem = refs[:held], refs[held:-1], refs[-1]
    mine = pl.multiple_of(place[1] * half, half)
    pairs = list(zip((e_bias, e_gain, g_norm, b_norm, n_bias), vectors))
    for j in range(held):
        inner, outer = node_rows(width, held, j)
        pairs += [
            (w_edge.at[j, pl.ds(mine, half)], packs[0].at[edge_rows(width, j)[0]]),
            (w_in.at[j, pl.ds(0, width)], packs[j].at[inner, pl.ds(0, half)]),
            (w_in.at[j, pl.ds(width, width)], packs[j].at[inner, pl.ds(half, half)]),
            (w_out.at[j], packs[j].at[outer]),
        ]
    copies = fetch_all(pairs, sem)
    for copy in copies[:5]:
        copy.wait()
    for j in range(held):
        packs[0][edge_rows(width, j)[1], :] = vector_rows([ref[j : j + 1, :] for ref in vectors], width)
    for copy in copies[5:]:
        copy.wait()


def columns(rows):
    rows = rows.astype(F32)
    missing = -rows.shape[0] % 8
    if missing:
        rows = jnp.concatenate([rows, jnp.zeros((missing, rows.shape[1]), F32)], axis=0)
    return rows.T


def one_hot_rows(index_columns, coef_columns, count, nodes, hot, spread):
    rows = index_columns.shape[0]
    lane = lax.broadcasted_iota(jnp.int32, (rows, nodes), 1).astype(F32)
    for k in range(count):
        hot[k * rows : (k + 1) * rows, :] = jnp.where(
            index_columns[:, k : k + 1] == lane, 1.0, 0.0
        ).astype(BF16)
        spread[k * rows : (k + 1) * rows, :] = jnp.broadcast_to(
            coef_columns[:, k : k + 1], (rows, LANES)
        )


def pieces(values):
    high = values.astype(BF16)
    rest = values - high.astype(F32)
    middle = rest.astype(BF16)
    return high, middle, (rest - middle.astype(F32)).astype(BF16)


def cross_prep_kernel(place, latents, src, coef, recv, _, latent, hot, spread, scatter, *refs):
    rounds, slots = recv.shape
    raw, here, sem = refs[0], refs[1:4], refs[4]
    copies = fetch_all([*zip((src, coef, recv), here), (latents.at[place[0]], latent)], sem)
    for copy in copies[:3]:
        copy.wait()
    nodes, width = latent.shape
    whole = [jnp.concatenate([ref[r] for r in range(rounds)], axis=0) for ref in here[:2]]
    one_hot_rows(columns(whole[0]), columns(whole[1]), whole[0].shape[0], nodes, hot, spread)
    row = lax.broadcasted_iota(jnp.int32, (nodes, slots), 0)
    for r in range(rounds):
        scatter[:, r * slots : (r + 1) * slots] = jnp.where(
            here[2][r : r + 1, :] == row, 1.0, 0.0
        ).astype(BF16)
    copies[3].wait()
    each = src.shape[1] * slots
    mine = pl.multiple_of(place[1] * each, each)
    raw[0:each, :] = dot(hot[pl.ds(mine, each), :], latent[...]).astype(BF16)
    coefs = here[1][place[1]]
    rows = [piece[x : x + 1, :] for x in range(src.shape[1]) for piece in pieces(coefs)]
    raw[each : each + VECTORS, :] = vector_rows(rows, width)


def inner_prep_kernel(neighbors, coef, _, hot, spread, neighbors_here, coef_here, sem):
    for copy in fetch_all([(neighbors, neighbors_here), (coef, coef_here)], sem):
        copy.wait()
    degree, nodes = neighbors.shape
    one_hot_rows(columns(neighbors_here[...]), columns(coef_here[...]), degree, nodes, hot, spread)


def wide(spread):
    return jnp.concatenate([spread, spread], axis=1)


def cross_sums(source, gain, hot, spread, outs):
    slots = outs[0].shape[0]
    each = hot.shape[0] // (len(outs) * slots)
    for r, out in enumerate(outs):
        total = None
        for x in range(each):
            rows = pl.ds((r * each + x) * slots, slots)
            hidden = jnp.maximum(dot(hot[rows, :], source) + wide(spread[rows, :]) * gain, 0.0)
            total = hidden if total is None else total + hidden
        out[...] = total.astype(BF16)


def choose(which, refs, rows):
    value = refs[0][rows, :]
    for r in range(1, len(refs)):
        value = jnp.where(which == r, refs[r][rows, :], value)
    return value


def place_of(segment, segments, place):
    return lax.rem(place[0] - segment + segments, segments)


def edge_weights(place, which, j, mine, other, width):
    edge, under = edge_rows(width, j)
    a, b = (choose(which, refs, edge) for refs in (mine, other))
    first = place[1] == 0
    weights = jnp.concatenate([jnp.where(first, a, b), jnp.where(first, b, a)], axis=0)
    return weights, choose(which, mine, under).astype(F32)


def send_side(place, which, j, mine, other, latent, hot, spread, source, outs):
    weights, vectors = edge_weights(place, which, j, mine, other, latent.shape[1])
    table = (dot(latent, weights) + vectors[0:1, :]).astype(BF16)
    source[...] = table
    cross_sums(table, vectors[1:2, :], hot, spread, outs)


def partner_sums_kernel(segments, place, *refs):
    mine, other = refs[:segments], refs[segments : 2 * segments]
    raw, outs = refs[2 * segments : 2 * segments + 2], refs[2 * segments + 2 :]
    slots, width = outs[0].shape
    each = (raw[0].shape[0] - VECTORS) // slots
    weights, vectors = edge_weights(place, place_of(0, segments, place), 0, mine, other, width)
    for r, out in enumerate(outs):
        block = jnp.where(place[1] == r, raw[0][...], raw[1][...])
        table = (dot(block[0 : each * slots, :], weights) + vectors[0:1, :]).astype(BF16).astype(F32)
        rows = block[each * slots :, 0:slots].astype(F32)
        coefs = [sum(rows[i : i + 1] for i in range(3 * x + 1, 3 * x + 3)) + rows[3 * x : 3 * x + 1] for x in range(each)]
        coefs = columns(jnp.concatenate(coefs, axis=0))
        total = None
        for x in range(each):
            hidden = table[x * slots : (x + 1) * slots] + coefs[:, x : x + 1] * vectors[1:2, :]
            hidden = jnp.maximum(hidden, 0.0)
            total = hidden if total is None else total + hidden
        out[...] = total.astype(BF16)


def inner_kernel(segments, segment, j, first, place, *refs):
    mine, other = refs[:segments], refs[segments : 2 * segments]
    source, hot, spread, sums = refs[2 * segments :]
    nodes, width = sums.shape
    which = place_of(segment, segments, place)
    table = source[...]
    if first:
        weights, vectors = edge_weights(place, which, j, mine, other, width)
        table = (dot(table, weights) + vectors[0:1, :]).astype(BF16)
    gain = choose(which, mine, edge_rows(width, j)[1]).astype(F32)[1:2, :]
    total = None
    for k in range(hot.shape[0] // nodes):
        rows = pl.ds(k * nodes, nodes)
        hidden = jnp.maximum(dot(hot[rows, :], table) + wide(spread[rows, :]) * gain, 0.0)
        total = hidden if total is None else total + hidden
    sums[...] = total


def weights_kernel(segments, held, segment, j, place, *refs):
    mine, other, vec_mine, vec_other = (refs[i * segments : (i + 1) * segments] for i in range(4))
    latent, before, chosen = refs[4 * segments :]
    width = before.shape[1]
    half = width // 2
    inner, outer = node_rows(width, held, j)
    which = place_of(segment, segments, place)
    in_a, in_b = (choose(which, refs, inner) for refs in (mine, other))
    vec_a, vec_b = (choose(which, refs, edge_rows(width, j)[1]) for refs in (vec_mine, vec_other))
    joined = jnp.concatenate([in_a[:, :half], in_b[:, :half]], axis=1)
    bias = jnp.concatenate([vec_a[:, :half], vec_b[:, :half]], axis=1).astype(F32)[4:5, :]
    before[...] = dot(latent[...], joined) + bias
    chosen[0:width, :] = jnp.concatenate([in_a[:, half:], in_b[:, half:]], axis=1)
    chosen[width : width + half, :] = choose(which, mine, outer)
    chosen[width + half : 2 * width, :] = choose(which, other, outer)
    chosen[2 * width : 2 * width + VECTORS, :] = vec_a


def node_kernel(segments, segment, j, last, rounds, place, *refs):
    arrived, refs = refs[:rounds], refs[rounds:]
    latent, sums, before, chosen, scatter = refs[:5]
    width = sums.shape[1]
    half = width // 2
    summed = sums[...] + dot(scatter[...], jnp.concatenate([block[...] for block in arrived[::-1]], axis=0))
    hidden = before[...] + dot(summed.astype(BF16), chosen[0:width, :])
    hidden = jnp.maximum(hidden, 0.0).astype(BF16)
    mixed = dot(hidden[:, :half], chosen[width : width + half, :]).astype(BF16).astype(F32)
    mixed = mixed + dot(hidden[:, half:], chosen[width + half : 2 * width, :]).astype(BF16).astype(F32)
    vectors = chosen[2 * width : 2 * width + VECTORS, :].astype(F32)
    centred = mixed - jnp.mean(mixed, axis=1, keepdims=True)
    spread_of = jnp.mean(centred * centred, axis=1, keepdims=True)
    normed = centred * lax.rsqrt(spread_of + 1e-05) * vectors[2:3, :] + vectors[3:4, :]
    fresh = (latent[...].astype(F32) + normed).astype(BF16)
    if last:
        refs[5][0] = fresh
        return
    mine, other = refs[5 : 5 + segments], refs[5 + segments : 5 + 2 * segments]
    hot, spread, result, source, *outs = refs[5 + 2 * segments :]
    result[...] = fresh
    which = place_of(segment, segments, place)
    send_side(place, which, j, mine, other, fresh, hot, spread, source, outs)


def partner_route(count, r):
    return [(i, i ^ 1 << r) for i in range(count) if i ^ 1 << r < count]


def per_device(
    latents,
    neighbors,
    edge_coef,
    cross_src,
    cross_coef,
    recv_node,
    w_edge,
    w_node_in,
    w_node_out,
    edge_bias,
    edge_gain,
    node_bias,
    norm_gain,
    norm_bias,
):
    segments, cores, parts = (lax.axis_size(a) for a in ("segment", "chan", "dom"))
    micro, nodes, width = latents.shape
    held = w_edge.shape[0]
    rounds, slots = recv_node.shape
    degree, edges = neighbors.shape[0], cross_src.shape[0] * cross_src.shape[1]
    half = width // 2
    assert micro == segments and cores == rounds == 2
    place = jnp.stack([lax.axis_index("segment"), lax.axis_index("chan")]).astype(jnp.int32)

    def in_hbm(*arrays):
        return [pltpu.with_memory_space_constraint(array, pltpu.HBM) for array in arrays]

    def buffers(*arrays):
        return [pltpu.VMEM(array.shape, array.dtype) for array in arrays]

    def swap(block):
        return lax.ppermute(block, "chan", [(0, 1), (1, 0)])

    def exchange(blocks):
        return [lax.ppermute(block, "dom", partner_route(parts, r)) for r, block in enumerate(blocks)]

    def once(arrays, made):
        return lax.optimization_barrier((arrays, made))[0]

    vectors = (edge_bias, edge_gain, norm_gain, norm_bias, node_bias)
    packs = kernel_call(
        pack_kernel,
        [shape((node_rows(width, held, j)[1].stop, width), BF16) for j in range(held)],
        [place, *in_hbm(w_edge, w_node_in, w_node_out, *vectors)],
        1 << 10,
        scratch=[*buffers(*vectors), pltpu.SemaphoreType.DMA((5 + 4 * held,))],
    )
    graph = (cross_src, cross_coef, recv_node)
    latent, hot_c, spread_c, scatter, raw = kernel_call(
        cross_prep_kernel,
        [
            shape((nodes, width), BF16),
            shape((edges * slots, nodes), BF16),
            shape((edges * slots, LANES), F32),
            shape((nodes, rounds * slots), BF16),
            shape((edges // rounds * slots + VECTORS, width), BF16),
        ],
        [place, *in_hbm(latents, *graph), packs[0]],
        1 << 10,
        after=1,
        scratch=[*buffers(*graph), pltpu.SemaphoreType.DMA((4,))],
    )
    route = []
    for core in range(cores):
        route += [(a * cores + core, b * cores + core) for a, b in partner_route(parts, core)]
    raw = lax.ppermute(raw, ("dom", "chan"), route)
    hot, spread = kernel_call(
        inner_prep_kernel,
        [shape((degree * nodes, nodes), BF16), shape((degree * nodes, LANES), F32)],
        [*in_hbm(neighbors, edge_coef), scatter],
        1 << 30,
        smem=0,
        after=1,
        scratch=[*buffers(neighbors, edge_coef), pltpu.SemaphoreType.DMA((2,))],
    )
    routes = [[(i, (i + r) % segments) for i in range(segments)] for r in range(1, segments)]
    mine_of, other_of = [], []
    for j in range(held):
        ready = once(packs[j], scatter if j else latents)
        mine_of.append([packs[j], *[lax.ppermute(ready, "segment", route) for route in routes]])

    total = segments * held
    sends = [shape((nodes, width), BF16)] + [shape((slots, width), BF16)] * rounds
    def swaps(j, made):
        return [swap(once(packs[j], scatter)), *map(swap, once(mine_of[j][1:], made))]

    source = latent
    for layer in range(total):
        segment, j = divmod(layer, held)
        if layer == 0:
            other_of.append(swaps(0, (raw, hot)))
        weights = [*mine_of[0], *other_of[0]]
        sums = kernel_call(
            functools.partial(inner_kernel, segments, segment, j, layer == 0),
            shape((nodes, width), F32),
            [place, *weights, source, hot, spread],
            1 << 31,
        )
        before, chosen = kernel_call(
            functools.partial(weights_kernel, segments, held, segment, j),
            [shape((nodes, width), F32), shape((2 * width + VECTORS, width), BF16)],
            [place, *mine_of[j], *other_of[j], *weights, latent],
            1 << 28,
        )
        if layer == 0:
            arrived = kernel_call(
                functools.partial(partner_sums_kernel, segments),
                sends[1:],
                [place, *weights, raw, swap(raw)],
                1 << 28,
            )
        else:
            arrived = exchange(blocks)
        operands = [place, *arrived[::-1], latent, sums, before, chosen, scatter]
        last = layer == total - 1
        follow, step = divmod(layer + 1, held)
        if last:
            outs = [shape((1, nodes, width), BF16)]
        else:
            operands += [*weights, hot_c, spread_c]
            outs = [shape((nodes, width), BF16), *sends]
        latent, *rest = kernel_call(
            functools.partial(node_kernel, segments, follow, step, last, rounds), outs, operands, 1 << 30
        )
        if not last:
            source, *blocks = rest
        if layer + 1 < held:
            other_of.append(swaps(layer + 1, source))
    return latent


def solution(mesh):
    return jax.shard_map(
        per_device,
        mesh=mesh,
        in_specs=(
            P(None, ("groups", "dom"), None),
            P(None, ("groups", "dom")),
            P(None, ("groups", "dom")),
            P(None, None, ("groups", "dom")),
            P(None, None, ("groups", "dom")),
            P(None, ("groups", "dom")),
            P("segment", None, None),
            P("segment", None, "chan"),
            P("segment", "chan", None),
            P("segment", None),
            P("segment", None),
            P("segment", "chan"),
            P("segment", None),
            P("segment", None),
        ),
        out_specs=P("segment", ("groups", "dom"), None),
        check_vma=False,
    )
```

time: 65.5 us -> 46 us (0.70)
  starting transfers between devices: 27.8 us -> 18.8 us
  local copies, waits for them, and re-layouts: 8.31 us -> 0 us
  waiting for transfers between devices: 11.3 us -> 3.35 us
  Pallas kernels: 17.4 us -> 23.3 us
    unnamed x30 -> x0, local copies, waits for them, and re-layouts: 8.28 us -> none
    ppermute x10 -> x9, waiting for transfers between devices: 11.3 us -> 3.33 us  [the longest x1 1.87 us: per_device(): raw = lax.ppermute(raw, ('dom', 'chan'), route)]
    ppermute x10 -> x9, starting transfers between devices: 25.2 us -> 18 us  [the longest x6 11.6 us: exchange(): lax.ppermute(block, 'dom', partner_route(parts, r))]
    pallas_call x12 -> x16, Pallas kernels: 17.4 us -> 23.3 us  [kernel_call(): pl.pallas_call(body, out_shape=outs, in_specs=[SMEM] * smem + [HBM if scr...]
    ppermute x6 -> x5, starting transfers between devices: 2.62 us -> 0.8 us  [swap(): return lax.ppermute(block, 'chan', [(0, 1), (1, 0)])]
  transfers between devices with their start and end apart: 16 -> 14, of which waited for: 6 -> 7; matrix products, arithmetic and copies ran while one was open for 0% -> 0% of each run, Pallas kernels for 15% -> 35%
where the time goes in v3:
time: 46 us; the launch traced here: 45.7 us
  Pallas kernels  23.3 us (51%)
  starting transfers between devices  18.8 us (41%)
  waiting for transfers between devices  3.35 us (7%)
    pallas_call x16, Pallas kernels, kernel_call(): pl.pallas_call(body, out_shape=outs, in_specs=[SMEM] * smem + [HBM if scr...  23.3 us
    ppermute x6, starting transfers between devices, exchange(): lax.ppermute(block, 'dom', partner_route(parts, r))  11.6 us
    ppermute x2, starting transfers between devices, per_device(): lax.ppermute(ready, 'segment', route)  4.74 us
    ppermute x1, waiting for transfers between devices, per_device(): raw = lax.ppermute(raw, ('dom', 'chan'), route)  1.87 us
    ppermute x1, starting transfers between devices, per_device(): raw = lax.ppermute(raw, ('dom', 'chan'), route)  1.64 us
    ppermute x6, waiting for transfers between devices, exchange(): lax.ppermute(block, 'dom', partner_route(parts, r))  1.08 us
  transfers between devices with their start and end apart: 14, of which 7 were waited for; matrix products, arithmetic and copies ran while one was open for 0% of the time, Pallas kernels for 35%

profile of v3, /device:TPU:0, one launch (start us, length us, event | category | flops | bytes accessed | tf_op | source)
XLA Modules:
  0.0 45.7 jit_solution(16786204899799685628)
XLA Ops:
  0.1 1.8 %shard_map.136 = (bf16[672,256]{1,0:T(8,128)(2,1)S(1)}, bf16[384,256]{1,0:T(8,128)(2,1)S(1)}) custom-call(s32[2]{0:T(128)S(1)} %pad_add_fusion.place, bf16[2,256,256]{2,1,0:T(8,128)(2,1)} %w_edge.1, bf16[2,512,128]{2,1,0:T(8,128)(2,1)} %w_in.1, bf16[2,128,256]{2,1,0:T(8,128)(2,1)} %w_out.1, bf16[2,256]{1,0:T(2,128)(2,1)} %e_bias.1, bf16[2,256]{1,0:T(2,128)(2,1)} %e_gain.1, ...), custom_call_target="tpu_custom_call" | custom-call | flops 1024 | bytes 65536 | tf_op jit(solution)/shard_map/pallas_call | solution.py:25
  1.9 3.0 %collective-permute-start = (bf16[672,256]{1,0:T(8,128)(2,1)S(1)}, bf16[672,256]{1,0:T(8,128)(2,1)S(1)}, u32[]{:S(2)}, u32[]{:S(2)}) collective-permute-start(bf16[672,256]{1,0:T(8,128)(2,1)S(1)} %get-tuple-element.44._.refs_0_.refs_4_.refs_7_), channel_id=1, source_target_pairs={{0,2},{2,0},{1,3},{3,1},{4,6},{6,4},{5,7},{7,5},{8,10},{10,8},{9,1... | collective-permute-start | bytes 1032200 | tf_op jit(solution)/shard_map/ppermute | solution.py:359
  4.9 2.0 %shard_map.137 = (bf16[512,256]{1,0:T(8,128)(2,1)S(1)}, bf16[512,512]{1,0:T(8,128)(2,1)S(1)}, f32[512,128]{1,0:T(8,128)S(1)}, bf16[512,256]{1,0:T(8,128)(2,1)S(1)}, bf16[272,256]{1,0:T(8,128)(2,1)S(1)}) custom-call(s32[2]{0:T(128)S(1)} %pad_add_fusion.place, bf16[2,512,256]{2,1,0:T(8,128)(2,1)} %latents.1, s32[2,2,128]{2,1,0:T(2,128)} %src.1, ...), custom_call_target="tpu_custom_call" | custom-call | flops 1024 | bytes 65536 | tf_op jit(solution)/shard_map/pallas_call | solution.py:25
  6.8 1.6 %collective-permute-start.2 = (bf16[272,256]{1,0:T(8,128)(2,1)S(1)}, bf16[272,256]{1,0:T(8,128)(2,1)S(1)}, u32[]{:S(2)}, u32[]{:S(2)}) collective-permute-start(bf16[272,256]{1,0:T(8,128)(2,1)S(1)} %get-tuple-element.45), channel_id=1, source_target_pairs={{0,4},{4,0},{8,12},{12,8},{1,9},{5,13},{9,1},{13,5},{2,6},{6,2},{1... | collective-permute-start | bytes 417800 | tf_op jit(solution)/shard_map/ppermute | solution.py:345
  8.5 0.3 collective-permute-start.1
  8.8 1.9 %shard_map.138 = (bf16[3072,512]{1,0:T(8,128)(2,1)S(1)}, f32[3072,128]{1,0:T(8,128)S(1)}) custom-call(s32[6,512]{1,0:T(8,128)} %neighbors.1, f32[6,512]{1,0:T(8,128)} %coef.3, bf16[512,256]{1,0:T(8,128)(2,1)S(1)} %get-tuple-element.43._.refs_6_), custom_call_target="tpu_custom_call" | custom-call | flops 1073741824 | bytes 65536 | tf_op jit(solution)/shard_map/pallas_call | solution.py:25
  10.7 1.9 %collective-permute-done.2.refs_4_ = bf16[272,256]{1,0:T(8,128)(2,1)S(1)} collective-permute-done((bf16[272,256]{1,0:T(8,128)(2,1)S(1)}, bf16[272,256]{1,0:T(8,128)(2,1)S(1)}, u32[]{:S(2)}, u32[]{:S(2)}) %collective-permute-start.2) | collective-permute-done | bytes 139296 | tf_op jit(solution)/shard_map/ppermute | solution.py:345
  12.6 0.4 collective-permute-done.refs_1_.refs_5_.refs_8_
  12.9 0.5 %collective-permute-start.8 = (bf16[384,256]{1,0:T(8,128)(2,1)S(1)}, bf16[384,256]{1,0:T(8,128)(2,1)S(1)}, u32[]{:S(2)}, u32[]{:S(2)}) collective-permute-start(bf16[384,256]{1,0:T(8,128)(2,1)S(1)} %get-tuple-element.61.refs_0_), channel_id=1, source_target_pairs={{0,1},{1,0},{2,3},{3,2},{4,5},{5,4},{6,7},{7,6},{8,9},{9,8},{10,11... | collective-permute-start | bytes 589832 | tf_op jit(solution)/shard_map/ppermute | solution.py:311
  13.5 1.7 %collective-permute-start.7 = (bf16[384,256]{1,0:T(8,128)(2,1)S(1)}, bf16[384,256]{1,0:T(8,128)(2,1)S(1)}, u32[]{:S(2)}, u32[]{:S(2)}) collective-permute-start(bf16[384,256]{1,0:T(8,128)(2,1)S(1)} %get-tuple-element.61.refs_0_), channel_id=1, source_target_pairs={{0,2},{2,0},{1,3},{3,1},{4,6},{6,4},{5,7},{7,5},{8,10},{10,8},{9,1... | collective-permute-start | bytes 589832 | tf_op jit(solution)/shard_map/ppermute | solution.py:359
  15.2 1.8 %shard_map.140.refs_3_ = f32[512,256]{1,0:T(8,128)S(1)} custom-call(s32[2]{0:T(128)S(1)} %pad_add_fusion.place, bf16[672,256]{1,0:T(8,128)(2,1)S(1)} %get-tuple-element.44._.refs_0_.refs_4_.refs_7_, bf16[672,256]{1,0:T(8,128)(2,1)S(1)} %collective-permute-done.refs_1_.refs_5_.refs_8_, bf16[672,256]{1,0:T(8,128)(2,1)S(1)} %collective-permute-done.1.refs_2_.refs_6_.refs_9_, ...), custom_call_target="tpu_custom_call" | custom-call | flops 2147483648 | bytes 65536 | tf_op jit(solution)/shard_map/pallas_call | solution.py:25
  17.0 0.8 %shard_map.141 = (f32[512,256]{1,0:T(8,128)S(1)}, bf16[528,256]{1,0:T(8,128)(2,1)S(1)}) custom-call(s32[2]{0:T(128)S(1)} %pad_add_fusion.place, bf16[672,256]{1,0:T(8,128)(2,1)S(1)} %get-tuple-element.44._.refs_0_.refs_4_.refs_7_, bf16[672,256]{1,0:T(8,128)(2,1)S(1)} %collective-permute-done.refs_1_.refs_5_.refs_8_, ...), custom_call_target="tpu_custom_call" | custom-call | flops 268435456 | bytes 65536 | tf_op jit(solution)/shard_map/pallas_call | solution.py:25
  17.8 0.9 %shard_map.139 = (bf16[128,256]{1,0:T(8,128)(2,1)S(1)}, bf16[128,256]{1,0:T(8,128)(2,1)S(1)}) custom-call(s32[2]{0:T(128)S(1)} %pad_add_fusion.place, bf16[672,256]{1,0:T(8,128)(2,1)S(1)} %get-tuple-element.44._.refs_0_.refs_4_.refs_7_, bf16[672,256]{1,0:T(8,128)(2,1)S(1)} %collective-permute-done.refs_1_.refs_5_.refs_8_, ...), custom_call_target="tpu_custom_call" | custom-call | flops 268435456 | bytes 65536 | tf_op jit(solution)/shard_map/pallas_call | solution.py:25
  18.6 1.8 %shard_map.142 = (bf16[512,256]{1,0:T(8,128)(2,1)S(1)}, bf16[512,256]{1,0:T(8,128)(2,1)S(1)}, bf16[128,256]{1,0:T(8,128)(2,1)S(1)}, bf16[128,256]{1,0:T(8,128)(2,1)S(1)}) custom-call(s32[2]{0:T(128)S(1)} %pad_add_fusion.place, bf16[128,256]{1,0:T(8,128)(2,1)S(1)} %get-tuple-element.48.refs_0_, bf16[128,256]{1,0:T(8,128)(2,1)S(1)} %get-tuple-element.49.refs_1_, ...), custom_call_target="tpu_custom_call" | custom-call | flops 1073741824 | bytes 65536 | tf_op jit(solution)/shard_map/pallas_call | solution.py:25
  20.4 2.7 %collective-permute-start.5 = (bf16[128,256]{1,0:T(8,128)(2,1)S(1)}, bf16[128,256]{1,0:T(8,128)(2,1)S(1)}, u32[]{:S(2)}, u32[]{:S(2)}) collective-permute-start(bf16[128,256]{1,0:T(8,128)(2,1)S(1)} %get-tuple-element.56), channel_id=1, source_target_pairs={{0,8},{4,12},{8,0},{12,4},{1,9},{5,13},{9,1},{13,5},{2,10},{6,14},... | collective-permute-start | bytes 196616 | tf_op jit(solution)/shard_map/ppermute | solution.py:314
  23.1 1.7 %collective-permute-start.6 = (bf16[128,256]{1,0:T(8,128)(2,1)S(1)}, bf16[128,256]{1,0:T(8,128)(2,1)S(1)}, u32[]{:S(2)}, u32[]{:S(2)}) collective-permute-start(bf16[128,256]{1,0:T(8,128)(2,1)S(1)} %get-tuple-element.57), channel_id=1, source_target_pairs={{0,4},{4,0},{8,12},{12,8},{1,5},{5,1},{9,13},{13,9},{2,6},{6,2},{1... | collective-permute-start | bytes 196616 | tf_op jit(solution)/shard_map/ppermute | solution.py:314
  24.8 1.5 %shard_map.143.refs_3_ = f32[512,256]{1,0:T(8,128)S(1)} custom-call(s32[2]{0:T(128)S(1)} %pad_add_fusion.place, bf16[672,256]{1,0:T(8,128)(2,1)S(1)} %get-tuple-element.44._.refs_0_.refs_4_.refs_7_, bf16[672,256]{1,0:T(8,128)(2,1)S(1)} %collective-permute-done.refs_1_.refs_5_.refs_8_, bf16[672,256]{1,0:T(8,128)(2,1)S(1)} %collective-permute-done.1.refs_2_.refs_6_.refs_9_, ...), custom_call_target="tpu_custom_call" | custom-call | flops 2147483648 | bytes 65536 | tf_op jit(solution)/shard_map/pallas_call | solution.py:25
  26.4 0.8 %shard_map.144 = (f32[512,256]{1,0:T(8,128)S(1)}, bf16[528,256]{1,0:T(8,128)(2,1)S(1)}) custom-call(s32[2]{0:T(128)S(1)} %pad_add_fusion.place, bf16[384,256]{1,0:T(8,128)(2,1)S(1)} %get-tuple-element.61.refs_0_, bf16[384,256]{1,0:T(8,128)(2,1)S(1)} %collective-permute-done.7.refs_1_, bf16[384,256]{1,0:T(8,128)(2,1)S(1)} %collective-permute-done.8.refs_2_, ...), custom_call_target="tpu_custom_call" | custom-call | flops 268435456 | bytes 65536 | tf_op jit(solution)/shard_map/pallas_call | solution.py:25
  27.2 0.4 collective-permute-done.6.refs_1_
  27.7 1.8 %shard_map.145 = (bf16[512,256]{1,0:T(8,128)(2,1)S(1)}, bf16[512,256]{1,0:T(8,128)(2,1)S(1)}, bf16[128,256]{1,0:T(8,128)(2,1)S(1)}, bf16[128,256]{1,0:T(8,128)(2,1)S(1)}) custom-call(s32[2]{0:T(128)S(1)} %pad_add_fusion.place, bf16[128,256]{1,0:T(8,128)(2,1)S(1)} %collective-permute-done.5.refs_0_, bf16[128,256]{1,0:T(8,128)(2,1)S(1)} %collective-permute-done.6.refs_1_, ...), custom_call_target="tpu_custom_call" | custom-call | flops 1073741824 | bytes 65536 | tf_op jit(solution)/shard_map/pallas_call | solution.py:25
  29.4 1.3 %collective-permute-start.10 = (bf16[128,256]{1,0:T(8,128)(2,1)S(1)}, bf16[128,256]{1,0:T(8,128)(2,1)S(1)}, u32[]{:S(2)}, u32[]{:S(2)}) collective-permute-start(bf16[128,256]{1,0:T(8,128)(2,1)S(1)} %get-tuple-element.65), channel_id=1, source_target_pairs={{0,8},{4,12},{8,0},{12,4},{1,9},{5,13},{9,1},{13,5},{2,10},{6,14},... | collective-permute-start | bytes 196616 | tf_op jit(solution)/shard_map/ppermute | solution.py:314
  30.8 2.4 %collective-permute-start.11 = (bf16[128,256]{1,0:T(8,128)(2,1)S(1)}, bf16[128,256]{1,0:T(8,128)(2,1)S(1)}, u32[]{:S(2)}, u32[]{:S(2)}) collective-permute-start(bf16[128,256]{1,0:T(8,128)(2,1)S(1)} %get-tuple-element.66), channel_id=1, source_target_pairs={{0,4},{4,0},{8,12},{12,8},{1,5},{5,1},{9,13},{13,9},{2,6},{6,2},{1... | collective-permute-start | bytes 196616 | tf_op jit(solution)/shard_map/ppermute | solution.py:314
  33.2 1.5 %shard_map.146.refs_3_ = f32[512,256]{1,0:T(8,128)S(1)} custom-call(s32[2]{0:T(128)S(1)} %pad_add_fusion.place, bf16[672,256]{1,0:T(8,128)(2,1)S(1)} %get-tuple-element.44._.refs_0_.refs_4_.refs_7_, bf16[672,256]{1,0:T(8,128)(2,1)S(1)} %collective-permute-done.refs_1_.refs_5_.refs_8_, bf16[672,256]{1,0:T(8,128)(2,1)S(1)} %collective-permute-done.1.refs_2_.refs_6_.refs_9_, ...), custom_call_target="tpu_custom_call" | custom-call | flops 2147483648 | bytes 65536 | tf_op jit(solution)/shard_map/pallas_call | solution.py:25
  34.7 0.8 %shard_map.147 = (f32[512,256]{1,0:T(8,128)S(1)}, bf16[528,256]{1,0:T(8,128)(2,1)S(1)}) custom-call(s32[2]{0:T(128)S(1)} %pad_add_fusion.place, bf16[672,256]{1,0:T(8,128)(2,1)S(1)} %get-tuple-element.44._.refs_0_.refs_4_.refs_7_, bf16[672,256]{1,0:T(8,128)(2,1)S(1)} %collective-permute-done.refs_1_.refs_5_.refs_8_, ...), custom_call_target="tpu_custom_call" | custom-call | flops 268435456 | bytes 65536 | tf_op jit(solution)/shard_map/pallas_call | solution.py:25
  35.5 0.4 collective-permute-done.10.refs_0_
  36.0 1.8 %shard_map.148 = (bf16[512,256]{1,0:T(8,128)(2,1)S(1)}, bf16[512,256]{1,0:T(8,128)(2,1)S(1)}, bf16[128,256]{1,0:T(8,128)(2,1)S(1)}, bf16[128,256]{1,0:T(8,128)(2,1)S(1)}) custom-call(s32[2]{0:T(128)S(1)} %pad_add_fusion.place, bf16[128,256]{1,0:T(8,128)(2,1)S(1)} %collective-permute-done.10.refs_0_, bf16[128,256]{1,0:T(8,128)(2,1)S(1)} %collective-permute-done.11.refs_1_, ...), custom_call_target="tpu_custom_call" | custom-call | flops 1073741824 | bytes 65536 | tf_op jit(solution)/shard_map/pallas_call | solution.py:25
  37.8 1.1 %collective-permute-start.12 = (bf16[128,256]{1,0:T(8,128)(2,1)S(1)}, bf16[128,256]{1,0:T(8,128)(2,1)S(1)}, u32[]{:S(2)}, u32[]{:S(2)}) collective-permute-start(bf16[128,256]{1,0:T(8,128)(2,1)S(1)} %get-tuple-element.71), channel_id=1, source_target_pairs={{0,8},{4,12},{8,0},{12,4},{1,9},{5,13},{9,1},{13,5},{2,10},{6,14},... | collective-permute-start | bytes 196616 | tf_op jit(solution)/shard_map/ppermute | solution.py:314
  38.9 2.4 %collective-permute-start.13 = (bf16[128,256]{1,0:T(8,128)(2,1)S(1)}, bf16[128,256]{1,0:T(8,128)(2,1)S(1)}, u32[]{:S(2)}, u32[]{:S(2)}) collective-permute-start(bf16[128,256]{1,0:T(8,128)(2,1)S(1)} %get-tuple-element.72), channel_id=1, source_target_pairs={{0,4},{4,0},{8,12},{12,8},{1,5},{5,1},{9,13},{13,9},{2,6},{6,2},{1... | collective-permute-start | bytes 196616 | tf_op jit(solution)/shard_map/ppermute | solution.py:314
  41.3 1.5 %shard_map.149.refs_3_ = f32[512,256]{1,0:T(8,128)S(1)} custom-call(s32[2]{0:T(128)S(1)} %pad_add_fusion.place, bf16[672,256]{1,0:T(8,128)(2,1)S(1)} %get-tuple-element.44._.refs_0_.refs_4_.refs_7_, bf16[672,256]{1,0:T(8,128)(2,1)S(1)} %collective-permute-done.refs_1_.refs_5_.refs_8_, bf16[672,256]{1,0:T(8,128)(2,1)S(1)} %collective-permute-done.1.refs_2_.refs_6_.refs_9_, ...), custom_call_target="tpu_custom_call" | custom-call | flops 2147483648 | bytes 65536 | tf_op jit(solution)/shard_map/pallas_call | solution.py:25
  42.8 0.8 %shard_map.150 = (f32[512,256]{1,0:T(8,128)S(1)}, bf16[528,256]{1,0:T(8,128)(2,1)S(1)}) custom-call(s32[2]{0:T(128)S(1)} %pad_add_fusion.place, bf16[384,256]{1,0:T(8,128)(2,1)S(1)} %get-tuple-element.61.refs_0_, bf16[384,256]{1,0:T(8,128)(2,1)S(1)} %collective-permute-done.7.refs_1_, bf16[384,256]{1,0:T(8,128)(2,1)S(1)} %collective-permute-done.8.refs_2_, ...), custom_call_target="tpu_custom_call" | custom-call | flops 268435456 | bytes 65536 | tf_op jit(solution)/shard_map/pallas_call | solution.py:25
  43.6 0.1 collective-permute-done.13.refs_1_
  43.7 2.0 %shard_map.151 = bf16[1,512,256]{2,1,0:T(8,128)(2,1)} custom-call(s32[2]{0:T(128)S(1)} %pad_add_fusion.place, bf16[128,256]{1,0:T(8,128)(2,1)S(1)} %collective-permute-done.12.refs_0_, bf16[128,256]{1,0:T(8,128)(2,1)S(1)} %collective-permute-done.13.refs_1_, bf16[512,256]{1,0:T(8,128)(2,1)S(1)} %get-tuple-element.73.refs_8_.refs_2_, ...), custom_call_target="tpu_custom_call" | custom-call | flops 1073741824 | bytes 65536 | tf_op jit(solution)/shard_map/pallas_call | solution.py:25
  (13 shorter events, 0.3 us)
Async XLA Ops:
  1.9 11.1 %collective-permute-start = (bf16[672,256]{1,0:T(8,128)(2,1)S(1)}, bf16[672,256]{1,0:T(8,128)(2,1)S(1)}, u32[]{:S(2)}, u32[]{:S(2)}) collective-permute-start(bf16[672,256]{1,0:T(8,128)(2,1)S(1)} %get-tuple-element.44._.refs_0_.refs_4_.refs_7_), channel_id=1, source_target_pairs={{0,2},{2,0},{1,3},{3,1},{4,6},{6,4},{5,7},{7,5},{8,10},{10,8},{9,1... | collective-permute-start | bytes 1032200 | tf_op jit(solution)/shard_map/ppermute | solution.py:359
  6.8 5.7 %collective-permute-start.2 = (bf16[272,256]{1,0:T(8,128)(2,1)S(1)}, bf16[272,256]{1,0:T(8,128)(2,1)S(1)}, u32[]{:S(2)}, u32[]{:S(2)}) collective-permute-start(bf16[272,256]{1,0:T(8,128)(2,1)S(1)} %get-tuple-element.45), channel_id=1, source_target_pairs={{0,4},{4,0},{8,12},{12,8},{1,9},{5,13},{9,1},{13,5},{2,6},{6,2},{1... | collective-permute-start | bytes 417800 | tf_op jit(solution)/shard_map/ppermute | solution.py:345
  8.5 6.7 %collective-permute-start.1 = (bf16[672,256]{1,0:T(8,128)(2,1)S(1)}, bf16[672,256]{1,0:T(8,128)(2,1)S(1)}, u32[]{:S(2)}, u32[]{:S(2)}) collective-permute-start(bf16[672,256]{1,0:T(8,128)(2,1)S(1)} %get-tuple-element.44._.refs_0_.refs_4_.refs_7_), channel_id=1, source_target_pairs={{0,1},{1,0},{2,3},{3,2},{4,5},{5,4},{6,7},{7,6},{8,9},{9,8},{10,11... | collective-permute-start | bytes 1032200 | tf_op jit(solution)/shard_map/ppermute | solution.py:311
  12.9 2.3 %collective-permute-start.3 = (bf16[672,256]{1,0:T(8,128)(2,1)S(1)}, bf16[672,256]{1,0:T(8,128)(2,1)S(1)}, u32[]{:S(2)}, u32[]{:S(2)}) collective-permute-start(bf16[672,256]{1,0:T(8,128)(2,1)S(1)} %collective-permute-done.refs_1_.refs_5_.refs_8_), channel_id=1, source_target_pairs={{0,1},{1,0},{2,3},{3,2},{4,5},{5,4},{6,7},{7,6},{8,9},{9,8},{10,11... | collective-permute-start | bytes 1032200 | tf_op jit(solution)/shard_map/ppermute | solution.py:311
  12.9 13.4 %collective-permute-start.8 = (bf16[384,256]{1,0:T(8,128)(2,1)S(1)}, bf16[384,256]{1,0:T(8,128)(2,1)S(1)}, u32[]{:S(2)}, u32[]{:S(2)}) collective-permute-start(bf16[384,256]{1,0:T(8,128)(2,1)S(1)} %get-tuple-element.61.refs_0_), channel_id=1, source_target_pairs={{0,1},{1,0},{2,3},{3,2},{4,5},{5,4},{6,7},{7,6},{8,9},{9,8},{10,11... | collective-permute-start | bytes 589832 | tf_op jit(solution)/shard_map/ppermute | solution.py:311
  13.5 7.0 %collective-permute-start.7 = (bf16[384,256]{1,0:T(8,128)(2,1)S(1)}, bf16[384,256]{1,0:T(8,128)(2,1)S(1)}, u32[]{:S(2)}, u32[]{:S(2)}) collective-permute-start(bf16[384,256]{1,0:T(8,128)(2,1)S(1)} %get-tuple-element.61.refs_0_), channel_id=1, source_target_pairs={{0,2},{2,0},{1,3},{3,1},{4,6},{6,4},{5,7},{7,5},{8,10},{10,8},{9,1... | collective-permute-start | bytes 589832 | tf_op jit(solution)/shard_map/ppermute | solution.py:359
  15.2 2.6 %collective-permute-start.4 = (bf16[272,256]{1,0:T(8,128)(2,1)S(1)}, bf16[272,256]{1,0:T(8,128)(2,1)S(1)}, u32[]{:S(2)}, u32[]{:S(2)}) collective-permute-start(bf16[272,256]{1,0:T(8,128)(2,1)S(1)} %collective-permute-done.2.refs_4_), channel_id=1, source_target_pairs={{0,1},{1,0},{2,3},{3,2},{4,5},{5,4},{6,7},{7,6},{8,9},{9,8},{10,11... | collective-permute-start | bytes 417800 | tf_op jit(solution)/shard_map/ppermute | solution.py:311
  20.4 6.8 %collective-permute-start.5 = (bf16[128,256]{1,0:T(8,128)(2,1)S(1)}, bf16[128,256]{1,0:T(8,128)(2,1)S(1)}, u32[]{:S(2)}, u32[]{:S(2)}) collective-permute-start(bf16[128,256]{1,0:T(8,128)(2,1)S(1)} %get-tuple-element.56), channel_id=1, source_target_pairs={{0,8},{4,12},{8,0},{12,4},{1,9},{5,13},{9,1},{13,5},{2,10},{6,14},... | collective-permute-start | bytes 196616 | tf_op jit(solution)/shard_map/ppermute | solution.py:314
  23.1 4.6 %collective-permute-start.6 = (bf16[128,256]{1,0:T(8,128)(2,1)S(1)}, bf16[128,256]{1,0:T(8,128)(2,1)S(1)}, u32[]{:S(2)}, u32[]{:S(2)}) collective-permute-start(bf16[128,256]{1,0:T(8,128)(2,1)S(1)} %get-tuple-element.57), channel_id=1, source_target_pairs={{0,4},{4,0},{8,12},{12,8},{1,5},{5,1},{9,13},{13,9},{2,6},{6,2},{1... | collective-permute-start | bytes 196616 | tf_op jit(solution)/shard_map/ppermute | solution.py:314
  24.8 1.6 %collective-permute-start.9 = (bf16[384,256]{1,0:T(8,128)(2,1)S(1)}, bf16[384,256]{1,0:T(8,128)(2,1)S(1)}, u32[]{:S(2)}, u32[]{:S(2)}) collective-permute-start(bf16[384,256]{1,0:T(8,128)(2,1)S(1)} %collective-permute-done.7.refs_1_), channel_id=1, source_target_pairs={{0,1},{1,0},{2,3},{3,2},{4,5},{5,4},{6,7},{7,6},{8,9},{9,8},{10,11... | collective-permute-start | bytes 589832 | tf_op jit(solution)/shard_map/ppermute | solution.py:311
  29.4 6.5 %collective-permute-start.10 = (bf16[128,256]{1,0:T(8,128)(2,1)S(1)}, bf16[128,256]{1,0:T(8,128)(2,1)S(1)}, u32[]{:S(2)}, u32[]{:S(2)}) collective-permute-start(bf16[128,256]{1,0:T(8,128)(2,1)S(1)} %get-tuple-element.65), channel_id=1, source_target_pairs={{0,8},{4,12},{8,0},{12,4},{1,9},{5,13},{9,1},{13,5},{2,10},{6,14},... | collective-permute-start | bytes 196616 | tf_op jit(solution)/shard_map/ppermute | solution.py:314
  30.8 5.3 %collective-permute-start.11 = (bf16[128,256]{1,0:T(8,128)(2,1)S(1)}, bf16[128,256]{1,0:T(8,128)(2,1)S(1)}, u32[]{:S(2)}, u32[]{:S(2)}) collective-permute-start(bf16[128,256]{1,0:T(8,128)(2,1)S(1)} %get-tuple-element.66), channel_id=1, source_target_pairs={{0,4},{4,0},{8,12},{12,8},{1,5},{5,1},{9,13},{13,9},{2,6},{6,2},{1... | collective-permute-start | bytes 196616 | tf_op jit(solution)/shard_map/ppermute | solution.py:314
  37.8 5.8 %collective-permute-start.12 = (bf16[128,256]{1,0:T(8,128)(2,1)S(1)}, bf16[128,256]{1,0:T(8,128)(2,1)S(1)}, u32[]{:S(2)}, u32[]{:S(2)}) collective-permute-start(bf16[128,256]{1,0:T(8,128)(2,1)S(1)} %get-tuple-element.71), channel_id=1, source_target_pairs={{0,8},{4,12},{8,0},{12,4},{1,9},{5,13},{9,1},{13,5},{2,10},{6,14},... | collective-permute-start | bytes 196616 | tf_op jit(solution)/shard_map/ppermute | solution.py:314
  38.9 4.9 %collective-permute-start.13 = (bf16[128,256]{1,0:T(8,128)(2,1)S(1)}, bf16[128,256]{1,0:T(8,128)(2,1)S(1)}, u32[]{:S(2)}, u32[]{:S(2)}) collective-permute-start(bf16[128,256]{1,0:T(8,128)(2,1)S(1)} %get-tuple-element.72), channel_id=1, source_target_pairs={{0,4},{4,0},{8,12},{12,8},{1,5},{5,1},{9,13},{13,9},{2,6},{6,2},{1... | collective-permute-start | bytes 196616 | tf_op jit(solution)/shard_map/ppermute | solution.py:314

commit v4 on v3

--- a/solution.py
+++ b/solution.py
@@ -10,7 +10,6 @@
 F32 = jnp.float32
 BF16 = jnp.bfloat16
 VMEM = pl.BlockSpec(memory_space=pltpu.VMEM)
-SMEM = pl.BlockSpec(memory_space=pltpu.SMEM)
 HBM = pl.BlockSpec(memory_space=pltpu.HBM)
 ANY = pl.BlockSpec(memory_space=pl.ANY)
 LANES = 128
@@ -20,12 +19,12 @@
     return jnp.dot(a, b, preferred_element_type=F32)
 
 
-def kernel_call(body, outs, operands, flops, smem=1, scratch=(), after=0):
-    plain = len(operands) - smem - after
+def kernel_call(body, outs, operands, flops, scratch=(), after=0):
+    plain = len(operands) - after
     return pl.pallas_call(
         body,
         out_shape=outs,
-        in_specs=[SMEM] * smem + [HBM if scratch else VMEM] * plain + [ANY] * after,
+        in_specs=[HBM if scratch else VMEM] * plain + [ANY] * after,
         out_specs=jax.tree.map(lambda _: VMEM, outs),
         scratch_shapes=scratch,
         cost_estimate=pl.CostEstimate(flops=flops, bytes_accessed=1 << 16, transcendentals=0),
@@ -70,10 +69,10 @@
     return slice(start, start + width), slice(start + width, start + width + half)
 
 
-def pack_kernel(place, w_edge, w_in, w_out, e_bias, e_gain, g_norm, b_norm, n_bias, *refs):
+def pack_kernel(w_edge, w_in, w_out, e_bias, e_gain, g_norm, b_norm, n_bias, *refs):
     held, half, width = w_out.shape
     packs, vectors, sem = refs[:held], refs[held:-1], refs[-1]
-    mine = pl.multiple_of(place[1] * half, half)
+    mine = pl.multiple_of(lax.axis_index("chan") * half, half)
     pairs = list(zip((e_bias, e_gain, g_norm, b_norm, n_bias), vectors))
     for j in range(held):
         inner, outer = node_rows(width, held, j)
@@ -119,10 +118,10 @@
     return high, middle, (rest - middle.astype(F32)).astype(BF16)
 
 
-def cross_prep_kernel(place, latents, src, coef, recv, _, latent, hot, spread, scatter, *refs):
+def cross_prep_kernel(latents, src, coef, recv, _, latent, hot, spread, scatter, *refs):
     rounds, slots = recv.shape
     raw, here, sem = refs[0], refs[1:4], refs[4]
-    copies = fetch_all([*zip((src, coef, recv), here), (latents.at[place[0]], latent)], sem)
+    copies = fetch_all([*zip((src, coef, recv), here), (latents.at[lax.axis_index("segment")], latent)], sem)
     for copy in copies[:3]:
         copy.wait()
     nodes, width = latent.shape
@@ -135,9 +134,9 @@
         ).astype(BF16)
     copies[3].wait()
     each = src.shape[1] * slots
-    mine = pl.multiple_of(place[1] * each, each)
+    mine = pl.multiple_of(lax.axis_index("chan") * each, each)
     raw[0:each, :] = dot(hot[pl.ds(mine, each), :], latent[...]).astype(BF16)
-    coefs = here[1][place[1]]
+    coefs = here[1][lax.axis_index("chan")]
     rows = [piece[x : x + 1, :] for x in range(src.shape[1]) for piece in pieces(coefs)]
     raw[each : each + VECTORS, :] = vector_rows(rows, width)
 
@@ -156,12 +155,11 @@
 def cross_sums(source, gain, hot, spread, outs):
     slots = outs[0].shape[0]
     each = hot.shape[0] // (len(outs) * slots)
+    hidden = jnp.maximum(dot(hot[...], source) + wide(spread[...]) * gain, 0.0)
     for r, out in enumerate(outs):
-        total = None
-        for x in range(each):
-            rows = pl.ds((r * each + x) * slots, slots)
-            hidden = jnp.maximum(dot(hot[rows, :], source) + wide(spread[rows, :]) * gain, 0.0)
-            total = hidden if total is None else total + hidden
+        total = hidden[r * each * slots : (r * each + 1) * slots]
+        for x in range(r * each + 1, (r + 1) * each):
+            total = total + hidden[x * slots : (x + 1) * slots]
         out[...] = total.astype(BF16)
 
 
@@ -172,33 +170,26 @@
     return value
 
 
-def place_of(segment, segments, place):
-    return lax.rem(place[0] - segment + segments, segments)
-
-
-def edge_weights(place, which, j, mine, other, width):
+def place_of(segment, segments):
+    return lax.rem(lax.axis_index("segment") - segment + segments, segments)
+
+
+def edge_weights(which, j, mine, other, width):
     edge, under = edge_rows(width, j)
     a, b = (choose(which, refs, edge) for refs in (mine, other))
-    first = place[1] == 0
+    first = lax.axis_index("chan") == 0
     weights = jnp.concatenate([jnp.where(first, a, b), jnp.where(first, b, a)], axis=0)
     return weights, choose(which, mine, under).astype(F32)
 
 
-def send_side(place, which, j, mine, other, latent, hot, spread, source, outs):
-    weights, vectors = edge_weights(place, which, j, mine, other, latent.shape[1])
-    table = (dot(latent, weights) + vectors[0:1, :]).astype(BF16)
-    source[...] = table
-    cross_sums(table, vectors[1:2, :], hot, spread, outs)
-
-
-def partner_sums_kernel(segments, place, *refs):
+def partner_sums_kernel(segments, *refs):
     mine, other = refs[:segments], refs[segments : 2 * segments]
     raw, outs = refs[2 * segments : 2 * segments + 2], refs[2 * segments + 2 :]
     slots, width = outs[0].shape
     each = (raw[0].shape[0] - VECTORS) // slots
-    weights, vectors = edge_weights(place, place_of(0, segments, place), 0, mine, other, width)
+    weights, vectors = edge_weights(place_of(0, segments), 0, mine, other, width)
     for r, out in enumerate(outs):
-        block = jnp.where(place[1] == r, raw[0][...], raw[1][...])
+        block = jnp.where(lax.axis_index("chan") == r, raw[0][...], raw[1][...])
         table = (dot(block[0 : each * slots, :], weights) + vectors[0:1, :]).astype(BF16).astype(F32)
         rows = block[each * slots :, 0:slots].astype(F32)
         coefs = [sum(rows[i : i + 1] for i in range(3 * x + 1, 3 * x + 3)) + rows[3 * x : 3 * x + 1] for x in range(each)]
@@ -211,14 +202,14 @@
         out[...] = total.astype(BF16)
 
 
-def inner_kernel(segments, segment, j, first, place, *refs):
+def inner_kernel(segments, segment, j, first, *refs):
     mine, other = refs[:segments], refs[segments : 2 * segments]
     source, hot, spread, sums = refs[2 * segments :]
     nodes, width = sums.shape
-    which = place_of(segment, segments, place)
+    which = place_of(segment, segments)
     table = source[...]
     if first:
-        weights, vectors = edge_weights(place, which, j, mine, other, width)
+        weights, vectors = edge_weights(which, j, mine, other, width)
         table = (dot(table, weights) + vectors[0:1, :]).astype(BF16)
     gain = choose(which, mine, edge_rows(width, j)[1]).astype(F32)[1:2, :]
     total = None
@@ -229,47 +220,55 @@
     sums[...] = total
 
 
-def weights_kernel(segments, held, segment, j, place, *refs):
+def weights_kernel(segments, held, segment, j, *refs):
     mine, other, vec_mine, vec_other = (refs[i * segments : (i + 1) * segments] for i in range(4))
     latent, before, chosen = refs[4 * segments :]
     width = before.shape[1]
     half = width // 2
     inner, outer = node_rows(width, held, j)
-    which = place_of(segment, segments, place)
+    which = place_of(segment, segments)
     in_a, in_b = (choose(which, refs, inner) for refs in (mine, other))
     vec_a, vec_b = (choose(which, refs, edge_rows(width, j)[1]) for refs in (vec_mine, vec_other))
     joined = jnp.concatenate([in_a[:, :half], in_b[:, :half]], axis=1)
     bias = jnp.concatenate([vec_a[:, :half], vec_b[:, :half]], axis=1).astype(F32)[4:5, :]
     before[...] = dot(latent[...], joined) + bias
     chosen[0:width, :] = jnp.concatenate([in_a[:, half:], in_b[:, half:]], axis=1)
-    chosen[width : width + half, :] = choose(which, mine, outer)
-    chosen[width + half : 2 * width, :] = choose(which, other, outer)
+    for start, refs in ((width, mine), (width + half, other)):
+        out = choose(which, refs, outer).astype(F32)
+        chosen[start : start + half, :] = (out - jnp.mean(out, axis=1, keepdims=True)).astype(BF16)
     chosen[2 * width : 2 * width + VECTORS, :] = vec_a
 
 
-def node_kernel(segments, segment, j, last, rounds, place, *refs):
+def node_kernel(segments, segment, j, last, rounds, *refs):
     arrived, refs = refs[:rounds], refs[rounds:]
     latent, sums, before, chosen, scatter = refs[:5]
     width = sums.shape[1]
     half = width // 2
-    summed = sums[...] + dot(scatter[...], jnp.concatenate([block[...] for block in arrived[::-1]], axis=0))
+    nodes = sums.shape[0]
+    mine, other = refs[5 : 5 + segments], refs[5 + segments : 5 + 2 * segments]
+    if last:
+        (result,) = refs[5:]
+    else:
+        hot, spread, result, source, *outs = refs[5 + 2 * segments :]
+        weights, edge_vectors = edge_weights(
+            place_of(segment, segments), j, mine, other, width
+        )
+    blocks = jnp.concatenate([block[...] for block in arrived[::-1]], axis=0)
+    vectors = chosen[2 * width : 2 * width + VECTORS, :].astype(F32)
+    summed = sums[...] + dot(scatter[...], blocks)
     hidden = before[...] + dot(summed.astype(BF16), chosen[0:width, :])
     hidden = jnp.maximum(hidden, 0.0).astype(BF16)
-    mixed = dot(hidden[:, :half], chosen[width : width + half, :]).astype(BF16).astype(F32)
-    mixed = mixed + dot(hidden[:, half:], chosen[width + half : 2 * width, :]).astype(BF16).astype(F32)
-    vectors = chosen[2 * width : 2 * width + VECTORS, :].astype(F32)
-    centred = mixed - jnp.mean(mixed, axis=1, keepdims=True)
-    spread_of = jnp.mean(centred * centred, axis=1, keepdims=True)
-    normed = centred * lax.rsqrt(spread_of + 1e-05) * vectors[2:3, :] + vectors[3:4, :]
+    centred = dot(hidden, chosen[width : 2 * width, :])
+    variance = jnp.mean(centred * centred, axis=1, keepdims=True)
+    normed = centred * lax.rsqrt(variance + 1e-05) * vectors[2:3, :] + vectors[3:4, :]
     fresh = (latent[...].astype(F32) + normed).astype(BF16)
     if last:
-        refs[5][0] = fresh
+        result[0] = fresh
         return
-    mine, other = refs[5 : 5 + segments], refs[5 + segments : 5 + 2 * segments]
-    hot, spread, result, source, *outs = refs[5 + 2 * segments :]
     result[...] = fresh
-    which = place_of(segment, segments, place)
-    send_side(place, which, j, mine, other, fresh, hot, spread, source, outs)
+    table = (dot(fresh, weights) + edge_vectors[0:1, :]).astype(BF16)
+    source[...] = table
+    cross_sums(table, edge_vectors[1:2, :], hot, spread, outs)
 
 
 def partner_route(count, r):
@@ -299,7 +298,6 @@
     degree, edges = neighbors.shape[0], cross_src.shape[0] * cross_src.shape[1]
     half = width // 2
     assert micro == segments and cores == rounds == 2
-    place = jnp.stack([lax.axis_index("segment"), lax.axis_index("chan")]).astype(jnp.int32)
 
     def in_hbm(*arrays):
         return [pltpu.with_memory_space_constraint(array, pltpu.HBM) for array in arrays]
@@ -320,7 +318,7 @@
     packs = kernel_call(
         pack_kernel,
         [shape((node_rows(width, held, j)[1].stop, width), BF16) for j in range(held)],
-        [place, *in_hbm(w_edge, w_node_in, w_node_out, *vectors)],
+        [*in_hbm(w_edge, w_node_in, w_node_out, *vectors)],
         1 << 10,
         scratch=[*buffers(*vectors), pltpu.SemaphoreType.DMA((5 + 4 * held,))],
     )
@@ -334,7 +332,7 @@
             shape((nodes, rounds * slots), BF16),
             shape((edges // rounds * slots + VECTORS, width), BF16),
         ],
-        [place, *in_hbm(latents, *graph), packs[0]],
+        [*in_hbm(latents, *graph), packs[0]],
         1 << 10,
         after=1,
         scratch=[*buffers(*graph), pltpu.SemaphoreType.DMA((4,))],
@@ -348,7 +346,6 @@
         [shape((degree * nodes, nodes), BF16), shape((degree * nodes, LANES), F32)],
         [*in_hbm(neighbors, edge_coef), scatter],
         1 << 30,
-        smem=0,
         after=1,
         scratch=[*buffers(neighbors, edge_coef), pltpu.SemaphoreType.DMA((2,))],
     )
@@ -372,25 +369,25 @@
         sums = kernel_call(
             functools.partial(inner_kernel, segments, segment, j, layer == 0),
             shape((nodes, width), F32),
-            [place, *weights, source, hot, spread],
+            [*weights, source, hot, spread],
             1 << 31,
         )
         before, chosen = kernel_call(
             functools.partial(weights_kernel, segments, held, segment, j),
             [shape((nodes, width), F32), shape((2 * width + VECTORS, width), BF16)],
-            [place, *mine_of[j], *other_of[j], *weights, latent],
+            [*mine_of[j], *other_of[j], *weights, latent],
             1 << 28,
         )
         if layer == 0:
             arrived = kernel_call(
                 functools.partial(partner_sums_kernel, segments),
                 sends[1:],
-                [place, *weights, raw, swap(raw)],
+                [*weights, raw, swap(raw)],
                 1 << 28,
             )
         else:
             arrived = exchange(blocks)
-        operands = [place, *arrived[::-1], latent, sums, before, chosen, scatter]
+        operands = [*arrived[::-1], latent, sums, before, chosen, scatter]
         last = layer == total - 1
         follow, step = divmod(layer + 1, held)
         if last:

time: 46 us -> 42.4 us (0.922)
  Pallas kernels: 23.3 us -> 14.6 us
  waiting for transfers between devices: 3.35 us -> 9.18 us
  starting transfers between devices: 18.8 us -> 18.2 us
    pallas_call x16, Pallas kernels: 23.3 us -> 14.6 us  [kernel_call(): pl.pallas_call(body, out_shape=outs, in_specs=[HBM if scratch else VMEM]...]
    ppermute x6, waiting for transfers between devices: 1.08 us -> 3.8 us  [exchange(): lax.ppermute(block, 'dom', partner_route(parts, r))]
    ppermute x2, waiting for transfers between devices: 0.38 us -> 3.07 us  [per_device(): lax.ppermute(ready, 'segment', route)]
    ppermute x6, starting transfers between devices: 11.6 us -> 11 us  [exchange(): lax.ppermute(block, 'dom', partner_route(parts, r))]
  transfers between devices with their start and end apart: 14 -> 14, of which waited for: 7 -> 9; matrix products, arithmetic and copies ran while one was open for 0% -> 0% of each run, Pallas kernels for 35% -> 23%
where the time goes in v4:
time: 42.4 us; the launch traced here: 42.1 us
  starting transfers between devices  18.2 us (43%)
  Pallas kernels  14.6 us (34%)
  waiting for transfers between devices  9.18 us (22%)
    pallas_call x16, Pallas kernels, kernel_call(): pl.pallas_call(body, out_shape=outs, in_specs=[HBM if scratch else VMEM]...  14.6 us
    ppermute x6, starting transfers between devices, exchange(): lax.ppermute(block, 'dom', partner_route(parts, r))  11 us
    ppermute x2, starting transfers between devices, per_device(): lax.ppermute(ready, 'segment', route)  4.74 us
    ppermute x6, waiting for transfers between devices, exchange(): lax.ppermute(block, 'dom', partner_route(parts, r))  3.8 us
    ppermute x2, waiting for transfers between devices, per_device(): lax.ppermute(ready, 'segment', route)  3.07 us
    ppermute x1, waiting for transfers between devices, per_device(): raw = lax.ppermute(raw, ('dom', 'chan'), route)  1.87 us
    ppermute x1, starting transfers between devices, per_device(): raw = lax.ppermute(raw, ('dom', 'chan'), route)  1.64 us
  transfers between devices with their start and end apart: 14, of which 9 were waited for; matrix products, arithmetic and copies ran while one was open for 0% of the time, Pallas kernels for 23%

profile of v4, /device:TPU:0, one launch (start us, length us, event | category | flops | bytes accessed | tf_op | source)
XLA Modules:
  0.0 42.1 jit_solution(536033750081503929)
XLA Ops:
  0.0 1.3 %shard_map.136 = (bf16[672,256]{1,0:T(8,128)(2,1)S(1)}, bf16[384,256]{1,0:T(8,128)(2,1)S(1)}) custom-call(bf16[2,256,256]{2,1,0:T(8,128)(2,1)} %w_edge.1, bf16[2,512,128]{2,1,0:T(8,128)(2,1)} %w_in.1, bf16[2,128,256]{2,1,0:T(8,128)(2,1)} %w_out.1, bf16[2,256]{1,0:T(2,128)(2,1)} %e_bias.1, bf16[2,256]{1,0:T(2,128)(2,1)} %e_gain.1, bf16[2,256]{1,0:T(2,128)(2,1)} %g_norm.1, ...), custom_call_target="tpu_custom_call" | custom-call | flops 1024 | bytes 65536 | tf_op jit(solution)/shard_map/pallas_call | solution.py:24
  1.3 3.0 %collective-permute-start = (bf16[672,256]{1,0:T(8,128)(2,1)S(1)}, bf16[672,256]{1,0:T(8,128)(2,1)S(1)}, u32[]{:S(2)}, u32[]{:S(2)}) collective-permute-start(bf16[672,256]{1,0:T(8,128)(2,1)S(1)} %get-tuple-element.44._.refs_0_.refs_4_.refs_7_), channel_id=1, source_target_pairs={{0,2},{2,0},{1,3},{3,1},{4,6},{6,4},{5,7},{7,5},{8,10},{10,8},{9,1... | collective-permute-start | bytes 1032200 | tf_op jit(solution)/shard_map/ppermute | solution.py:356
  4.3 1.4 %shard_map.137 = (bf16[512,256]{1,0:T(8,128)(2,1)S(1)}, bf16[512,512]{1,0:T(8,128)(2,1)S(1)}, f32[512,128]{1,0:T(8,128)S(1)}, bf16[512,256]{1,0:T(8,128)(2,1)S(1)}, bf16[272,256]{1,0:T(8,128)(2,1)S(1)}) custom-call(bf16[2,512,256]{2,1,0:T(8,128)(2,1)} %latents.1, s32[2,2,128]{2,1,0:T(2,128)} %src.1, f32[2,2,128]{2,1,0:T(2,128)} %coef.2, s32[2,128]{1,0:T(2,128)} %recv.1, ...), custom_call_target="tpu_custom_call" | custom-call | flops 1024 | bytes 65536 | tf_op jit(solution)/shard_map/pallas_call | solution.py:24
  5.7 1.6 %collective-permute-start.2 = (bf16[272,256]{1,0:T(8,128)(2,1)S(1)}, bf16[272,256]{1,0:T(8,128)(2,1)S(1)}, u32[]{:S(2)}, u32[]{:S(2)}) collective-permute-start(bf16[272,256]{1,0:T(8,128)(2,1)S(1)} %get-tuple-element.45), channel_id=1, source_target_pairs={{0,4},{4,0},{8,12},{12,8},{1,9},{5,13},{9,1},{13,5},{2,6},{6,2},{1... | collective-permute-start | bytes 417800 | tf_op jit(solution)/shard_map/ppermute | solution.py:343
  7.3 0.3 collective-permute-start.1
  7.6 1.9 %shard_map.138 = (bf16[3072,512]{1,0:T(8,128)(2,1)S(1)}, f32[3072,128]{1,0:T(8,128)S(1)}) custom-call(s32[6,512]{1,0:T(8,128)} %neighbors.1, f32[6,512]{1,0:T(8,128)} %coef.3, bf16[512,256]{1,0:T(8,128)(2,1)S(1)} %get-tuple-element.43._.refs_6_), custom_call_target="tpu_custom_call" | custom-call | flops 1073741824 | bytes 65536 | tf_op jit(solution)/shard_map/pallas_call | solution.py:24
  9.5 1.9 %collective-permute-done.2.refs_4_ = bf16[272,256]{1,0:T(8,128)(2,1)S(1)} collective-permute-done((bf16[272,256]{1,0:T(8,128)(2,1)S(1)}, bf16[272,256]{1,0:T(8,128)(2,1)S(1)}, u32[]{:S(2)}, u32[]{:S(2)}) %collective-permute-start.2) | collective-permute-done | bytes 139296 | tf_op jit(solution)/shard_map/ppermute | solution.py:343
  11.4 0.9 %collective-permute-done.refs_1_.refs_5_.refs_8_ = bf16[672,256]{1,0:T(8,128)(2,1)S(1)} collective-permute-done((bf16[672,256]{1,0:T(8,128)(2,1)S(1)}, bf16[672,256]{1,0:T(8,128)(2,1)S(1)}, u32[]{:S(2)}, u32[]{:S(2)}) %collective-permute-start) | collective-permute-done | bytes 344096 | tf_op jit(solution)/shard_map/ppermute | solution.py:356
  12.3 0.5 %collective-permute-start.8 = (bf16[384,256]{1,0:T(8,128)(2,1)S(1)}, bf16[384,256]{1,0:T(8,128)(2,1)S(1)}, u32[]{:S(2)}, u32[]{:S(2)}) collective-permute-start(bf16[384,256]{1,0:T(8,128)(2,1)S(1)} %get-tuple-element.61.refs_0_), channel_id=1, source_target_pairs={{0,1},{1,0},{2,3},{3,2},{4,5},{5,4},{6,7},{7,6},{8,9},{9,8},{10,11... | collective-permute-start | bytes 589832 | tf_op jit(solution)/shard_map/ppermute | solution.py:309
  12.8 1.7 %collective-permute-start.7 = (bf16[384,256]{1,0:T(8,128)(2,1)S(1)}, bf16[384,256]{1,0:T(8,128)(2,1)S(1)}, u32[]{:S(2)}, u32[]{:S(2)}) collective-permute-start(bf16[384,256]{1,0:T(8,128)(2,1)S(1)} %get-tuple-element.61.refs_0_), channel_id=1, source_target_pairs={{0,2},{2,0},{1,3},{3,1},{4,6},{6,4},{5,7},{7,5},{8,10},{10,8},{9,1... | collective-permute-start | bytes 589832 | tf_op jit(solution)/shard_map/ppermute | solution.py:356
  14.6 1.2 %shard_map.140.refs_3_ = f32[512,256]{1,0:T(8,128)S(1)} custom-call(bf16[672,256]{1,0:T(8,128)(2,1)S(1)} %get-tuple-element.44._.refs_0_.refs_4_.refs_7_, bf16[672,256]{1,0:T(8,128)(2,1)S(1)} %collective-permute-done.refs_1_.refs_5_.refs_8_, bf16[672,256]{1,0:T(8,128)(2,1)S(1)} %collective-permute-done.1.refs_2_.refs_6_.refs_9_, ...), custom_call_target="tpu_custom_call" | custom-call | flops 2147483648 | bytes 65536 | tf_op jit(solution)/shard_map/pallas_call | solution.py:24
  16.1 0.3 shard_map.139
  16.4 1.1 %shard_map.142 = (bf16[512,256]{1,0:T(8,128)(2,1)S(1)}, bf16[512,256]{1,0:T(8,128)(2,1)S(1)}, bf16[128,256]{1,0:T(8,128)(2,1)S(1)}, bf16[128,256]{1,0:T(8,128)(2,1)S(1)}) custom-call(bf16[128,256]{1,0:T(8,128)(2,1)S(1)} %get-tuple-element.48.refs_0_, bf16[128,256]{1,0:T(8,128)(2,1)S(1)} %get-tuple-element.49.refs_1_, ...), custom_call_target="tpu_custom_call" | custom-call | flops 1073741824 | bytes 65536 | tf_op jit(solution)/shard_map/pallas_call | solution.py:24
  17.5 2.2 %collective-permute-done.7.refs_1_ = bf16[384,256]{1,0:T(8,128)(2,1)S(1)} collective-permute-done((bf16[384,256]{1,0:T(8,128)(2,1)S(1)}, bf16[384,256]{1,0:T(8,128)(2,1)S(1)}, u32[]{:S(2)}, u32[]{:S(2)}) %collective-permute-start.7) | collective-permute-done | bytes 196640 | tf_op jit(solution)/shard_map/ppermute | solution.py:356
  19.6 2.8 %collective-permute-start.5 = (bf16[128,256]{1,0:T(8,128)(2,1)S(1)}, bf16[128,256]{1,0:T(8,128)(2,1)S(1)}, u32[]{:S(2)}, u32[]{:S(2)}) collective-permute-start(bf16[128,256]{1,0:T(8,128)(2,1)S(1)} %get-tuple-element.56), channel_id=1, source_target_pairs={{0,8},{4,12},{8,0},{12,4},{1,9},{5,13},{9,1},{13,5},{2,10},{6,14},... | collective-permute-start | bytes 196616 | tf_op jit(solution)/shard_map/ppermute | solution.py:312
  22.5 1.6 %collective-permute-start.6 = (bf16[128,256]{1,0:T(8,128)(2,1)S(1)}, bf16[128,256]{1,0:T(8,128)(2,1)S(1)}, u32[]{:S(2)}, u32[]{:S(2)}) collective-permute-start(bf16[128,256]{1,0:T(8,128)(2,1)S(1)} %get-tuple-element.57), channel_id=1, source_target_pairs={{0,4},{4,0},{8,12},{12,8},{1,5},{5,1},{9,13},{13,9},{2,6},{6,2},{1... | collective-permute-start | bytes 196616 | tf_op jit(solution)/shard_map/ppermute | solution.py:312
  24.1 1.0 %shard_map.143.refs_3_ = f32[512,256]{1,0:T(8,128)S(1)} custom-call(bf16[672,256]{1,0:T(8,128)(2,1)S(1)} %get-tuple-element.44._.refs_0_.refs_4_.refs_7_, bf16[672,256]{1,0:T(8,128)(2,1)S(1)} %collective-permute-done.refs_1_.refs_5_.refs_8_, bf16[672,256]{1,0:T(8,128)(2,1)S(1)} %collective-permute-done.1.refs_2_.refs_6_.refs_9_, ...), custom_call_target="tpu_custom_call" | custom-call | flops 2147483648 | bytes 65536 | tf_op jit(solution)/shard_map/pallas_call | solution.py:24
  25.1 0.4 %collective-permute-done.9.refs_3_ = bf16[384,256]{1,0:T(8,128)(2,1)S(1)} collective-permute-done((bf16[384,256]{1,0:T(8,128)(2,1)S(1)}, bf16[384,256]{1,0:T(8,128)(2,1)S(1)}, u32[]{:S(2)}, u32[]{:S(2)}) %collective-permute-start.9) | collective-permute-done | bytes 196640 | tf_op jit(solution)/shard_map/ppermute | solution.py:309
  25.8 1.0 %collective-permute-done.6.refs_1_ = bf16[128,256]{1,0:T(8,128)(2,1)S(1)} collective-permute-done((bf16[128,256]{1,0:T(8,128)(2,1)S(1)}, bf16[128,256]{1,0:T(8,128)(2,1)S(1)}, u32[]{:S(2)}, u32[]{:S(2)}) %collective-permute-start.6) | collective-permute-done | bytes 65568 | tf_op jit(solution)/shard_map/ppermute | solution.py:312
  26.8 1.1 %shard_map.145 = (bf16[512,256]{1,0:T(8,128)(2,1)S(1)}, bf16[512,256]{1,0:T(8,128)(2,1)S(1)}, bf16[128,256]{1,0:T(8,128)(2,1)S(1)}, bf16[128,256]{1,0:T(8,128)(2,1)S(1)}) custom-call(bf16[128,256]{1,0:T(8,128)(2,1)S(1)} %collective-permute-done.5.refs_0_, bf16[128,256]{1,0:T(8,128)(2,1)S(1)} %collective-permute-done.6.refs_1_, ...), custom_call_target="tpu_custom_call" | custom-call | flops 1073741824 | bytes 65536 | tf_op jit(solution)/shard_map/pallas_call | solution.py:24
  27.8 1.2 %collective-permute-start.10 = (bf16[128,256]{1,0:T(8,128)(2,1)S(1)}, bf16[128,256]{1,0:T(8,128)(2,1)S(1)}, u32[]{:S(2)}, u32[]{:S(2)}) collective-permute-start(bf16[128,256]{1,0:T(8,128)(2,1)S(1)} %get-tuple-element.65), channel_id=1, source_target_pairs={{0,8},{4,12},{8,0},{12,4},{1,9},{5,13},{9,1},{13,5},{2,10},{6,14},... | collective-permute-start | bytes 196616 | tf_op jit(solution)/shard_map/ppermute | solution.py:312
  29.1 1.9 %collective-permute-start.11 = (bf16[128,256]{1,0:T(8,128)(2,1)S(1)}, bf16[128,256]{1,0:T(8,128)(2,1)S(1)}, u32[]{:S(2)}, u32[]{:S(2)}) collective-permute-start(bf16[128,256]{1,0:T(8,128)(2,1)S(1)} %get-tuple-element.66), channel_id=1, source_target_pairs={{0,4},{4,0},{8,12},{12,8},{1,5},{5,1},{9,13},{13,9},{2,6},{6,2},{1... | collective-permute-start | bytes 196616 | tf_op jit(solution)/shard_map/ppermute | solution.py:312
  31.0 1.0 %shard_map.146.refs_3_ = f32[512,256]{1,0:T(8,128)S(1)} custom-call(bf16[672,256]{1,0:T(8,128)(2,1)S(1)} %get-tuple-element.44._.refs_0_.refs_4_.refs_7_, bf16[672,256]{1,0:T(8,128)(2,1)S(1)} %collective-permute-done.refs_1_.refs_5_.refs_8_, bf16[672,256]{1,0:T(8,128)(2,1)S(1)} %collective-permute-done.1.refs_2_.refs_6_.refs_9_, ...), custom_call_target="tpu_custom_call" | custom-call | flops 2147483648 | bytes 65536 | tf_op jit(solution)/shard_map/pallas_call | solution.py:24
  32.2 0.9 %collective-permute-done.10.refs_0_ = bf16[128,256]{1,0:T(8,128)(2,1)S(1)} collective-permute-done((bf16[128,256]{1,0:T(8,128)(2,1)S(1)}, bf16[128,256]{1,0:T(8,128)(2,1)S(1)}, u32[]{:S(2)}, u32[]{:S(2)}) %collective-permute-start.10) | collective-permute-done | bytes 65568 | tf_op jit(solution)/shard_map/ppermute | solution.py:312
  33.1 0.7 %collective-permute-done.11.refs_1_ = bf16[128,256]{1,0:T(8,128)(2,1)S(1)} collective-permute-done((bf16[128,256]{1,0:T(8,128)(2,1)S(1)}, bf16[128,256]{1,0:T(8,128)(2,1)S(1)}, u32[]{:S(2)}, u32[]{:S(2)}) %collective-permute-start.11) | collective-permute-done | bytes 65568 | tf_op jit(solution)/shard_map/ppermute | solution.py:312
  33.8 1.1 %shard_map.148 = (bf16[512,256]{1,0:T(8,128)(2,1)S(1)}, bf16[512,256]{1,0:T(8,128)(2,1)S(1)}, bf16[128,256]{1,0:T(8,128)(2,1)S(1)}, bf16[128,256]{1,0:T(8,128)(2,1)S(1)}) custom-call(bf16[128,256]{1,0:T(8,128)(2,1)S(1)} %collective-permute-done.10.refs_0_, bf16[128,256]{1,0:T(8,128)(2,1)S(1)} %collective-permute-done.11.refs_1_, ...), custom_call_target="tpu_custom_call" | custom-call | flops 1073741824 | bytes 65536 | tf_op jit(solution)/shard_map/pallas_call | solution.py:24
  34.9 1.6 %collective-permute-start.12 = (bf16[128,256]{1,0:T(8,128)(2,1)S(1)}, bf16[128,256]{1,0:T(8,128)(2,1)S(1)}, u32[]{:S(2)}, u32[]{:S(2)}) collective-permute-start(bf16[128,256]{1,0:T(8,128)(2,1)S(1)} %get-tuple-element.71), channel_id=1, source_target_pairs={{0,8},{4,12},{8,0},{12,4},{1,9},{5,13},{9,1},{13,5},{2,10},{6,14},... | collective-permute-start | bytes 196616 | tf_op jit(solution)/shard_map/ppermute | solution.py:312
  36.5 1.8 %collective-permute-start.13 = (bf16[128,256]{1,0:T(8,128)(2,1)S(1)}, bf16[128,256]{1,0:T(8,128)(2,1)S(1)}, u32[]{:S(2)}, u32[]{:S(2)}) collective-permute-start(bf16[128,256]{1,0:T(8,128)(2,1)S(1)} %get-tuple-element.72), channel_id=1, source_target_pairs={{0,4},{4,0},{8,12},{12,8},{1,5},{5,1},{9,13},{13,9},{2,6},{6,2},{1... | collective-permute-start | bytes 196616 | tf_op jit(solution)/shard_map/ppermute | solution.py:312
  38.3 1.0 %shard_map.149.refs_3_ = f32[512,256]{1,0:T(8,128)S(1)} custom-call(bf16[672,256]{1,0:T(8,128)(2,1)S(1)} %get-tuple-element.44._.refs_0_.refs_4_.refs_7_, bf16[672,256]{1,0:T(8,128)(2,1)S(1)} %collective-permute-done.refs_1_.refs_5_.refs_8_, bf16[672,256]{1,0:T(8,128)(2,1)S(1)} %collective-permute-done.1.refs_2_.refs_6_.refs_9_, ...), custom_call_target="tpu_custom_call" | custom-call | flops 2147483648 | bytes 65536 | tf_op jit(solution)/shard_map/pallas_call | solution.py:24
  39.5 0.6 %collective-permute-done.12.refs_0_ = bf16[128,256]{1,0:T(8,128)(2,1)S(1)} collective-permute-done((bf16[128,256]{1,0:T(8,128)(2,1)S(1)}, bf16[128,256]{1,0:T(8,128)(2,1)S(1)}, u32[]{:S(2)}, u32[]{:S(2)}) %collective-permute-start.12) | collective-permute-done | bytes 65568 | tf_op jit(solution)/shard_map/ppermute | solution.py:312
  40.1 0.7 %collective-permute-done.13.refs_1_ = bf16[128,256]{1,0:T(8,128)(2,1)S(1)} collective-permute-done((bf16[128,256]{1,0:T(8,128)(2,1)S(1)}, bf16[128,256]{1,0:T(8,128)(2,1)S(1)}, u32[]{:S(2)}, u32[]{:S(2)}) %collective-permute-start.13) | collective-permute-done | bytes 65568 | tf_op jit(solution)/shard_map/ppermute | solution.py:312
  40.8 1.3 %shard_map.151 = bf16[1,512,256]{2,1,0:T(8,128)(2,1)} custom-call(bf16[128,256]{1,0:T(8,128)(2,1)S(1)} %collective-permute-done.12.refs_0_, bf16[128,256]{1,0:T(8,128)(2,1)S(1)} %collective-permute-done.13.refs_1_, bf16[512,256]{1,0:T(8,128)(2,1)S(1)} %get-tuple-element.73.refs_8_.refs_2_, f32[512,256]{1,0:T(8,128)S(1)} %shard_map.149.refs_3_, ...), custom_call_target="tpu_custom_call" | custom-call | flops 1073741824 | bytes 65536 | tf_op jit(solution)/shard_map/pallas_call | solution.py:24
  (12 shorter events, 1.0 us)
Async XLA Ops:
  1.3 11.1 %collective-permute-start = (bf16[672,256]{1,0:T(8,128)(2,1)S(1)}, bf16[672,256]{1,0:T(8,128)(2,1)S(1)}, u32[]{:S(2)}, u32[]{:S(2)}) collective-permute-start(bf16[672,256]{1,0:T(8,128)(2,1)S(1)} %get-tuple-element.44._.refs_0_.refs_4_.refs_7_), channel_id=1, source_target_pairs={{0,2},{2,0},{1,3},{3,1},{4,6},{6,4},{5,7},{7,5},{8,10},{10,8},{9,1... | collective-permute-start | bytes 1032200 | tf_op jit(solution)/shard_map/ppermute | solution.py:356
  5.7 5.7 %collective-permute-start.2 = (bf16[272,256]{1,0:T(8,128)(2,1)S(1)}, bf16[272,256]{1,0:T(8,128)(2,1)S(1)}, u32[]{:S(2)}, u32[]{:S(2)}) collective-permute-start(bf16[272,256]{1,0:T(8,128)(2,1)S(1)} %get-tuple-element.45), channel_id=1, source_target_pairs={{0,4},{4,0},{8,12},{12,8},{1,9},{5,13},{9,1},{13,5},{2,6},{6,2},{1... | collective-permute-start | bytes 417800 | tf_op jit(solution)/shard_map/ppermute | solution.py:343
  7.3 7.3 %collective-permute-start.1 = (bf16[672,256]{1,0:T(8,128)(2,1)S(1)}, bf16[672,256]{1,0:T(8,128)(2,1)S(1)}, u32[]{:S(2)}, u32[]{:S(2)}) collective-permute-start(bf16[672,256]{1,0:T(8,128)(2,1)S(1)} %get-tuple-element.44._.refs_0_.refs_4_.refs_7_), channel_id=1, source_target_pairs={{0,1},{1,0},{2,3},{3,2},{4,5},{5,4},{6,7},{7,6},{8,9},{9,8},{10,11... | collective-permute-start | bytes 1032200 | tf_op jit(solution)/shard_map/ppermute | solution.py:309
  12.3 2.3 %collective-permute-start.3 = (bf16[672,256]{1,0:T(8,128)(2,1)S(1)}, bf16[672,256]{1,0:T(8,128)(2,1)S(1)}, u32[]{:S(2)}, u32[]{:S(2)}) collective-permute-start(bf16[672,256]{1,0:T(8,128)(2,1)S(1)} %collective-permute-done.refs_1_.refs_5_.refs_8_), channel_id=1, source_target_pairs={{0,1},{1,0},{2,3},{3,2},{4,5},{5,4},{6,7},{7,6},{8,9},{9,8},{10,11... | collective-permute-start | bytes 1032200 | tf_op jit(solution)/shard_map/ppermute | solution.py:309
  12.3 12.7 %collective-permute-start.8 = (bf16[384,256]{1,0:T(8,128)(2,1)S(1)}, bf16[384,256]{1,0:T(8,128)(2,1)S(1)}, u32[]{:S(2)}, u32[]{:S(2)}) collective-permute-start(bf16[384,256]{1,0:T(8,128)(2,1)S(1)} %get-tuple-element.61.refs_0_), channel_id=1, source_target_pairs={{0,1},{1,0},{2,3},{3,2},{4,5},{5,4},{6,7},{7,6},{8,9},{9,8},{10,11... | collective-permute-start | bytes 589832 | tf_op jit(solution)/shard_map/ppermute | solution.py:309
  12.8 6.8 %collective-permute-start.7 = (bf16[384,256]{1,0:T(8,128)(2,1)S(1)}, bf16[384,256]{1,0:T(8,128)(2,1)S(1)}, u32[]{:S(2)}, u32[]{:S(2)}) collective-permute-start(bf16[384,256]{1,0:T(8,128)(2,1)S(1)} %get-tuple-element.61.refs_0_), channel_id=1, source_target_pairs={{0,2},{2,0},{1,3},{3,1},{4,6},{6,4},{5,7},{7,5},{8,10},{10,8},{9,1... | collective-permute-start | bytes 589832 | tf_op jit(solution)/shard_map/ppermute | solution.py:356
  14.6 1.5 %collective-permute-start.4 = (bf16[272,256]{1,0:T(8,128)(2,1)S(1)}, bf16[272,256]{1,0:T(8,128)(2,1)S(1)}, u32[]{:S(2)}, u32[]{:S(2)}) collective-permute-start(bf16[272,256]{1,0:T(8,128)(2,1)S(1)} %collective-permute-done.2.refs_4_), channel_id=1, source_target_pairs={{0,1},{1,0},{2,3},{3,2},{4,5},{5,4},{6,7},{7,6},{8,9},{9,8},{10,11... | collective-permute-start | bytes 417800 | tf_op jit(solution)/shard_map/ppermute | solution.py:309
  19.6 6.1 %collective-permute-start.5 = (bf16[128,256]{1,0:T(8,128)(2,1)S(1)}, bf16[128,256]{1,0:T(8,128)(2,1)S(1)}, u32[]{:S(2)}, u32[]{:S(2)}) collective-permute-start(bf16[128,256]{1,0:T(8,128)(2,1)S(1)} %get-tuple-element.56), channel_id=1, source_target_pairs={{0,8},{4,12},{8,0},{12,4},{1,9},{5,13},{9,1},{13,5},{2,10},{6,14},... | collective-permute-start | bytes 196616 | tf_op jit(solution)/shard_map/ppermute | solution.py:312
  22.5 4.3 %collective-permute-start.6 = (bf16[128,256]{1,0:T(8,128)(2,1)S(1)}, bf16[128,256]{1,0:T(8,128)(2,1)S(1)}, u32[]{:S(2)}, u32[]{:S(2)}) collective-permute-start(bf16[128,256]{1,0:T(8,128)(2,1)S(1)} %get-tuple-element.57), channel_id=1, source_target_pairs={{0,4},{4,0},{8,12},{12,8},{1,5},{5,1},{9,13},{13,9},{2,6},{6,2},{1... | collective-permute-start | bytes 196616 | tf_op jit(solution)/shard_map/ppermute | solution.py:312
  24.1 1.4 %collective-permute-start.9 = (bf16[384,256]{1,0:T(8,128)(2,1)S(1)}, bf16[384,256]{1,0:T(8,128)(2,1)S(1)}, u32[]{:S(2)}, u32[]{:S(2)}) collective-permute-start(bf16[384,256]{1,0:T(8,128)(2,1)S(1)} %collective-permute-done.7.refs_1_), channel_id=1, source_target_pairs={{0,1},{1,0},{2,3},{3,2},{4,5},{5,4},{6,7},{7,6},{8,9},{9,8},{10,11... | collective-permute-start | bytes 589832 | tf_op jit(solution)/shard_map/ppermute | solution.py:309
  27.8 5.3 %collective-permute-start.10 = (bf16[128,256]{1,0:T(8,128)(2,1)S(1)}, bf16[128,256]{1,0:T(8,128)(2,1)S(1)}, u32[]{:S(2)}, u32[]{:S(2)}) collective-permute-start(bf16[128,256]{1,0:T(8,128)(2,1)S(1)} %get-tuple-element.65), channel_id=1, source_target_pairs={{0,8},{4,12},{8,0},{12,4},{1,9},{5,13},{9,1},{13,5},{2,10},{6,14},... | collective-permute-start | bytes 196616 | tf_op jit(solution)/shard_map/ppermute | solution.py:312
  29.1 4.7 %collective-permute-start.11 = (bf16[128,256]{1,0:T(8,128)(2,1)S(1)}, bf16[128,256]{1,0:T(8,128)(2,1)S(1)}, u32[]{:S(2)}, u32[]{:S(2)}) collective-permute-start(bf16[128,256]{1,0:T(8,128)(2,1)S(1)} %get-tuple-element.66), channel_id=1, source_target_pairs={{0,4},{4,0},{8,12},{12,8},{1,5},{5,1},{9,13},{13,9},{2,6},{6,2},{1... | collective-permute-start | bytes 196616 | tf_op jit(solution)/shard_map/ppermute | solution.py:312
  34.9 5.2 %collective-permute-start.12 = (bf16[128,256]{1,0:T(8,128)(2,1)S(1)}, bf16[128,256]{1,0:T(8,128)(2,1)S(1)}, u32[]{:S(2)}, u32[]{:S(2)}) collective-permute-start(bf16[128,256]{1,0:T(8,128)(2,1)S(1)} %get-tuple-element.71), channel_id=1, source_target_pairs={{0,8},{4,12},{8,0},{12,4},{1,9},{5,13},{9,1},{13,5},{2,10},{6,14},... | collective-permute-start | bytes 196616 | tf_op jit(solution)/shard_map/ppermute | solution.py:312
  36.5 4.3 %collective-permute-start.13 = (bf16[128,256]{1,0:T(8,128)(2,1)S(1)}, bf16[128,256]{1,0:T(8,128)(2,1)S(1)}, u32[]{:S(2)}, u32[]{:S(2)}) collective-permute-start(bf16[128,256]{1,0:T(8,128)(2,1)S(1)} %get-tuple-element.72), channel_id=1, source_target_pairs={{0,4},{4,0},{8,12},{12,8},{1,5},{5,1},{9,13},{13,9},{2,6},{6,2},{1... | collective-permute-start | bytes 196616 | tf_op jit(solution)/shard_map/ppermute | solution.py:312

commit v5 on v4

--- a/solution.py
+++ b/solution.py
@@ -63,30 +63,23 @@
     return slice(start, start + half), slice(start + half, start + half + VECTORS)
 
 
-def node_rows(width, held, j):
-    half = width // 2
-    start = 0 if j else edge_rows(width, held)[0].start
-    return slice(start, start + width), slice(start + width, start + width + half)
-
-
-def pack_kernel(w_edge, w_in, w_out, e_bias, e_gain, g_norm, b_norm, n_bias, *refs):
+def pack_kernel(w_edge, w_in, w_out, e_bias, e_gain, g_norm, b_norm, n_bias, edge_pack, *refs):
     held, half, width = w_out.shape
     packs, vectors, sem = refs[:held], refs[held:-1], refs[-1]
     mine = pl.multiple_of(lax.axis_index("chan") * half, half)
     pairs = list(zip((e_bias, e_gain, g_norm, b_norm, n_bias), vectors))
+    pairs += [(w_edge.at[j, pl.ds(mine, half)], edge_pack.at[edge_rows(width, j)[0]]) for j in range(held)]
     for j in range(held):
-        inner, outer = node_rows(width, held, j)
         pairs += [
-            (w_edge.at[j, pl.ds(mine, half)], packs[0].at[edge_rows(width, j)[0]]),
-            (w_in.at[j, pl.ds(0, width)], packs[j].at[inner, pl.ds(0, half)]),
-            (w_in.at[j, pl.ds(width, width)], packs[j].at[inner, pl.ds(half, half)]),
-            (w_out.at[j], packs[j].at[outer]),
+            (w_in.at[j, pl.ds(0, width)], packs[j].at[pl.ds(0, width), pl.ds(0, half)]),
+            (w_in.at[j, pl.ds(width, width)], packs[j].at[pl.ds(0, width), pl.ds(half, half)]),
+            (w_out.at[j], packs[j].at[pl.ds(width, half)]),
         ]
     copies = fetch_all(pairs, sem)
     for copy in copies[:5]:
         copy.wait()
     for j in range(held):
-        packs[0][edge_rows(width, j)[1], :] = vector_rows([ref[j : j + 1, :] for ref in vectors], width)
+        edge_pack[edge_rows(width, j)[1], :] = vector_rows([ref[j : j + 1, :] for ref in vectors], width)
     for copy in copies[5:]:
         copy.wait()
 
@@ -204,7 +197,7 @@
 
 def inner_kernel(segments, segment, j, first, *refs):
     mine, other = refs[:segments], refs[segments : 2 * segments]
-    source, hot, spread, sums = refs[2 * segments :]
+    source, hot, spread, *_, sums = refs[2 * segments :]
     nodes, width = sums.shape
     which = place_of(segment, segments)
     table = source[...]
@@ -220,12 +213,12 @@
     sums[...] = total
 
 
-def weights_kernel(segments, held, segment, j, *refs):
+def weights_kernel(segments, segment, j, *refs):
     mine, other, vec_mine, vec_other = (refs[i * segments : (i + 1) * segments] for i in range(4))
     latent, before, chosen = refs[4 * segments :]
     width = before.shape[1]
     half = width // 2
-    inner, outer = node_rows(width, held, j)
+    inner, outer = slice(0, width), slice(width, width + half)
     which = place_of(segment, segments)
     in_a, in_b = (choose(which, refs, inner) for refs in (mine, other))
     vec_a, vec_b = (choose(which, refs, edge_rows(width, j)[1]) for refs in (vec_mine, vec_other))
@@ -315,9 +308,9 @@
         return lax.optimization_barrier((arrays, made))[0]
 
     vectors = (edge_bias, edge_gain, norm_gain, norm_bias, node_bias)
-    packs = kernel_call(
+    edge_pack, *node_packs = kernel_call(
         pack_kernel,
-        [shape((node_rows(width, held, j)[1].stop, width), BF16) for j in range(held)],
+        [shape((edge_rows(width, held)[0].start, width), BF16)] + [shape((width + half, width), BF16)] * held,
         [*in_hbm(w_edge, w_node_in, w_node_out, *vectors)],
         1 << 10,
         scratch=[*buffers(*vectors), pltpu.SemaphoreType.DMA((5 + 4 * held,))],
@@ -332,7 +325,7 @@
             shape((nodes, rounds * slots), BF16),
             shape((edges // rounds * slots + VECTORS, width), BF16),
         ],
-        [*in_hbm(latents, *graph), packs[0]],
+        [*in_hbm(latents, *graph), edge_pack],
         1 << 10,
         after=1,
         scratch=[*buffers(*graph), pltpu.SemaphoreType.DMA((4,))],
@@ -350,33 +343,30 @@
         scratch=[*buffers(neighbors, edge_coef), pltpu.SemaphoreType.DMA((2,))],
     )
     routes = [[(i, (i + r) % segments) for i in range(segments)] for r in range(1, segments)]
-    mine_of, other_of = [], []
-    for j in range(held):
-        ready = once(packs[j], scatter if j else latents)
-        mine_of.append([packs[j], *[lax.ppermute(ready, "segment", route) for route in routes]])
-
+
+    def spread_out(pack):
+        return [lax.ppermute(pack, "segment", route) for route in routes]
+
+    edges_mine = spread_out(edge_pack)
+    nodes_mine = [spread_out(once(pack, scatter) if j else pack) for j, pack in enumerate(node_packs)]
+
+    def swaps(own, received, made):
+        return [own, *received, swap(once(own, scatter)), *map(swap, once(received, made))]
+
+    weights = swaps(edge_pack, edges_mine, (raw, hot))
+    node_weights = [None] * held
+    node_weights[0] = swaps(node_packs[0], nodes_mine[0], weights[-1])
     total = segments * held
     sends = [shape((nodes, width), BF16)] + [shape((slots, width), BF16)] * rounds
-    def swaps(j, made):
-        return [swap(once(packs[j], scatter)), *map(swap, once(mine_of[j][1:], made))]
-
     source = latent
     for layer in range(total):
         segment, j = divmod(layer, held)
-        if layer == 0:
-            other_of.append(swaps(0, (raw, hot)))
-        weights = [*mine_of[0], *other_of[0]]
         sums = kernel_call(
             functools.partial(inner_kernel, segments, segment, j, layer == 0),
             shape((nodes, width), F32),
-            [*weights, source, hot, spread],
+            [*weights, source, hot, spread, *(() if layer else nodes_mine[0])],
             1 << 31,
-        )
-        before, chosen = kernel_call(
-            functools.partial(weights_kernel, segments, held, segment, j),
-            [shape((nodes, width), F32), shape((2 * width + VECTORS, width), BF16)],
-            [*mine_of[j], *other_of[j], *weights, latent],
-            1 << 28,
+            after=0 if layer else segments - 1,
         )
         if layer == 0:
             arrived = kernel_call(
@@ -387,6 +377,14 @@
             )
         else:
             arrived = exchange(blocks)
+        if 0 < layer < held:
+            node_weights[j] = swaps(node_packs[j], nodes_mine[j], arrived[0])
+        before, chosen = kernel_call(
+            functools.partial(weights_kernel, segments, segment, j),
+            [shape((nodes, width), F32), shape((2 * width + VECTORS, width), BF16)],
+            [*node_weights[j], *weights, latent],
+            1 << 28,
+        )
         operands = [*arrived[::-1], latent, sums, before, chosen, scatter]
         last = layer == total - 1
         follow, step = divmod(layer + 1, held)
@@ -400,8 +398,6 @@
         )
         if not last:
             source, *blocks = rest
-        if layer + 1 < held:
-            other_of.append(swaps(layer + 1, source))
     return latent
 
 

time: 42.4 us -> 41.2 us (0.972)
  starting transfers between devices: 18.2 us -> 14.9 us
  waiting for transfers between devices: 9.18 us -> 11.3 us
    ppermute x6, waiting for transfers between devices: 3.8 us -> 7.4 us  [exchange(): lax.ppermute(block, 'dom', partner_route(parts, r))]
    ppermute x6, starting transfers between devices: 11 us -> 7.96 us  [exchange(): lax.ppermute(block, 'dom', partner_route(parts, r))]
    ppermute x2 -> x3, waiting for transfers between devices: 3.07 us -> 1.81 us  [spread_out(): return [lax.ppermute(pack, 'segment', route) for route in routes]]
    ppermute x2 -> x3, starting transfers between devices: 4.74 us -> 4.04 us  [spread_out(): return [lax.ppermute(pack, 'segment', route) for route in routes]]
    ppermute x5 -> x7, starting transfers between devices: 0.8 us -> 1.23 us  [swap(): return lax.ppermute(block, 'chan', [(0, 1), (1, 0)])]
  transfers between devices with their start and end apart: 14 -> 17, of which waited for: 9 -> 8; matrix products, arithmetic and copies ran while one was open for 0% -> 0% of each run, Pallas kernels for 23% -> 24%
where the time goes in v5:
time: 41.2 us; the launch traced here: 41 us
  starting transfers between devices  14.9 us (36%)
  Pallas kernels  14.6 us (35%)
  waiting for transfers between devices  11.3 us (27%)
    pallas_call x16, Pallas kernels, kernel_call(): pl.pallas_call(body, out_shape=outs, in_specs=[HBM if scratch else VMEM]...  14.6 us
    ppermute x6, starting transfers between devices, exchange(): lax.ppermute(block, 'dom', partner_route(parts, r))  7.96 us
    ppermute x6, waiting for transfers between devices, exchange(): lax.ppermute(block, 'dom', partner_route(parts, r))  7.4 us
    ppermute x3, starting transfers between devices, spread_out(): return [lax.ppermute(pack, 'segment', route) for route in routes]  4.04 us
    ppermute x3, waiting for transfers between devices, spread_out(): return [lax.ppermute(pack, 'segment', route) for route in routes]  1.81 us
    ppermute x1, starting transfers between devices, per_device(): raw = lax.ppermute(raw, ('dom', 'chan'), route)  1.64 us
    ppermute x1, waiting for transfers between devices, per_device(): raw = lax.ppermute(raw, ('dom', 'chan'), route)  1.62 us
    ppermute x7, starting transfers between devices, swap(): return lax.ppermute(block, 'chan', [(0, 1), (1, 0)])  1.23 us
  transfers between devices with their start and end apart: 17, of which 8 were waited for; matrix products, arithmetic and copies ran while one was open for 0% of the time, Pallas kernels for 24%

profile of v5, /device:TPU:0, one launch (start us, length us, event | category | flops | bytes accessed | tf_op | source)
XLA Modules:
  0.0 41.0 jit_solution(5256768784415365943)
XLA Ops:
  0.0 1.3 %shard_map.136 = (bf16[288,256]{1,0:T(8,128)(2,1)S(1)}, bf16[384,256]{1,0:T(8,128)(2,1)S(1)}, bf16[384,256]{1,0:T(8,128)(2,1)S(1)}) custom-call(bf16[2,256,256]{2,1,0:T(8,128)(2,1)} %w_edge.1, bf16[2,512,128]{2,1,0:T(8,128)(2,1)} %w_in.1, bf16[2,128,256]{2,1,0:T(8,128)(2,1)} %w_out.1, bf16[2,256]{1,0:T(2,128)(2,1)} %e_bias.1, bf16[2,256]{1,0:T(2,128)(2,1)} %e_gain.1, ...), custom_call_target="tpu_custom_call" | custom-call | flops 1024 | bytes 65536 | tf_op jit(solution)/shard_map/pallas_call | solution.py:24
  1.3 3.0 %collective-permute-start = (bf16[288,256]{1,0:T(8,128)(2,1)S(1)}, bf16[288,256]{1,0:T(8,128)(2,1)S(1)}, u32[]{:S(2)}, u32[]{:S(2)}) collective-permute-start(bf16[288,256]{1,0:T(8,128)(2,1)S(1)} %get-tuple-element.45._.refs_0_.refs_4_.refs_7_), channel_id=1, source_target_pairs={{0,2},{2,0},{1,3},{3,1},{4,6},{6,4},{5,7},{7,5},{8,10},{10,8},{9,1... | collective-permute-start | bytes 442376 | tf_op jit(solution)/shard_map/ppermute | solution.py:348
  4.3 1.4 %shard_map.137 = (bf16[512,256]{1,0:T(8,128)(2,1)S(1)}, bf16[512,512]{1,0:T(8,128)(2,1)S(1)}, f32[512,128]{1,0:T(8,128)S(1)}, bf16[512,256]{1,0:T(8,128)(2,1)S(1)}, bf16[272,256]{1,0:T(8,128)(2,1)S(1)}) custom-call(bf16[2,512,256]{2,1,0:T(8,128)(2,1)} %latents.1, s32[2,2,128]{2,1,0:T(2,128)} %src.1, f32[2,2,128]{2,1,0:T(2,128)} %coef.2, s32[2,128]{1,0:T(2,128)} %recv.1, ...), custom_call_target="tpu_custom_call" | custom-call | flops 1024 | bytes 65536 | tf_op jit(solution)/shard_map/pallas_call | solution.py:24
  5.7 1.6 %collective-permute-start.2 = (bf16[272,256]{1,0:T(8,128)(2,1)S(1)}, bf16[272,256]{1,0:T(8,128)(2,1)S(1)}, u32[]{:S(2)}, u32[]{:S(2)}) collective-permute-start(bf16[272,256]{1,0:T(8,128)(2,1)S(1)} %get-tuple-element.46), channel_id=1, source_target_pairs={{0,4},{4,0},{8,12},{12,8},{1,9},{5,13},{9,1},{13,5},{2,6},{6,2},{1... | collective-permute-start | bytes 417800 | tf_op jit(solution)/shard_map/ppermute | solution.py:336
  7.3 0.5 %collective-permute-start.5 = (bf16[384,256]{1,0:T(8,128)(2,1)S(1)}, bf16[384,256]{1,0:T(8,128)(2,1)S(1)}, u32[]{:S(2)}, u32[]{:S(2)}) collective-permute-start(bf16[384,256]{1,0:T(8,128)(2,1)S(1)} %get-tuple-element.54.refs_0_), channel_id=1, source_target_pairs={{0,2},{2,0},{1,3},{3,1},{4,6},{6,4},{5,7},{7,5},{8,10},{10,8},{9,1... | collective-permute-start | bytes 589832 | tf_op jit(solution)/shard_map/ppermute | solution.py:348
  7.9 1.9 %shard_map.138 = (bf16[3072,512]{1,0:T(8,128)(2,1)S(1)}, f32[3072,128]{1,0:T(8,128)S(1)}) custom-call(s32[6,512]{1,0:T(8,128)} %neighbors.1, f32[6,512]{1,0:T(8,128)} %coef.3, bf16[512,256]{1,0:T(8,128)(2,1)S(1)} %get-tuple-element.44._.refs_6_), custom_call_target="tpu_custom_call" | custom-call | flops 1073741824 | bytes 65536 | tf_op jit(solution)/shard_map/pallas_call | solution.py:24
  9.8 1.6 %collective-permute-done.2.refs_4_ = bf16[272,256]{1,0:T(8,128)(2,1)S(1)} collective-permute-done((bf16[272,256]{1,0:T(8,128)(2,1)S(1)}, bf16[272,256]{1,0:T(8,128)(2,1)S(1)}, u32[]{:S(2)}, u32[]{:S(2)}) %collective-permute-start.2) | collective-permute-done | bytes 139296 | tf_op jit(solution)/shard_map/ppermute | solution.py:336
  11.6 0.3 collective-permute-start.1
  12.1 0.5 %collective-permute-start.10 = (bf16[384,256]{1,0:T(8,128)(2,1)S(1)}, bf16[384,256]{1,0:T(8,128)(2,1)S(1)}, u32[]{:S(2)}, u32[]{:S(2)}) collective-permute-start(bf16[384,256]{1,0:T(8,128)(2,1)S(1)} %get-tuple-element.65.refs_0_), channel_id=1, source_target_pairs={{0,2},{2,0},{1,3},{3,1},{4,6},{6,4},{5,7},{7,5},{8,10},{10,8},{9,1... | collective-permute-start | bytes 589832 | tf_op jit(solution)/shard_map/ppermute | solution.py:348
  12.6 1.8 %collective-permute-done.5.refs_7_.refs_1_ = bf16[384,256]{1,0:T(8,128)(2,1)S(1)} collective-permute-done((bf16[384,256]{1,0:T(8,128)(2,1)S(1)}, bf16[384,256]{1,0:T(8,128)(2,1)S(1)}, u32[]{:S(2)}, u32[]{:S(2)}) %collective-permute-start.5) | collective-permute-done | bytes 196640 | tf_op jit(solution)/shard_map/ppermute | solution.py:348
  14.4 0.5 %collective-permute-start.7 = (bf16[384,256]{1,0:T(8,128)(2,1)S(1)}, bf16[384,256]{1,0:T(8,128)(2,1)S(1)}, u32[]{:S(2)}, u32[]{:S(2)}) collective-permute-start(bf16[384,256]{1,0:T(8,128)(2,1)S(1)} %collective-permute-done.5.refs_7_.refs_1_), channel_id=1, source_target_pairs={{0,1},{1,0},{2,3},{3,2},{4,5},{5,4},{6,7},{7,6},{8,9},{9,8},{10,11... | collective-permute-start | bytes 589832 | tf_op jit(solution)/shard_map/ppermute | solution.py:302
  14.9 1.2 %shard_map.140.refs_3_ = f32[512,256]{1,0:T(8,128)S(1)} custom-call(bf16[288,256]{1,0:T(8,128)(2,1)S(1)} %get-tuple-element.45._.refs_0_.refs_4_.refs_7_, bf16[288,256]{1,0:T(8,128)(2,1)S(1)} %collective-permute-done.refs_1_.refs_5_.refs_8_, bf16[288,256]{1,0:T(8,128)(2,1)S(1)} %collective-permute-done.1.refs_2_.refs_6_.refs_9_, ...), custom_call_target="tpu_custom_call" | custom-call | flops 2147483648 | bytes 65536 | tf_op jit(solution)/shard_map/pallas_call | solution.py:24
  16.2 0.3 shard_map.139
  16.8 1.1 %shard_map.142 = (bf16[512,256]{1,0:T(8,128)(2,1)S(1)}, bf16[512,256]{1,0:T(8,128)(2,1)S(1)}, bf16[128,256]{1,0:T(8,128)(2,1)S(1)}, bf16[128,256]{1,0:T(8,128)(2,1)S(1)}) custom-call(bf16[128,256]{1,0:T(8,128)(2,1)S(1)} %get-tuple-element.49.refs_0_, bf16[128,256]{1,0:T(8,128)(2,1)S(1)} %get-tuple-element.50.refs_1_, ...), custom_call_target="tpu_custom_call" | custom-call | flops 1073741824 | bytes 65536 | tf_op jit(solution)/shard_map/pallas_call | solution.py:24
  17.9 0.8 %collective-permute-start.9 = (bf16[128,256]{1,0:T(8,128)(2,1)S(1)}, bf16[128,256]{1,0:T(8,128)(2,1)S(1)}, u32[]{:S(2)}, u32[]{:S(2)}) collective-permute-start(bf16[128,256]{1,0:T(8,128)(2,1)S(1)} %get-tuple-element.61), channel_id=1, source_target_pairs={{0,4},{4,0},{8,12},{12,8},{1,5},{5,1},{9,13},{13,9},{2,6},{6,2},{1... | collective-permute-start | bytes 196616 | tf_op jit(solution)/shard_map/ppermute | solution.py:305
  18.7 2.2 %collective-permute-start.8 = (bf16[128,256]{1,0:T(8,128)(2,1)S(1)}, bf16[128,256]{1,0:T(8,128)(2,1)S(1)}, u32[]{:S(2)}, u32[]{:S(2)}) collective-permute-start(bf16[128,256]{1,0:T(8,128)(2,1)S(1)} %get-tuple-element.60), channel_id=1, source_target_pairs={{0,8},{4,12},{8,0},{12,4},{1,9},{5,13},{9,1},{13,5},{2,10},{6,14},... | collective-permute-start | bytes 196616 | tf_op jit(solution)/shard_map/ppermute | solution.py:305
  20.9 1.3 %collective-permute-done.9.refs_1_ = bf16[128,256]{1,0:T(8,128)(2,1)S(1)} collective-permute-done((bf16[128,256]{1,0:T(8,128)(2,1)S(1)}, bf16[128,256]{1,0:T(8,128)(2,1)S(1)}, u32[]{:S(2)}, u32[]{:S(2)}) %collective-permute-start.9) | collective-permute-done | bytes 65568 | tf_op jit(solution)/shard_map/ppermute | solution.py:305
  22.2 1.0 %shard_map.143.refs_3_ = f32[512,256]{1,0:T(8,128)S(1)} custom-call(bf16[288,256]{1,0:T(8,128)(2,1)S(1)} %get-tuple-element.45._.refs_0_.refs_4_.refs_7_, bf16[288,256]{1,0:T(8,128)(2,1)S(1)} %collective-permute-done.refs_1_.refs_5_.refs_8_, bf16[288,256]{1,0:T(8,128)(2,1)S(1)} %collective-permute-done.1.refs_2_.refs_6_.refs_9_, ...), custom_call_target="tpu_custom_call" | custom-call | flops 2147483648 | bytes 65536 | tf_op jit(solution)/shard_map/pallas_call | solution.py:24
  23.2 0.4 %collective-permute-done.12.refs_3_ = bf16[384,256]{1,0:T(8,128)(2,1)S(1)} collective-permute-done((bf16[384,256]{1,0:T(8,128)(2,1)S(1)}, bf16[384,256]{1,0:T(8,128)(2,1)S(1)}, u32[]{:S(2)}, u32[]{:S(2)}) %collective-permute-start.12) | collective-permute-done | bytes 196640 | tf_op jit(solution)/shard_map/ppermute | solution.py:302
  23.9 1.6 %collective-permute-done.8.refs_0_ = bf16[128,256]{1,0:T(8,128)(2,1)S(1)} collective-permute-done((bf16[128,256]{1,0:T(8,128)(2,1)S(1)}, bf16[128,256]{1,0:T(8,128)(2,1)S(1)}, u32[]{:S(2)}, u32[]{:S(2)}) %collective-permute-start.8) | collective-permute-done | bytes 65568 | tf_op jit(solution)/shard_map/ppermute | solution.py:305
  25.5 1.1 %shard_map.145 = (bf16[512,256]{1,0:T(8,128)(2,1)S(1)}, bf16[512,256]{1,0:T(8,128)(2,1)S(1)}, bf16[128,256]{1,0:T(8,128)(2,1)S(1)}, bf16[128,256]{1,0:T(8,128)(2,1)S(1)}) custom-call(bf16[128,256]{1,0:T(8,128)(2,1)S(1)} %collective-permute-done.8.refs_0_, bf16[128,256]{1,0:T(8,128)(2,1)S(1)} %collective-permute-done.9.refs_1_, ...), custom_call_target="tpu_custom_call" | custom-call | flops 1073741824 | bytes 65536 | tf_op jit(solution)/shard_map/pallas_call | solution.py:24
  26.6 0.9 %collective-permute-start.13 = (bf16[128,256]{1,0:T(8,128)(2,1)S(1)}, bf16[128,256]{1,0:T(8,128)(2,1)S(1)}, u32[]{:S(2)}, u32[]{:S(2)}) collective-permute-start(bf16[128,256]{1,0:T(8,128)(2,1)S(1)} %get-tuple-element.69), channel_id=1, source_target_pairs={{0,8},{4,12},{8,0},{12,4},{1,9},{5,13},{9,1},{13,5},{2,10},{6,14},... | collective-permute-start | bytes 196616 | tf_op jit(solution)/shard_map/ppermute | solution.py:305
  27.6 1.5 %collective-permute-start.14 = (bf16[128,256]{1,0:T(8,128)(2,1)S(1)}, bf16[128,256]{1,0:T(8,128)(2,1)S(1)}, u32[]{:S(2)}, u32[]{:S(2)}) collective-permute-start(bf16[128,256]{1,0:T(8,128)(2,1)S(1)} %get-tuple-element.70), channel_id=1, source_target_pairs={{0,4},{4,0},{8,12},{12,8},{1,5},{5,1},{9,13},{13,9},{2,6},{6,2},{1... | collective-permute-start | bytes 196616 | tf_op jit(solution)/shard_map/ppermute | solution.py:305
  29.1 1.0 %shard_map.146.refs_3_ = f32[512,256]{1,0:T(8,128)S(1)} custom-call(bf16[288,256]{1,0:T(8,128)(2,1)S(1)} %get-tuple-element.45._.refs_0_.refs_4_.refs_7_, bf16[288,256]{1,0:T(8,128)(2,1)S(1)} %collective-permute-done.refs_1_.refs_5_.refs_8_, bf16[288,256]{1,0:T(8,128)(2,1)S(1)} %collective-permute-done.1.refs_2_.refs_6_.refs_9_, ...), custom_call_target="tpu_custom_call" | custom-call | flops 2147483648 | bytes 65536 | tf_op jit(solution)/shard_map/pallas_call | solution.py:24
  30.3 1.8 %collective-permute-done.13.refs_0_ = bf16[128,256]{1,0:T(8,128)(2,1)S(1)} collective-permute-done((bf16[128,256]{1,0:T(8,128)(2,1)S(1)}, bf16[128,256]{1,0:T(8,128)(2,1)S(1)}, u32[]{:S(2)}, u32[]{:S(2)}) %collective-permute-start.13) | collective-permute-done | bytes 65568 | tf_op jit(solution)/shard_map/ppermute | solution.py:305
  32.1 0.4 collective-permute-done.14.refs_1_
  32.5 1.1 %shard_map.148 = (bf16[512,256]{1,0:T(8,128)(2,1)S(1)}, bf16[512,256]{1,0:T(8,128)(2,1)S(1)}, bf16[128,256]{1,0:T(8,128)(2,1)S(1)}, bf16[128,256]{1,0:T(8,128)(2,1)S(1)}) custom-call(bf16[128,256]{1,0:T(8,128)(2,1)S(1)} %collective-permute-done.13.refs_0_, bf16[128,256]{1,0:T(8,128)(2,1)S(1)} %collective-permute-done.14.refs_1_, ...), custom_call_target="tpu_custom_call" | custom-call | flops 1073741824 | bytes 65536 | tf_op jit(solution)/shard_map/pallas_call | solution.py:24
  33.6 1.4 %collective-permute-start.15 = (bf16[128,256]{1,0:T(8,128)(2,1)S(1)}, bf16[128,256]{1,0:T(8,128)(2,1)S(1)}, u32[]{:S(2)}, u32[]{:S(2)}) collective-permute-start(bf16[128,256]{1,0:T(8,128)(2,1)S(1)} %get-tuple-element.75), channel_id=1, source_target_pairs={{0,8},{4,12},{8,0},{12,4},{1,9},{5,13},{9,1},{13,5},{2,10},{6,14},... | collective-permute-start | bytes 196616 | tf_op jit(solution)/shard_map/ppermute | solution.py:305
  35.0 1.0 %collective-permute-start.16 = (bf16[128,256]{1,0:T(8,128)(2,1)S(1)}, bf16[128,256]{1,0:T(8,128)(2,1)S(1)}, u32[]{:S(2)}, u32[]{:S(2)}) collective-permute-start(bf16[128,256]{1,0:T(8,128)(2,1)S(1)} %get-tuple-element.76), channel_id=1, source_target_pairs={{0,4},{4,0},{8,12},{12,8},{1,5},{5,1},{9,13},{13,9},{2,6},{6,2},{1... | collective-permute-start | bytes 196616 | tf_op jit(solution)/shard_map/ppermute | solution.py:305
  36.1 1.0 %shard_map.149.refs_3_ = f32[512,256]{1,0:T(8,128)S(1)} custom-call(bf16[288,256]{1,0:T(8,128)(2,1)S(1)} %get-tuple-element.45._.refs_0_.refs_4_.refs_7_, bf16[288,256]{1,0:T(8,128)(2,1)S(1)} %collective-permute-done.refs_1_.refs_5_.refs_8_, bf16[288,256]{1,0:T(8,128)(2,1)S(1)} %collective-permute-done.1.refs_2_.refs_6_.refs_9_, ...), custom_call_target="tpu_custom_call" | custom-call | flops 2147483648 | bytes 65536 | tf_op jit(solution)/shard_map/pallas_call | solution.py:24
  37.3 2.3 %collective-permute-done.15.refs_0_ = bf16[128,256]{1,0:T(8,128)(2,1)S(1)} collective-permute-done((bf16[128,256]{1,0:T(8,128)(2,1)S(1)}, bf16[128,256]{1,0:T(8,128)(2,1)S(1)}, u32[]{:S(2)}, u32[]{:S(2)}) %collective-permute-start.15) | collective-permute-done | bytes 65568 | tf_op jit(solution)/shard_map/ppermute | solution.py:305
  39.6 1.3 %shard_map.151 = bf16[1,512,256]{2,1,0:T(8,128)(2,1)} custom-call(bf16[128,256]{1,0:T(8,128)(2,1)S(1)} %collective-permute-done.15.refs_0_, bf16[128,256]{1,0:T(8,128)(2,1)S(1)} %collective-permute-done.16.refs_1_, bf16[512,256]{1,0:T(8,128)(2,1)S(1)} %get-tuple-element.77.refs_8_.refs_2_, f32[512,256]{1,0:T(8,128)S(1)} %shard_map.149.refs_3_, ...), custom_call_target="tpu_custom_call" | custom-call | flops 1073741824 | bytes 65536 | tf_op jit(solution)/shard_map/pallas_call | solution.py:24
  (18 shorter events, 1.4 us)
Async XLA Ops:
  1.3 10.2 %collective-permute-start = (bf16[288,256]{1,0:T(8,128)(2,1)S(1)}, bf16[288,256]{1,0:T(8,128)(2,1)S(1)}, u32[]{:S(2)}, u32[]{:S(2)}) collective-permute-start(bf16[288,256]{1,0:T(8,128)(2,1)S(1)} %get-tuple-element.45._.refs_0_.refs_4_.refs_7_), channel_id=1, source_target_pairs={{0,2},{2,0},{1,3},{3,1},{4,6},{6,4},{5,7},{7,5},{8,10},{10,8},{9,1... | collective-permute-start | bytes 442376 | tf_op jit(solution)/shard_map/ppermute | solution.py:348
  5.7 5.7 %collective-permute-start.2 = (bf16[272,256]{1,0:T(8,128)(2,1)S(1)}, bf16[272,256]{1,0:T(8,128)(2,1)S(1)}, u32[]{:S(2)}, u32[]{:S(2)}) collective-permute-start(bf16[272,256]{1,0:T(8,128)(2,1)S(1)} %get-tuple-element.46), channel_id=1, source_target_pairs={{0,4},{4,0},{8,12},{12,8},{1,9},{5,13},{9,1},{13,5},{2,6},{6,2},{1... | collective-permute-start | bytes 417800 | tf_op jit(solution)/shard_map/ppermute | solution.py:336
  7.3 7.1 %collective-permute-start.5 = (bf16[384,256]{1,0:T(8,128)(2,1)S(1)}, bf16[384,256]{1,0:T(8,128)(2,1)S(1)}, u32[]{:S(2)}, u32[]{:S(2)}) collective-permute-start(bf16[384,256]{1,0:T(8,128)(2,1)S(1)} %get-tuple-element.54.refs_0_), channel_id=1, source_target_pairs={{0,2},{2,0},{1,3},{3,1},{4,6},{6,4},{5,7},{7,5},{8,10},{10,8},{9,1... | collective-permute-start | bytes 589832 | tf_op jit(solution)/shard_map/ppermute | solution.py:348
  11.4 3.0 %collective-permute-start.3 = (bf16[288,256]{1,0:T(8,128)(2,1)S(1)}, bf16[288,256]{1,0:T(8,128)(2,1)S(1)}, u32[]{:S(2)}, u32[]{:S(2)}) collective-permute-start(bf16[288,256]{1,0:T(8,128)(2,1)S(1)} %collective-permute-done.refs_1_.refs_5_.refs_8_), channel_id=1, source_target_pairs={{0,1},{1,0},{2,3},{3,2},{4,5},{5,4},{6,7},{7,6},{8,9},{9,8},{10,11... | collective-permute-start | bytes 442376 | tf_op jit(solution)/shard_map/ppermute | solution.py:302
  11.6 3.3 %collective-permute-start.1 = (bf16[288,256]{1,0:T(8,128)(2,1)S(1)}, bf16[288,256]{1,0:T(8,128)(2,1)S(1)}, u32[]{:S(2)}, u32[]{:S(2)}) collective-permute-start(bf16[288,256]{1,0:T(8,128)(2,1)S(1)} %get-tuple-element.45._.refs_0_.refs_4_.refs_7_), channel_id=1, source_target_pairs={{0,1},{1,0},{2,3},{3,2},{4,5},{5,4},{6,7},{7,6},{8,9},{9,8},{10,11... | collective-permute-start | bytes 442376 | tf_op jit(solution)/shard_map/ppermute | solution.py:302
  11.9 4.6 %collective-permute-start.6 = (bf16[384,256]{1,0:T(8,128)(2,1)S(1)}, bf16[384,256]{1,0:T(8,128)(2,1)S(1)}, u32[]{:S(2)}, u32[]{:S(2)}) collective-permute-start(bf16[384,256]{1,0:T(8,128)(2,1)S(1)} %get-tuple-element.54.refs_0_), channel_id=1, source_target_pairs={{0,1},{1,0},{2,3},{3,2},{4,5},{5,4},{6,7},{7,6},{8,9},{9,8},{10,11... | collective-permute-start | bytes 589832 | tf_op jit(solution)/shard_map/ppermute | solution.py:302
  12.1 8.8 %collective-permute-start.10 = (bf16[384,256]{1,0:T(8,128)(2,1)S(1)}, bf16[384,256]{1,0:T(8,128)(2,1)S(1)}, u32[]{:S(2)}, u32[]{:S(2)}) collective-permute-start(bf16[384,256]{1,0:T(8,128)(2,1)S(1)} %get-tuple-element.65.refs_0_), channel_id=1, source_target_pairs={{0,2},{2,0},{1,3},{3,1},{4,6},{6,4},{5,7},{7,5},{8,10},{10,8},{9,1... | collective-permute-start | bytes 589832 | tf_op jit(solution)/shard_map/ppermute | solution.py:348
  14.4 1.7 %collective-permute-start.4 = (bf16[272,256]{1,0:T(8,128)(2,1)S(1)}, bf16[272,256]{1,0:T(8,128)(2,1)S(1)}, u32[]{:S(2)}, u32[]{:S(2)}) collective-permute-start(bf16[272,256]{1,0:T(8,128)(2,1)S(1)} %collective-permute-done.2.refs_4_), channel_id=1, source_target_pairs={{0,1},{1,0},{2,3},{3,2},{4,5},{5,4},{6,7},{7,6},{8,9},{9,8},{10,11... | collective-permute-start | bytes 417800 | tf_op jit(solution)/shard_map/ppermute | solution.py:302
  14.4 2.1 %collective-permute-start.7 = (bf16[384,256]{1,0:T(8,128)(2,1)S(1)}, bf16[384,256]{1,0:T(8,128)(2,1)S(1)}, u32[]{:S(2)}, u32[]{:S(2)}) collective-permute-start(bf16[384,256]{1,0:T(8,128)(2,1)S(1)} %collective-permute-done.5.refs_7_.refs_1_), channel_id=1, source_target_pairs={{0,1},{1,0},{2,3},{3,2},{4,5},{5,4},{6,7},{7,6},{8,9},{9,8},{10,11... | collective-permute-start | bytes 589832 | tf_op jit(solution)/shard_map/ppermute | solution.py:302
  17.9 4.3 %collective-permute-start.9 = (bf16[128,256]{1,0:T(8,128)(2,1)S(1)}, bf16[128,256]{1,0:T(8,128)(2,1)S(1)}, u32[]{:S(2)}, u32[]{:S(2)}) collective-permute-start(bf16[128,256]{1,0:T(8,128)(2,1)S(1)} %get-tuple-element.61), channel_id=1, source_target_pairs={{0,4},{4,0},{8,12},{12,8},{1,5},{5,1},{9,13},{13,9},{2,6},{6,2},{1... | collective-permute-start | bytes 196616 | tf_op jit(solution)/shard_map/ppermute | solution.py:305
  18.7 4.5 %collective-permute-start.11 = (bf16[384,256]{1,0:T(8,128)(2,1)S(1)}, bf16[384,256]{1,0:T(8,128)(2,1)S(1)}, u32[]{:S(2)}, u32[]{:S(2)}) collective-permute-start(bf16[384,256]{1,0:T(8,128)(2,1)S(1)} %get-tuple-element.65.refs_0_), channel_id=1, source_target_pairs={{0,1},{1,0},{2,3},{3,2},{4,5},{5,4},{6,7},{7,6},{8,9},{9,8},{10,11... | collective-permute-start | bytes 589832 | tf_op jit(solution)/shard_map/ppermute | solution.py:302
  18.7 6.8 %collective-permute-start.8 = (bf16[128,256]{1,0:T(8,128)(2,1)S(1)}, bf16[128,256]{1,0:T(8,128)(2,1)S(1)}, u32[]{:S(2)}, u32[]{:S(2)}) collective-permute-start(bf16[128,256]{1,0:T(8,128)(2,1)S(1)} %get-tuple-element.60), channel_id=1, source_target_pairs={{0,8},{4,12},{8,0},{12,4},{1,9},{5,13},{9,1},{13,5},{2,10},{6,14},... | collective-permute-start | bytes 196616 | tf_op jit(solution)/shard_map/ppermute | solution.py:305
  22.2 1.4 %collective-permute-start.12 = (bf16[384,256]{1,0:T(8,128)(2,1)S(1)}, bf16[384,256]{1,0:T(8,128)(2,1)S(1)}, u32[]{:S(2)}, u32[]{:S(2)}) collective-permute-start(bf16[384,256]{1,0:T(8,128)(2,1)S(1)} %collective-permute-done.10.refs_1_), channel_id=1, source_target_pairs={{0,1},{1,0},{2,3},{3,2},{4,5},{5,4},{6,7},{7,6},{8,9},{9,8},{10,11... | collective-permute-start | bytes 589832 | tf_op jit(solution)/shard_map/ppermute | solution.py:302
  26.6 5.5 %collective-permute-start.13 = (bf16[128,256]{1,0:T(8,128)(2,1)S(1)}, bf16[128,256]{1,0:T(8,128)(2,1)S(1)}, u32[]{:S(2)}, u32[]{:S(2)}) collective-permute-start(bf16[128,256]{1,0:T(8,128)(2,1)S(1)} %get-tuple-element.69), channel_id=1, source_target_pairs={{0,8},{4,12},{8,0},{12,4},{1,9},{5,13},{9,1},{13,5},{2,10},{6,14},... | collective-permute-start | bytes 196616 | tf_op jit(solution)/shard_map/ppermute | solution.py:305
  27.6 5.0 %collective-permute-start.14 = (bf16[128,256]{1,0:T(8,128)(2,1)S(1)}, bf16[128,256]{1,0:T(8,128)(2,1)S(1)}, u32[]{:S(2)}, u32[]{:S(2)}) collective-permute-start(bf16[128,256]{1,0:T(8,128)(2,1)S(1)} %get-tuple-element.70), channel_id=1, source_target_pairs={{0,4},{4,0},{8,12},{12,8},{1,5},{5,1},{9,13},{13,9},{2,6},{6,2},{1... | collective-permute-start | bytes 196616 | tf_op jit(solution)/shard_map/ppermute | solution.py:305
  33.6 6.0 %collective-permute-start.15 = (bf16[128,256]{1,0:T(8,128)(2,1)S(1)}, bf16[128,256]{1,0:T(8,128)(2,1)S(1)}, u32[]{:S(2)}, u32[]{:S(2)}) collective-permute-start(bf16[128,256]{1,0:T(8,128)(2,1)S(1)} %get-tuple-element.75), channel_id=1, source_target_pairs={{0,8},{4,12},{8,0},{12,4},{1,9},{5,13},{9,1},{13,5},{2,10},{6,14},... | collective-permute-start | bytes 196616 | tf_op jit(solution)/shard_map/ppermute | solution.py:305
  35.0 4.6 %collective-permute-start.16 = (bf16[128,256]{1,0:T(8,128)(2,1)S(1)}, bf16[128,256]{1,0:T(8,128)(2,1)S(1)}, u32[]{:S(2)}, u32[]{:S(2)}) collective-permute-start(bf16[128,256]{1,0:T(8,128)(2,1)S(1)} %get-tuple-element.76), channel_id=1, source_target_pairs={{0,4},{4,0},{8,12},{12,8},{1,5},{5,1},{9,13},{13,9},{2,6},{6,2},{1... | collective-permute-start | bytes 196616 | tf_op jit(solution)/shard_map/ppermute | solution.py:305

commit v6 on v5

--- a/solution.py
+++ b/solution.py
@@ -353,9 +353,22 @@
     def swaps(own, received, made):
         return [own, *received, swap(once(own, scatter)), *map(swap, once(received, made))]
 
+    def crossed(pack):
+        return [
+            lax.ppermute(
+                pack,
+                ("segment", "chan"),
+                [(a * cores + core, b * cores + 1 - core) for a, b in route for core in range(cores)],
+            )
+            for route in routes
+        ]
+
     weights = swaps(edge_pack, edges_mine, (raw, hot))
     node_weights = [None] * held
     node_weights[0] = swaps(node_packs[0], nodes_mine[0], weights[-1])
+    for j in range(1, held):
+        pack = once(node_packs[j], scatter)
+        node_weights[j] = [node_packs[j], *nodes_mine[j], swap(pack), *crossed(pack)]
     total = segments * held
     sends = [shape((nodes, width), BF16)] + [shape((slots, width), BF16)] * rounds
     source = latent
@@ -377,8 +390,6 @@
             )
         else:
             arrived = exchange(blocks)
-        if 0 < layer < held:
-            node_weights[j] = swaps(node_packs[j], nodes_mine[j], arrived[0])
         before, chosen = kernel_call(
             functools.partial(weights_kernel, segments, segment, j),
             [shape((nodes, width), F32), shape((2 * width + VECTORS, width), BF16)],

time: 41.2 us -> 41 us (level)
  waiting for transfers between devices: 11.3 us -> 7.65 us
  starting transfers between devices: 14.9 us -> 18.2 us
    ppermute x6, waiting for transfers between devices: 7.4 us -> 4.16 us  [exchange(): lax.ppermute(block, 'dom', partner_route(parts, r))]
    ppermute x6, starting transfers between devices: 7.96 us -> 10.8 us  [exchange(): lax.ppermute(block, 'dom', partner_route(parts, r))]
    ppermute x0 -> x1, starting transfers between devices: none -> 0.45 us  [crossed(): lax.ppermute(pack, ('segment', 'chan'), [(a * cores + core, b * cores + 1...]
    ppermute x7 -> x6, waiting for transfers between devices: 0.45 us -> 0.02 us  [swap(): return lax.ppermute(block, 'chan', [(0, 1), (1, 0)])]
    ppermute x7 -> x6, starting transfers between devices: 1.23 us -> 1.22 us  [swap(): return lax.ppermute(block, 'chan', [(0, 1), (1, 0)])]
where the time goes in v6:
time: 41 us; the launch traced here: 40.7 us
  starting transfers between devices  18.2 us (44%)
  Pallas kernels  14.6 us (36%)
  waiting for transfers between devices  7.65 us (19%)
    pallas_call x16, Pallas kernels, kernel_call(): pl.pallas_call(body, out_shape=outs, in_specs=[HBM if scratch else VMEM]...  14.6 us
    ppermute x6, starting transfers between devices, exchange(): lax.ppermute(block, 'dom', partner_route(parts, r))  10.8 us
    ppermute x6, waiting for transfers between devices, exchange(): lax.ppermute(block, 'dom', partner_route(parts, r))  4.16 us
    ppermute x3, starting transfers between devices, spread_out(): return [lax.ppermute(pack, 'segment', route) for route in routes]  4.08 us
    ppermute x3, waiting for transfers between devices, spread_out(): return [lax.ppermute(pack, 'segment', route) for route in routes]  1.86 us
    ppermute x1, starting transfers between devices, per_device(): raw = lax.ppermute(raw, ('dom', 'chan'), route)  1.64 us
    ppermute x1, waiting for transfers between devices, per_device(): raw = lax.ppermute(raw, ('dom', 'chan'), route)  1.62 us
    ppermute x6, starting transfers between devices, swap(): return lax.ppermute(block, 'chan', [(0, 1), (1, 0)])  1.22 us
  transfers between devices with their start and end apart: 17, of which 8 were waited for; matrix products, arithmetic and copies ran while one was open for 0% of the time, Pallas kernels for 24%

profile of v6, /device:TPU:0, one launch (start us, length us, event | category | flops | bytes accessed | tf_op | source)
XLA Modules:
  0.0 40.7 jit_solution(9554142605710865861)
XLA Ops:
  0.0 1.3 %shard_map.136 = (bf16[288,256]{1,0:T(8,128)(2,1)S(1)}, bf16[384,256]{1,0:T(8,128)(2,1)S(1)}, bf16[384,256]{1,0:T(8,128)(2,1)S(1)}) custom-call(bf16[2,256,256]{2,1,0:T(8,128)(2,1)} %w_edge.1, bf16[2,512,128]{2,1,0:T(8,128)(2,1)} %w_in.1, bf16[2,128,256]{2,1,0:T(8,128)(2,1)} %w_out.1, bf16[2,256]{1,0:T(2,128)(2,1)} %e_bias.1, bf16[2,256]{1,0:T(2,128)(2,1)} %e_gain.1, ...), custom_call_target="tpu_custom_call" | custom-call | flops 1024 | bytes 65536 | tf_op jit(solution)/shard_map/pallas_call | solution.py:24
  1.3 3.0 %collective-permute-start = (bf16[288,256]{1,0:T(8,128)(2,1)S(1)}, bf16[288,256]{1,0:T(8,128)(2,1)S(1)}, u32[]{:S(2)}, u32[]{:S(2)}) collective-permute-start(bf16[288,256]{1,0:T(8,128)(2,1)S(1)} %get-tuple-element.44._.refs_0_.refs_4_.refs_7_), channel_id=1, source_target_pairs={{0,2},{2,0},{1,3},{3,1},{4,6},{6,4},{5,7},{7,5},{8,10},{10,8},{9,1... | collective-permute-start | bytes 442376 | tf_op jit(solution)/shard_map/ppermute | solution.py:348
  4.3 1.4 %shard_map.137 = (bf16[512,256]{1,0:T(8,128)(2,1)S(1)}, bf16[512,512]{1,0:T(8,128)(2,1)S(1)}, f32[512,128]{1,0:T(8,128)S(1)}, bf16[512,256]{1,0:T(8,128)(2,1)S(1)}, bf16[272,256]{1,0:T(8,128)(2,1)S(1)}) custom-call(bf16[2,512,256]{2,1,0:T(8,128)(2,1)} %latents.1, s32[2,2,128]{2,1,0:T(2,128)} %src.1, f32[2,2,128]{2,1,0:T(2,128)} %coef.2, s32[2,128]{1,0:T(2,128)} %recv.1, ...), custom_call_target="tpu_custom_call" | custom-call | flops 1024 | bytes 65536 | tf_op jit(solution)/shard_map/pallas_call | solution.py:24
  5.7 1.6 %collective-permute-start.2 = (bf16[272,256]{1,0:T(8,128)(2,1)S(1)}, bf16[272,256]{1,0:T(8,128)(2,1)S(1)}, u32[]{:S(2)}, u32[]{:S(2)}) collective-permute-start(bf16[272,256]{1,0:T(8,128)(2,1)S(1)} %get-tuple-element.45), channel_id=1, source_target_pairs={{0,4},{4,0},{8,12},{12,8},{1,9},{5,13},{9,1},{13,5},{2,6},{6,2},{1... | collective-permute-start | bytes 417800 | tf_op jit(solution)/shard_map/ppermute | solution.py:336
  7.3 0.5 %collective-permute-start.5 = (bf16[384,256]{1,0:T(8,128)(2,1)S(1)}, bf16[384,256]{1,0:T(8,128)(2,1)S(1)}, u32[]{:S(2)}, u32[]{:S(2)}) collective-permute-start(bf16[384,256]{1,0:T(8,128)(2,1)S(1)} %get-tuple-element.53.refs_0_), channel_id=1, source_target_pairs={{0,2},{2,0},{1,3},{3,1},{4,6},{6,4},{5,7},{7,5},{8,10},{10,8},{9,1... | collective-permute-start | bytes 589832 | tf_op jit(solution)/shard_map/ppermute | solution.py:348
  7.9 1.9 %shard_map.138 = (bf16[3072,512]{1,0:T(8,128)(2,1)S(1)}, f32[3072,128]{1,0:T(8,128)S(1)}) custom-call(s32[6,512]{1,0:T(8,128)} %neighbors.1, f32[6,512]{1,0:T(8,128)} %coef.3, bf16[512,256]{1,0:T(8,128)(2,1)S(1)} %get-tuple-element.43._.refs_6_), custom_call_target="tpu_custom_call" | custom-call | flops 1073741824 | bytes 65536 | tf_op jit(solution)/shard_map/pallas_call | solution.py:24
  9.8 1.6 %collective-permute-done.2.refs_4_ = bf16[272,256]{1,0:T(8,128)(2,1)S(1)} collective-permute-done((bf16[272,256]{1,0:T(8,128)(2,1)S(1)}, bf16[272,256]{1,0:T(8,128)(2,1)S(1)}, u32[]{:S(2)}, u32[]{:S(2)}) %collective-permute-start.2) | collective-permute-done | bytes 139296 | tf_op jit(solution)/shard_map/ppermute | solution.py:336
  11.6 0.3 collective-permute-start.1
  12.1 0.5 %collective-permute-start.12 = (bf16[384,256]{1,0:T(8,128)(2,1)S(1)}, bf16[384,256]{1,0:T(8,128)(2,1)S(1)}, u32[]{:S(2)}, u32[]{:S(2)}) collective-permute-start(bf16[384,256]{1,0:T(8,128)(2,1)S(1)} %get-tuple-element.64.refs_0_), channel_id=1, source_target_pairs={{0,3},{1,2},{2,1},{3,0},{4,7},{5,6},{6,5},{7,4},{8,11},{9,10},{10,... | collective-permute-start | bytes 589832 | tf_op jit(solution)/shard_map/ppermute | solution.py:358
  12.6 1.9 %collective-permute-done.5.refs_7_.refs_1_ = bf16[384,256]{1,0:T(8,128)(2,1)S(1)} collective-permute-done((bf16[384,256]{1,0:T(8,128)(2,1)S(1)}, bf16[384,256]{1,0:T(8,128)(2,1)S(1)}, u32[]{:S(2)}, u32[]{:S(2)}) %collective-permute-start.5) | collective-permute-done | bytes 196640 | tf_op jit(solution)/shard_map/ppermute | solution.py:348
  14.4 0.5 %collective-permute-start.10 = (bf16[384,256]{1,0:T(8,128)(2,1)S(1)}, bf16[384,256]{1,0:T(8,128)(2,1)S(1)}, u32[]{:S(2)}, u32[]{:S(2)}) collective-permute-start(bf16[384,256]{1,0:T(8,128)(2,1)S(1)} %get-tuple-element.64.refs_0_), channel_id=1, source_target_pairs={{0,2},{2,0},{1,3},{3,1},{4,6},{6,4},{5,7},{7,5},{8,10},{10,8},{9,1... | collective-permute-start | bytes 589832 | tf_op jit(solution)/shard_map/ppermute | solution.py:348
  15.2 0.3 collective-permute-start.7
  15.5 0.3 shard_map.139
  15.8 1.2 %shard_map.140.refs_3_ = f32[512,256]{1,0:T(8,128)S(1)} custom-call(bf16[288,256]{1,0:T(8,128)(2,1)S(1)} %get-tuple-element.44._.refs_0_.refs_4_.refs_7_, bf16[288,256]{1,0:T(8,128)(2,1)S(1)} %collective-permute-done.refs_1_.refs_5_.refs_8_, bf16[288,256]{1,0:T(8,128)(2,1)S(1)} %collective-permute-done.1.refs_2_.refs_6_.refs_9_, ...), custom_call_target="tpu_custom_call" | custom-call | flops 2147483648 | bytes 65536 | tf_op jit(solution)/shard_map/pallas_call | solution.py:24
  17.3 1.1 %shard_map.142 = (bf16[512,256]{1,0:T(8,128)(2,1)S(1)}, bf16[512,256]{1,0:T(8,128)(2,1)S(1)}, bf16[128,256]{1,0:T(8,128)(2,1)S(1)}, bf16[128,256]{1,0:T(8,128)(2,1)S(1)}) custom-call(bf16[128,256]{1,0:T(8,128)(2,1)S(1)} %get-tuple-element.48.refs_0_, bf16[128,256]{1,0:T(8,128)(2,1)S(1)} %get-tuple-element.49.refs_1_, ...), custom_call_target="tpu_custom_call" | custom-call | flops 1073741824 | bytes 65536 | tf_op jit(solution)/shard_map/pallas_call | solution.py:24
  18.4 1.8 %collective-permute-start.8 = (bf16[128,256]{1,0:T(8,128)(2,1)S(1)}, bf16[128,256]{1,0:T(8,128)(2,1)S(1)}, u32[]{:S(2)}, u32[]{:S(2)}) collective-permute-start(bf16[128,256]{1,0:T(8,128)(2,1)S(1)} %get-tuple-element.59), channel_id=1, source_target_pairs={{0,8},{4,12},{8,0},{12,4},{1,9},{5,13},{9,1},{13,5},{2,10},{6,14},... | collective-permute-start | bytes 196616 | tf_op jit(solution)/shard_map/ppermute | solution.py:305
  20.2 2.4 %collective-permute-start.9 = (bf16[128,256]{1,0:T(8,128)(2,1)S(1)}, bf16[128,256]{1,0:T(8,128)(2,1)S(1)}, u32[]{:S(2)}, u32[]{:S(2)}) collective-permute-start(bf16[128,256]{1,0:T(8,128)(2,1)S(1)} %get-tuple-element.60), channel_id=1, source_target_pairs={{0,4},{4,0},{8,12},{12,8},{1,5},{5,1},{9,13},{13,9},{2,6},{6,2},{1... | collective-permute-start | bytes 196616 | tf_op jit(solution)/shard_map/ppermute | solution.py:305
  22.5 1.0 %shard_map.143.refs_3_ = f32[512,256]{1,0:T(8,128)S(1)} custom-call(bf16[288,256]{1,0:T(8,128)(2,1)S(1)} %get-tuple-element.44._.refs_0_.refs_4_.refs_7_, bf16[288,256]{1,0:T(8,128)(2,1)S(1)} %collective-permute-done.refs_1_.refs_5_.refs_8_, bf16[288,256]{1,0:T(8,128)(2,1)S(1)} %collective-permute-done.1.refs_2_.refs_6_.refs_9_, ...), custom_call_target="tpu_custom_call" | custom-call | flops 2147483648 | bytes 65536 | tf_op jit(solution)/shard_map/pallas_call | solution.py:24
  23.8 1.3 %collective-permute-done.8.refs_0_ = bf16[128,256]{1,0:T(8,128)(2,1)S(1)} collective-permute-done((bf16[128,256]{1,0:T(8,128)(2,1)S(1)}, bf16[128,256]{1,0:T(8,128)(2,1)S(1)}, u32[]{:S(2)}, u32[]{:S(2)}) %collective-permute-start.8) | collective-permute-done | bytes 65568 | tf_op jit(solution)/shard_map/ppermute | solution.py:305
  25.3 1.1 %shard_map.145 = (bf16[512,256]{1,0:T(8,128)(2,1)S(1)}, bf16[512,256]{1,0:T(8,128)(2,1)S(1)}, bf16[128,256]{1,0:T(8,128)(2,1)S(1)}, bf16[128,256]{1,0:T(8,128)(2,1)S(1)}) custom-call(bf16[128,256]{1,0:T(8,128)(2,1)S(1)} %collective-permute-done.8.refs_0_, bf16[128,256]{1,0:T(8,128)(2,1)S(1)} %collective-permute-done.9.refs_1_, ...), custom_call_target="tpu_custom_call" | custom-call | flops 1073741824 | bytes 65536 | tf_op jit(solution)/shard_map/pallas_call | solution.py:24
  26.4 1.1 %collective-permute-start.13 = (bf16[128,256]{1,0:T(8,128)(2,1)S(1)}, bf16[128,256]{1,0:T(8,128)(2,1)S(1)}, u32[]{:S(2)}, u32[]{:S(2)}) collective-permute-start(bf16[128,256]{1,0:T(8,128)(2,1)S(1)} %get-tuple-element.67), channel_id=1, source_target_pairs={{0,8},{4,12},{8,0},{12,4},{1,9},{5,13},{9,1},{13,5},{2,10},{6,14},... | collective-permute-start | bytes 196616 | tf_op jit(solution)/shard_map/ppermute | solution.py:305
  27.5 2.2 %collective-permute-start.14 = (bf16[128,256]{1,0:T(8,128)(2,1)S(1)}, bf16[128,256]{1,0:T(8,128)(2,1)S(1)}, u32[]{:S(2)}, u32[]{:S(2)}) collective-permute-start(bf16[128,256]{1,0:T(8,128)(2,1)S(1)} %get-tuple-element.68), channel_id=1, source_target_pairs={{0,4},{4,0},{8,12},{12,8},{1,5},{5,1},{9,13},{13,9},{2,6},{6,2},{1... | collective-permute-start | bytes 196616 | tf_op jit(solution)/shard_map/ppermute | solution.py:305
  29.7 1.0 %shard_map.146.refs_3_ = f32[512,256]{1,0:T(8,128)S(1)} custom-call(bf16[288,256]{1,0:T(8,128)(2,1)S(1)} %get-tuple-element.44._.refs_0_.refs_4_.refs_7_, bf16[288,256]{1,0:T(8,128)(2,1)S(1)} %collective-permute-done.refs_1_.refs_5_.refs_8_, bf16[288,256]{1,0:T(8,128)(2,1)S(1)} %collective-permute-done.1.refs_2_.refs_6_.refs_9_, ...), custom_call_target="tpu_custom_call" | custom-call | flops 2147483648 | bytes 65536 | tf_op jit(solution)/shard_map/pallas_call | solution.py:24
  30.9 0.7 %collective-permute-done.13.refs_0_ = bf16[128,256]{1,0:T(8,128)(2,1)S(1)} collective-permute-done((bf16[128,256]{1,0:T(8,128)(2,1)S(1)}, bf16[128,256]{1,0:T(8,128)(2,1)S(1)}, u32[]{:S(2)}, u32[]{:S(2)}) %collective-permute-start.13) | collective-permute-done | bytes 65568 | tf_op jit(solution)/shard_map/ppermute | solution.py:305
  31.7 0.7 %collective-permute-done.14.refs_1_ = bf16[128,256]{1,0:T(8,128)(2,1)S(1)} collective-permute-done((bf16[128,256]{1,0:T(8,128)(2,1)S(1)}, bf16[128,256]{1,0:T(8,128)(2,1)S(1)}, u32[]{:S(2)}, u32[]{:S(2)}) %collective-permute-start.14) | collective-permute-done | bytes 65568 | tf_op jit(solution)/shard_map/ppermute | solution.py:305
  32.3 1.1 %shard_map.148 = (bf16[512,256]{1,0:T(8,128)(2,1)S(1)}, bf16[512,256]{1,0:T(8,128)(2,1)S(1)}, bf16[128,256]{1,0:T(8,128)(2,1)S(1)}, bf16[128,256]{1,0:T(8,128)(2,1)S(1)}) custom-call(bf16[128,256]{1,0:T(8,128)(2,1)S(1)} %collective-permute-done.13.refs_0_, bf16[128,256]{1,0:T(8,128)(2,1)S(1)} %collective-permute-done.14.refs_1_, ...), custom_call_target="tpu_custom_call" | custom-call | flops 1073741824 | bytes 65536 | tf_op jit(solution)/shard_map/pallas_call | solution.py:24
  33.4 1.6 %collective-permute-start.15 = (bf16[128,256]{1,0:T(8,128)(2,1)S(1)}, bf16[128,256]{1,0:T(8,128)(2,1)S(1)}, u32[]{:S(2)}, u32[]{:S(2)}) collective-permute-start(bf16[128,256]{1,0:T(8,128)(2,1)S(1)} %get-tuple-element.73), channel_id=1, source_target_pairs={{0,8},{4,12},{8,0},{12,4},{1,9},{5,13},{9,1},{13,5},{2,10},{6,14},... | collective-permute-start | bytes 196616 | tf_op jit(solution)/shard_map/ppermute | solution.py:305
  35.0 1.8 %collective-permute-start.16 = (bf16[128,256]{1,0:T(8,128)(2,1)S(1)}, bf16[128,256]{1,0:T(8,128)(2,1)S(1)}, u32[]{:S(2)}, u32[]{:S(2)}) collective-permute-start(bf16[128,256]{1,0:T(8,128)(2,1)S(1)} %get-tuple-element.74), channel_id=1, source_target_pairs={{0,4},{4,0},{8,12},{12,8},{1,5},{5,1},{9,13},{13,9},{2,6},{6,2},{1... | collective-permute-start | bytes 196616 | tf_op jit(solution)/shard_map/ppermute | solution.py:305
  36.8 1.0 %shard_map.149.refs_3_ = f32[512,256]{1,0:T(8,128)S(1)} custom-call(bf16[288,256]{1,0:T(8,128)(2,1)S(1)} %get-tuple-element.44._.refs_0_.refs_4_.refs_7_, bf16[288,256]{1,0:T(8,128)(2,1)S(1)} %collective-permute-done.refs_1_.refs_5_.refs_8_, bf16[288,256]{1,0:T(8,128)(2,1)S(1)} %collective-permute-done.1.refs_2_.refs_6_.refs_9_, ...), custom_call_target="tpu_custom_call" | custom-call | flops 2147483648 | bytes 65536 | tf_op jit(solution)/shard_map/pallas_call | solution.py:24
  38.1 0.6 %collective-permute-done.15.refs_0_ = bf16[128,256]{1,0:T(8,128)(2,1)S(1)} collective-permute-done((bf16[128,256]{1,0:T(8,128)(2,1)S(1)}, bf16[128,256]{1,0:T(8,128)(2,1)S(1)}, u32[]{:S(2)}, u32[]{:S(2)}) %collective-permute-start.15) | collective-permute-done | bytes 65568 | tf_op jit(solution)/shard_map/ppermute | solution.py:305
  38.7 0.7 %collective-permute-done.16.refs_1_ = bf16[128,256]{1,0:T(8,128)(2,1)S(1)} collective-permute-done((bf16[128,256]{1,0:T(8,128)(2,1)S(1)}, bf16[128,256]{1,0:T(8,128)(2,1)S(1)}, u32[]{:S(2)}, u32[]{:S(2)}) %collective-permute-start.16) | collective-permute-done | bytes 65568 | tf_op jit(solution)/shard_map/ppermute | solution.py:305
  39.4 1.3 %shard_map.151 = bf16[1,512,256]{2,1,0:T(8,128)(2,1)} custom-call(bf16[128,256]{1,0:T(8,128)(2,1)S(1)} %collective-permute-done.15.refs_0_, bf16[128,256]{1,0:T(8,128)(2,1)S(1)} %collective-permute-done.16.refs_1_, bf16[512,256]{1,0:T(8,128)(2,1)S(1)} %get-tuple-element.75.refs_8_.refs_2_, f32[512,256]{1,0:T(8,128)S(1)} %shard_map.149.refs_3_, ...), custom_call_target="tpu_custom_call" | custom-call | flops 1073741824 | bytes 65536 | tf_op jit(solution)/shard_map/pallas_call | solution.py:24
  (18 shorter events, 1.8 us)
Async XLA Ops:
  1.3 10.2 %collective-permute-start = (bf16[288,256]{1,0:T(8,128)(2,1)S(1)}, bf16[288,256]{1,0:T(8,128)(2,1)S(1)}, u32[]{:S(2)}, u32[]{:S(2)}) collective-permute-start(bf16[288,256]{1,0:T(8,128)(2,1)S(1)} %get-tuple-element.44._.refs_0_.refs_4_.refs_7_), channel_id=1, source_target_pairs={{0,2},{2,0},{1,3},{3,1},{4,6},{6,4},{5,7},{7,5},{8,10},{10,8},{9,1... | collective-permute-start | bytes 442376 | tf_op jit(solution)/shard_map/ppermute | solution.py:348
  5.7 5.7 %collective-permute-start.2 = (bf16[272,256]{1,0:T(8,128)(2,1)S(1)}, bf16[272,256]{1,0:T(8,128)(2,1)S(1)}, u32[]{:S(2)}, u32[]{:S(2)}) collective-permute-start(bf16[272,256]{1,0:T(8,128)(2,1)S(1)} %get-tuple-element.45), channel_id=1, source_target_pairs={{0,4},{4,0},{8,12},{12,8},{1,9},{5,13},{9,1},{13,5},{2,6},{6,2},{1... | collective-permute-start | bytes 417800 | tf_op jit(solution)/shard_map/ppermute | solution.py:336
  7.3 7.1 %collective-permute-start.5 = (bf16[384,256]{1,0:T(8,128)(2,1)S(1)}, bf16[384,256]{1,0:T(8,128)(2,1)S(1)}, u32[]{:S(2)}, u32[]{:S(2)}) collective-permute-start(bf16[384,256]{1,0:T(8,128)(2,1)S(1)} %get-tuple-element.53.refs_0_), channel_id=1, source_target_pairs={{0,2},{2,0},{1,3},{3,1},{4,6},{6,4},{5,7},{7,5},{8,10},{10,8},{9,1... | collective-permute-start | bytes 589832 | tf_op jit(solution)/shard_map/ppermute | solution.py:348
  11.4 3.0 %collective-permute-start.3 = (bf16[288,256]{1,0:T(8,128)(2,1)S(1)}, bf16[288,256]{1,0:T(8,128)(2,1)S(1)}, u32[]{:S(2)}, u32[]{:S(2)}) collective-permute-start(bf16[288,256]{1,0:T(8,128)(2,1)S(1)} %collective-permute-done.refs_1_.refs_5_.refs_8_), channel_id=1, source_target_pairs={{0,1},{1,0},{2,3},{3,2},{4,5},{5,4},{6,7},{7,6},{8,9},{9,8},{10,11... | collective-permute-start | bytes 442376 | tf_op jit(solution)/shard_map/ppermute | solution.py:302
  11.6 3.4 %collective-permute-start.1 = (bf16[288,256]{1,0:T(8,128)(2,1)S(1)}, bf16[288,256]{1,0:T(8,128)(2,1)S(1)}, u32[]{:S(2)}, u32[]{:S(2)}) collective-permute-start(bf16[288,256]{1,0:T(8,128)(2,1)S(1)} %get-tuple-element.44._.refs_0_.refs_4_.refs_7_), channel_id=1, source_target_pairs={{0,1},{1,0},{2,3},{3,2},{4,5},{5,4},{6,7},{7,6},{8,9},{9,8},{10,11... | collective-permute-start | bytes 442376 | tf_op jit(solution)/shard_map/ppermute | solution.py:302
  11.9 3.3 %collective-permute-start.4 = (bf16[272,256]{1,0:T(8,128)(2,1)S(1)}, bf16[272,256]{1,0:T(8,128)(2,1)S(1)}, u32[]{:S(2)}, u32[]{:S(2)}) collective-permute-start(bf16[272,256]{1,0:T(8,128)(2,1)S(1)} %collective-permute-done.2.refs_4_), channel_id=1, source_target_pairs={{0,1},{1,0},{2,3},{3,2},{4,5},{5,4},{6,7},{7,6},{8,9},{9,8},{10,11... | collective-permute-start | bytes 417800 | tf_op jit(solution)/shard_map/ppermute | solution.py:302
  12.1 11.4 %collective-permute-start.12 = (bf16[384,256]{1,0:T(8,128)(2,1)S(1)}, bf16[384,256]{1,0:T(8,128)(2,1)S(1)}, u32[]{:S(2)}, u32[]{:S(2)}) collective-permute-start(bf16[384,256]{1,0:T(8,128)(2,1)S(1)} %get-tuple-element.64.refs_0_), channel_id=1, source_target_pairs={{0,3},{1,2},{2,1},{3,0},{4,7},{5,6},{6,5},{7,4},{8,11},{9,10},{10,... | collective-permute-start | bytes 589832 | tf_op jit(solution)/shard_map/ppermute | solution.py:358
  14.4 9.1 %collective-permute-start.11 = (bf16[384,256]{1,0:T(8,128)(2,1)S(1)}, bf16[384,256]{1,0:T(8,128)(2,1)S(1)}, u32[]{:S(2)}, u32[]{:S(2)}) collective-permute-start(bf16[384,256]{1,0:T(8,128)(2,1)S(1)} %get-tuple-element.64.refs_0_), channel_id=1, source_target_pairs={{0,1},{1,0},{2,3},{3,2},{4,5},{5,4},{6,7},{7,6},{8,9},{9,8},{10,11... | collective-permute-start | bytes 589832 | tf_op jit(solution)/shard_map/ppermute | solution.py:302
  14.4 9.1 %collective-permute-start.10 = (bf16[384,256]{1,0:T(8,128)(2,1)S(1)}, bf16[384,256]{1,0:T(8,128)(2,1)S(1)}, u32[]{:S(2)}, u32[]{:S(2)}) collective-permute-start(bf16[384,256]{1,0:T(8,128)(2,1)S(1)} %get-tuple-element.64.refs_0_), channel_id=1, source_target_pairs={{0,2},{2,0},{1,3},{3,1},{4,6},{6,4},{5,7},{7,5},{8,10},{10,8},{9,1... | collective-permute-start | bytes 589832 | tf_op jit(solution)/shard_map/ppermute | solution.py:348
  15.0 2.1 %collective-permute-start.6 = (bf16[384,256]{1,0:T(8,128)(2,1)S(1)}, bf16[384,256]{1,0:T(8,128)(2,1)S(1)}, u32[]{:S(2)}, u32[]{:S(2)}) collective-permute-start(bf16[384,256]{1,0:T(8,128)(2,1)S(1)} %get-tuple-element.53.refs_0_), channel_id=1, source_target_pairs={{0,1},{1,0},{2,3},{3,2},{4,5},{5,4},{6,7},{7,6},{8,9},{9,8},{10,11... | collective-permute-start | bytes 589832 | tf_op jit(solution)/shard_map/ppermute | solution.py:302
  15.2 1.8 %collective-permute-start.7 = (bf16[384,256]{1,0:T(8,128)(2,1)S(1)}, bf16[384,256]{1,0:T(8,128)(2,1)S(1)}, u32[]{:S(2)}, u32[]{:S(2)}) collective-permute-start(bf16[384,256]{1,0:T(8,128)(2,1)S(1)} %collective-permute-done.5.refs_7_.refs_1_), channel_id=1, source_target_pairs={{0,1},{1,0},{2,3},{3,2},{4,5},{5,4},{6,7},{7,6},{8,9},{9,8},{10,11... | collective-permute-start | bytes 589832 | tf_op jit(solution)/shard_map/ppermute | solution.py:302
  18.4 6.7 %collective-permute-start.8 = (bf16[128,256]{1,0:T(8,128)(2,1)S(1)}, bf16[128,256]{1,0:T(8,128)(2,1)S(1)}, u32[]{:S(2)}, u32[]{:S(2)}) collective-permute-start(bf16[128,256]{1,0:T(8,128)(2,1)S(1)} %get-tuple-element.59), channel_id=1, source_target_pairs={{0,8},{4,12},{8,0},{12,4},{1,9},{5,13},{9,1},{13,5},{2,10},{6,14},... | collective-permute-start | bytes 196616 | tf_op jit(solution)/shard_map/ppermute | solution.py:305
  20.2 5.1 %collective-permute-start.9 = (bf16[128,256]{1,0:T(8,128)(2,1)S(1)}, bf16[128,256]{1,0:T(8,128)(2,1)S(1)}, u32[]{:S(2)}, u32[]{:S(2)}) collective-permute-start(bf16[128,256]{1,0:T(8,128)(2,1)S(1)} %get-tuple-element.60), channel_id=1, source_target_pairs={{0,4},{4,0},{8,12},{12,8},{1,5},{5,1},{9,13},{13,9},{2,6},{6,2},{1... | collective-permute-start | bytes 196616 | tf_op jit(solution)/shard_map/ppermute | solution.py:305
  26.4 5.3 %collective-permute-start.13 = (bf16[128,256]{1,0:T(8,128)(2,1)S(1)}, bf16[128,256]{1,0:T(8,128)(2,1)S(1)}, u32[]{:S(2)}, u32[]{:S(2)}) collective-permute-start(bf16[128,256]{1,0:T(8,128)(2,1)S(1)} %get-tuple-element.67), channel_id=1, source_target_pairs={{0,8},{4,12},{8,0},{12,4},{1,9},{5,13},{9,1},{13,5},{2,10},{6,14},... | collective-permute-start | bytes 196616 | tf_op jit(solution)/shard_map/ppermute | solution.py:305
  27.5 4.8 %collective-permute-start.14 = (bf16[128,256]{1,0:T(8,128)(2,1)S(1)}, bf16[128,256]{1,0:T(8,128)(2,1)S(1)}, u32[]{:S(2)}, u32[]{:S(2)}) collective-permute-start(bf16[128,256]{1,0:T(8,128)(2,1)S(1)} %get-tuple-element.68), channel_id=1, source_target_pairs={{0,4},{4,0},{8,12},{12,8},{1,5},{5,1},{9,13},{13,9},{2,6},{6,2},{1... | collective-permute-start | bytes 196616 | tf_op jit(solution)/shard_map/ppermute | solution.py:305
  33.4 5.2 %collective-permute-start.15 = (bf16[128,256]{1,0:T(8,128)(2,1)S(1)}, bf16[128,256]{1,0:T(8,128)(2,1)S(1)}, u32[]{:S(2)}, u32[]{:S(2)}) collective-permute-start(bf16[128,256]{1,0:T(8,128)(2,1)S(1)} %get-tuple-element.73), channel_id=1, source_target_pairs={{0,8},{4,12},{8,0},{12,4},{1,9},{5,13},{9,1},{13,5},{2,10},{6,14},... | collective-permute-start | bytes 196616 | tf_op jit(solution)/shard_map/ppermute | solution.py:305
  35.0 4.4 %collective-permute-start.16 = (bf16[128,256]{1,0:T(8,128)(2,1)S(1)}, bf16[128,256]{1,0:T(8,128)(2,1)S(1)}, u32[]{:S(2)}, u32[]{:S(2)}) collective-permute-start(bf16[128,256]{1,0:T(8,128)(2,1)S(1)} %get-tuple-element.74), channel_id=1, source_target_pairs={{0,4},{4,0},{8,12},{12,8},{1,5},{5,1},{9,13},{13,9},{2,6},{6,2},{1... | collective-permute-start | bytes 196616 | tf_op jit(solution)/shard_map/ppermute | solution.py:305

commit v7 on v6

--- a/solution.py
+++ b/solution.py
@@ -312,7 +312,7 @@
         pack_kernel,
         [shape((edge_rows(width, held)[0].start, width), BF16)] + [shape((width + half, width), BF16)] * held,
         [*in_hbm(w_edge, w_node_in, w_node_out, *vectors)],
-        1 << 10,
+        1 << 33,
         scratch=[*buffers(*vectors), pltpu.SemaphoreType.DMA((5 + 4 * held,))],
     )
     graph = (cross_src, cross_coef, recv_node)
@@ -326,7 +326,7 @@
             shape((edges // rounds * slots + VECTORS, width), BF16),
         ],
         [*in_hbm(latents, *graph), edge_pack],
-        1 << 10,
+        1 << 28,
         after=1,
         scratch=[*buffers(*graph), pltpu.SemaphoreType.DMA((4,))],
     )
@@ -368,7 +368,7 @@
     node_weights[0] = swaps(node_packs[0], nodes_mine[0], weights[-1])
     for j in range(1, held):
         pack = once(node_packs[j], scatter)
-        node_weights[j] = [node_packs[j], *nodes_mine[j], swap(pack), *crossed(pack)]
+        node_weights[j] = [node_packs[j], *nodes_mine[j], swap(once(node_packs[j], scatter)), *crossed(pack)]
     total = segments * held
     sends = [shape((nodes, width), BF16)] + [shape((slots, width), BF16)] * rounds
     source = latent
@@ -377,9 +377,9 @@
         sums = kernel_call(
             functools.partial(inner_kernel, segments, segment, j, layer == 0),
             shape((nodes, width), F32),
-            [*weights, source, hot, spread, *(() if layer else nodes_mine[0])],
-            1 << 31,
-            after=0 if layer else segments - 1,
+            [*weights, source, hot, spread, *(() if layer else [raw, *nodes_mine[0]])],
+            1 << 31 if layer == 0 else 1 << 31,
+            after=0 if layer else len([raw, *nodes_mine[0]]),
         )
         if layer == 0:
             arrived = kernel_call(
@@ -405,7 +405,7 @@
             operands += [*weights, hot_c, spread_c]
             outs = [shape((nodes, width), BF16), *sends]
         latent, *rest = kernel_call(
-            functools.partial(node_kernel, segments, follow, step, last, rounds), outs, operands, 1 << 30
+            functools.partial(node_kernel, segments, follow, step, last, rounds), outs, operands, 1 << 30 if layer == 0 else 1 << 30
         )
         if not last:
             source, *blocks = rest

time: 41 us -> 41 us (level)
  no operation moved by 1% of the time
where the time goes in v7:
time: 41 us; the launch traced here: 40.7 us
  starting transfers between devices  18.2 us (44%)
  Pallas kernels  14.7 us (36%)
  waiting for transfers between devices  7.67 us (19%)
    pallas_call x16, Pallas kernels, kernel_call(): pl.pallas_call(body, out_shape=outs, in_specs=[HBM if scratch else VMEM]...  14.7 us
    ppermute x6, starting transfers between devices, exchange(): lax.ppermute(block, 'dom', partner_route(parts, r))  10.8 us
    ppermute x6, waiting for transfers between devices, exchange(): lax.ppermute(block, 'dom', partner_route(parts, r))  4.17 us
    ppermute x3, starting transfers between devices, spread_out(): return [lax.ppermute(pack, 'segment', route) for route in routes]  4.08 us
    ppermute x3, waiting for transfers between devices, spread_out(): return [lax.ppermute(pack, 'segment', route) for route in routes]  1.86 us
    ppermute x1, starting transfers between devices, per_device(): raw = lax.ppermute(raw, ('dom', 'chan'), route)  1.64 us
    ppermute x1, waiting for transfers between devices, per_device(): raw = lax.ppermute(raw, ('dom', 'chan'), route)  1.62 us
    ppermute x6, starting transfers between devices, swap(): return lax.ppermute(block, 'chan', [(0, 1), (1, 0)])  1.22 us
  transfers between devices with their start and end apart: 17, of which 8 were waited for; matrix products, arithmetic and copies ran while one was open for 0% of the time, Pallas kernels for 24%

profile of v7, /device:TPU:0, one launch (start us, length us, event | category | flops | bytes accessed | tf_op | source)
XLA Modules:
  0.0 40.7 jit_solution(2891472340640506814)
XLA Ops:
  0.0 1.3 %shard_map.136 = (bf16[288,256]{1,0:T(8,128)(2,1)S(1)}, bf16[384,256]{1,0:T(8,128)(2,1)S(1)}, bf16[384,256]{1,0:T(8,128)(2,1)S(1)}) custom-call(bf16[2,256,256]{2,1,0:T(8,128)(2,1)} %w_edge.1, bf16[2,512,128]{2,1,0:T(8,128)(2,1)} %w_in.1, bf16[2,128,256]{2,1,0:T(8,128)(2,1)} %w_out.1, bf16[2,256]{1,0:T(2,128)(2,1)} %e_bias.1, bf16[2,256]{1,0:T(2,128)(2,1)} %e_gain.1, ...), custom_call_target="tpu_custom_call" | custom-call | flops 8589934592 | bytes 65536 | tf_op jit(solution)/shard_map/pallas_call | solution.py:24
  1.3 3.0 %collective-permute-start = (bf16[288,256]{1,0:T(8,128)(2,1)S(1)}, bf16[288,256]{1,0:T(8,128)(2,1)S(1)}, u32[]{:S(2)}, u32[]{:S(2)}) collective-permute-start(bf16[288,256]{1,0:T(8,128)(2,1)S(1)} %get-tuple-element.44._.refs_0_.refs_4_.refs_7_), channel_id=1, source_target_pairs={{0,2},{2,0},{1,3},{3,1},{4,6},{6,4},{5,7},{7,5},{8,10},{10,8},{9,1... | collective-permute-start | bytes 442376 | tf_op jit(solution)/shard_map/ppermute | solution.py:348
  4.3 1.4 %shard_map.137 = (bf16[512,256]{1,0:T(8,128)(2,1)S(1)}, bf16[512,512]{1,0:T(8,128)(2,1)S(1)}, f32[512,128]{1,0:T(8,128)S(1)}, bf16[512,256]{1,0:T(8,128)(2,1)S(1)}, bf16[272,256]{1,0:T(8,128)(2,1)S(1)}) custom-call(bf16[2,512,256]{2,1,0:T(8,128)(2,1)} %latents.1, s32[2,2,128]{2,1,0:T(2,128)} %src.1, f32[2,2,128]{2,1,0:T(2,128)} %coef.2, s32[2,128]{1,0:T(2,128)} %recv.1, ...), custom_call_target="tpu_custom_call" | custom-call | flops 268435456 | bytes 65536 | tf_op jit(solution)/shard_map/pallas_call | solution.py:24
  5.7 1.6 %collective-permute-start.2 = (bf16[272,256]{1,0:T(8,128)(2,1)S(1)}, bf16[272,256]{1,0:T(8,128)(2,1)S(1)}, u32[]{:S(2)}, u32[]{:S(2)}) collective-permute-start(bf16[272,256]{1,0:T(8,128)(2,1)S(1)} %get-tuple-element.45), channel_id=1, source_target_pairs={{0,4},{4,0},{8,12},{12,8},{1,9},{5,13},{9,1},{13,5},{2,6},{6,2},{1... | collective-permute-start | bytes 417800 | tf_op jit(solution)/shard_map/ppermute | solution.py:336
  7.3 0.5 %collective-permute-start.5 = (bf16[384,256]{1,0:T(8,128)(2,1)S(1)}, bf16[384,256]{1,0:T(8,128)(2,1)S(1)}, u32[]{:S(2)}, u32[]{:S(2)}) collective-permute-start(bf16[384,256]{1,0:T(8,128)(2,1)S(1)} %get-tuple-element.53.refs_0_), channel_id=1, source_target_pairs={{0,2},{2,0},{1,3},{3,1},{4,6},{6,4},{5,7},{7,5},{8,10},{10,8},{9,1... | collective-permute-start | bytes 589832 | tf_op jit(solution)/shard_map/ppermute | solution.py:348
  7.9 1.9 %shard_map.138 = (bf16[3072,512]{1,0:T(8,128)(2,1)S(1)}, f32[3072,128]{1,0:T(8,128)S(1)}) custom-call(s32[6,512]{1,0:T(8,128)} %neighbors.1, f32[6,512]{1,0:T(8,128)} %coef.3, bf16[512,256]{1,0:T(8,128)(2,1)S(1)} %get-tuple-element.43._.refs_6_), custom_call_target="tpu_custom_call" | custom-call | flops 1073741824 | bytes 65536 | tf_op jit(solution)/shard_map/pallas_call | solution.py:24
  9.8 1.6 %collective-permute-done.2.refs_4_.refs_7_ = bf16[272,256]{1,0:T(8,128)(2,1)S(1)} collective-permute-done((bf16[272,256]{1,0:T(8,128)(2,1)S(1)}, bf16[272,256]{1,0:T(8,128)(2,1)S(1)}, u32[]{:S(2)}, u32[]{:S(2)}) %collective-permute-start.2) | collective-permute-done | bytes 139296 | tf_op jit(solution)/shard_map/ppermute | solution.py:336
  11.6 0.3 collective-permute-start.1
  12.1 0.5 %collective-permute-start.12 = (bf16[384,256]{1,0:T(8,128)(2,1)S(1)}, bf16[384,256]{1,0:T(8,128)(2,1)S(1)}, u32[]{:S(2)}, u32[]{:S(2)}) collective-permute-start(bf16[384,256]{1,0:T(8,128)(2,1)S(1)} %get-tuple-element.64.refs_0_), channel_id=1, source_target_pairs={{0,3},{1,2},{2,1},{3,0},{4,7},{5,6},{6,5},{7,4},{8,11},{9,10},{10,... | collective-permute-start | bytes 589832 | tf_op jit(solution)/shard_map/ppermute | solution.py:358
  12.6 1.9 %collective-permute-done.5.refs_8_.refs_1_ = bf16[384,256]{1,0:T(8,128)(2,1)S(1)} collective-permute-done((bf16[384,256]{1,0:T(8,128)(2,1)S(1)}, bf16[384,256]{1,0:T(8,128)(2,1)S(1)}, u32[]{:S(2)}, u32[]{:S(2)}) %collective-permute-start.5) | collective-permute-done | bytes 196640 | tf_op jit(solution)/shard_map/ppermute | solution.py:348
  14.4 0.5 %collective-permute-start.10 = (bf16[384,256]{1,0:T(8,128)(2,1)S(1)}, bf16[384,256]{1,0:T(8,128)(2,1)S(1)}, u32[]{:S(2)}, u32[]{:S(2)}) collective-permute-start(bf16[384,256]{1,0:T(8,128)(2,1)S(1)} %get-tuple-element.64.refs_0_), channel_id=1, source_target_pairs={{0,2},{2,0},{1,3},{3,1},{4,6},{6,4},{5,7},{7,5},{8,10},{10,8},{9,1... | collective-permute-start | bytes 589832 | tf_op jit(solution)/shard_map/ppermute | solution.py:348
  15.2 0.3 collective-permute-start.7
  15.5 0.3 shard_map.139
  15.8 1.2 %shard_map.140.refs_3_ = f32[512,256]{1,0:T(8,128)S(1)} custom-call(bf16[288,256]{1,0:T(8,128)(2,1)S(1)} %get-tuple-element.44._.refs_0_.refs_4_.refs_7_, bf16[288,256]{1,0:T(8,128)(2,1)S(1)} %collective-permute-done.refs_1_.refs_5_.refs_8_, bf16[288,256]{1,0:T(8,128)(2,1)S(1)} %collective-permute-done.1.refs_2_.refs_6_.refs_9_, ...), custom_call_target="tpu_custom_call" | custom-call | flops 2147483648 | bytes 65536 | tf_op jit(solution)/shard_map/pallas_call | solution.py:24
  17.3 1.1 %shard_map.142 = (bf16[512,256]{1,0:T(8,128)(2,1)S(1)}, bf16[512,256]{1,0:T(8,128)(2,1)S(1)}, bf16[128,256]{1,0:T(8,128)(2,1)S(1)}, bf16[128,256]{1,0:T(8,128)(2,1)S(1)}) custom-call(bf16[128,256]{1,0:T(8,128)(2,1)S(1)} %get-tuple-element.48.refs_0_, bf16[128,256]{1,0:T(8,128)(2,1)S(1)} %get-tuple-element.49.refs_1_, ...), custom_call_target="tpu_custom_call" | custom-call | flops 1073741824 | bytes 65536 | tf_op jit(solution)/shard_map/pallas_call | solution.py:24
  18.4 1.8 %collective-permute-start.8 = (bf16[128,256]{1,0:T(8,128)(2,1)S(1)}, bf16[128,256]{1,0:T(8,128)(2,1)S(1)}, u32[]{:S(2)}, u32[]{:S(2)}) collective-permute-start(bf16[128,256]{1,0:T(8,128)(2,1)S(1)} %get-tuple-element.59), channel_id=1, source_target_pairs={{0,8},{4,12},{8,0},{12,4},{1,9},{5,13},{9,1},{13,5},{2,10},{6,14},... | collective-permute-start | bytes 196616 | tf_op jit(solution)/shard_map/ppermute | solution.py:305
  20.2 2.4 %collective-permute-start.9 = (bf16[128,256]{1,0:T(8,128)(2,1)S(1)}, bf16[128,256]{1,0:T(8,128)(2,1)S(1)}, u32[]{:S(2)}, u32[]{:S(2)}) collective-permute-start(bf16[128,256]{1,0:T(8,128)(2,1)S(1)} %get-tuple-element.60), channel_id=1, source_target_pairs={{0,4},{4,0},{8,12},{12,8},{1,5},{5,1},{9,13},{13,9},{2,6},{6,2},{1... | collective-permute-start | bytes 196616 | tf_op jit(solution)/shard_map/ppermute | solution.py:305
  22.6 1.0 %shard_map.143.refs_3_ = f32[512,256]{1,0:T(8,128)S(1)} custom-call(bf16[288,256]{1,0:T(8,128)(2,1)S(1)} %get-tuple-element.44._.refs_0_.refs_4_.refs_7_, bf16[288,256]{1,0:T(8,128)(2,1)S(1)} %collective-permute-done.refs_1_.refs_5_.refs_8_, bf16[288,256]{1,0:T(8,128)(2,1)S(1)} %collective-permute-done.1.refs_2_.refs_6_.refs_9_, ...), custom_call_target="tpu_custom_call" | custom-call | flops 2147483648 | bytes 65536 | tf_op jit(solution)/shard_map/pallas_call | solution.py:24
  23.9 1.3 %collective-permute-done.8.refs_0_ = bf16[128,256]{1,0:T(8,128)(2,1)S(1)} collective-permute-done((bf16[128,256]{1,0:T(8,128)(2,1)S(1)}, bf16[128,256]{1,0:T(8,128)(2,1)S(1)}, u32[]{:S(2)}, u32[]{:S(2)}) %collective-permute-start.8) | collective-permute-done | bytes 65568 | tf_op jit(solution)/shard_map/ppermute | solution.py:305
  25.3 1.1 %shard_map.145 = (bf16[512,256]{1,0:T(8,128)(2,1)S(1)}, bf16[512,256]{1,0:T(8,128)(2,1)S(1)}, bf16[128,256]{1,0:T(8,128)(2,1)S(1)}, bf16[128,256]{1,0:T(8,128)(2,1)S(1)}) custom-call(bf16[128,256]{1,0:T(8,128)(2,1)S(1)} %collective-permute-done.8.refs_0_, bf16[128,256]{1,0:T(8,128)(2,1)S(1)} %collective-permute-done.9.refs_1_, ...), custom_call_target="tpu_custom_call" | custom-call | flops 1073741824 | bytes 65536 | tf_op jit(solution)/shard_map/pallas_call | solution.py:24
  26.4 1.1 %collective-permute-start.13 = (bf16[128,256]{1,0:T(8,128)(2,1)S(1)}, bf16[128,256]{1,0:T(8,128)(2,1)S(1)}, u32[]{:S(2)}, u32[]{:S(2)}) collective-permute-start(bf16[128,256]{1,0:T(8,128)(2,1)S(1)} %get-tuple-element.67), channel_id=1, source_target_pairs={{0,8},{4,12},{8,0},{12,4},{1,9},{5,13},{9,1},{13,5},{2,10},{6,14},... | collective-permute-start | bytes 196616 | tf_op jit(solution)/shard_map/ppermute | solution.py:305
  27.6 2.1 %collective-permute-start.14 = (bf16[128,256]{1,0:T(8,128)(2,1)S(1)}, bf16[128,256]{1,0:T(8,128)(2,1)S(1)}, u32[]{:S(2)}, u32[]{:S(2)}) collective-permute-start(bf16[128,256]{1,0:T(8,128)(2,1)S(1)} %get-tuple-element.68), channel_id=1, source_target_pairs={{0,4},{4,0},{8,12},{12,8},{1,5},{5,1},{9,13},{13,9},{2,6},{6,2},{1... | collective-permute-start | bytes 196616 | tf_op jit(solution)/shard_map/ppermute | solution.py:305
  29.7 1.0 %shard_map.146.refs_3_ = f32[512,256]{1,0:T(8,128)S(1)} custom-call(bf16[288,256]{1,0:T(8,128)(2,1)S(1)} %get-tuple-element.44._.refs_0_.refs_4_.refs_7_, bf16[288,256]{1,0:T(8,128)(2,1)S(1)} %collective-permute-done.refs_1_.refs_5_.refs_8_, bf16[288,256]{1,0:T(8,128)(2,1)S(1)} %collective-permute-done.1.refs_2_.refs_6_.refs_9_, ...), custom_call_target="tpu_custom_call" | custom-call | flops 2147483648 | bytes 65536 | tf_op jit(solution)/shard_map/pallas_call | solution.py:24
  30.9 0.8 %collective-permute-done.13.refs_0_ = bf16[128,256]{1,0:T(8,128)(2,1)S(1)} collective-permute-done((bf16[128,256]{1,0:T(8,128)(2,1)S(1)}, bf16[128,256]{1,0:T(8,128)(2,1)S(1)}, u32[]{:S(2)}, u32[]{:S(2)}) %collective-permute-start.13) | collective-permute-done | bytes 65568 | tf_op jit(solution)/shard_map/ppermute | solution.py:305
  31.7 0.7 %collective-permute-done.14.refs_1_ = bf16[128,256]{1,0:T(8,128)(2,1)S(1)} collective-permute-done((bf16[128,256]{1,0:T(8,128)(2,1)S(1)}, bf16[128,256]{1,0:T(8,128)(2,1)S(1)}, u32[]{:S(2)}, u32[]{:S(2)}) %collective-permute-start.14) | collective-permute-done | bytes 65568 | tf_op jit(solution)/shard_map/ppermute | solution.py:305
  32.4 1.1 %shard_map.148 = (bf16[512,256]{1,0:T(8,128)(2,1)S(1)}, bf16[512,256]{1,0:T(8,128)(2,1)S(1)}, bf16[128,256]{1,0:T(8,128)(2,1)S(1)}, bf16[128,256]{1,0:T(8,128)(2,1)S(1)}) custom-call(bf16[128,256]{1,0:T(8,128)(2,1)S(1)} %collective-permute-done.13.refs_0_, bf16[128,256]{1,0:T(8,128)(2,1)S(1)} %collective-permute-done.14.refs_1_, ...), custom_call_target="tpu_custom_call" | custom-call | flops 1073741824 | bytes 65536 | tf_op jit(solution)/shard_map/pallas_call | solution.py:24
  33.5 1.6 %collective-permute-start.15 = (bf16[128,256]{1,0:T(8,128)(2,1)S(1)}, bf16[128,256]{1,0:T(8,128)(2,1)S(1)}, u32[]{:S(2)}, u32[]{:S(2)}) collective-permute-start(bf16[128,256]{1,0:T(8,128)(2,1)S(1)} %get-tuple-element.73), channel_id=1, source_target_pairs={{0,8},{4,12},{8,0},{12,4},{1,9},{5,13},{9,1},{13,5},{2,10},{6,14},... | collective-permute-start | bytes 196616 | tf_op jit(solution)/shard_map/ppermute | solution.py:305
  35.0 1.8 %collective-permute-start.16 = (bf16[128,256]{1,0:T(8,128)(2,1)S(1)}, bf16[128,256]{1,0:T(8,128)(2,1)S(1)}, u32[]{:S(2)}, u32[]{:S(2)}) collective-permute-start(bf16[128,256]{1,0:T(8,128)(2,1)S(1)} %get-tuple-element.74), channel_id=1, source_target_pairs={{0,4},{4,0},{8,12},{12,8},{1,5},{5,1},{9,13},{13,9},{2,6},{6,2},{1... | collective-permute-start | bytes 196616 | tf_op jit(solution)/shard_map/ppermute | solution.py:305
  36.9 1.0 %shard_map.149.refs_3_ = f32[512,256]{1,0:T(8,128)S(1)} custom-call(bf16[288,256]{1,0:T(8,128)(2,1)S(1)} %get-tuple-element.44._.refs_0_.refs_4_.refs_7_, bf16[288,256]{1,0:T(8,128)(2,1)S(1)} %collective-permute-done.refs_1_.refs_5_.refs_8_, bf16[288,256]{1,0:T(8,128)(2,1)S(1)} %collective-permute-done.1.refs_2_.refs_6_.refs_9_, ...), custom_call_target="tpu_custom_call" | custom-call | flops 2147483648 | bytes 65536 | tf_op jit(solution)/shard_map/pallas_call | solution.py:24
  38.1 0.6 %collective-permute-done.15.refs_0_ = bf16[128,256]{1,0:T(8,128)(2,1)S(1)} collective-permute-done((bf16[128,256]{1,0:T(8,128)(2,1)S(1)}, bf16[128,256]{1,0:T(8,128)(2,1)S(1)}, u32[]{:S(2)}, u32[]{:S(2)}) %collective-permute-start.15) | collective-permute-done | bytes 65568 | tf_op jit(solution)/shard_map/ppermute | solution.py:305
  38.7 0.7 %collective-permute-done.16.refs_1_ = bf16[128,256]{1,0:T(8,128)(2,1)S(1)} collective-permute-done((bf16[128,256]{1,0:T(8,128)(2,1)S(1)}, bf16[128,256]{1,0:T(8,128)(2,1)S(1)}, u32[]{:S(2)}, u32[]{:S(2)}) %collective-permute-start.16) | collective-permute-done | bytes 65568 | tf_op jit(solution)/shard_map/ppermute | solution.py:305
  39.4 1.3 %shard_map.151 = bf16[1,512,256]{2,1,0:T(8,128)(2,1)} custom-call(bf16[128,256]{1,0:T(8,128)(2,1)S(1)} %collective-permute-done.15.refs_0_, bf16[128,256]{1,0:T(8,128)(2,1)S(1)} %collective-permute-done.16.refs_1_, bf16[512,256]{1,0:T(8,128)(2,1)S(1)} %get-tuple-element.75.refs_8_.refs_2_, f32[512,256]{1,0:T(8,128)S(1)} %shard_map.149.refs_3_, ...), custom_call_target="tpu_custom_call" | custom-call | flops 1073741824 | bytes 65536 | tf_op jit(solution)/shard_map/pallas_call | solution.py:24
  (18 shorter events, 1.8 us)
Async XLA Ops:
  1.3 10.2 %collective-permute-start = (bf16[288,256]{1,0:T(8,128)(2,1)S(1)}, bf16[288,256]{1,0:T(8,128)(2,1)S(1)}, u32[]{:S(2)}, u32[]{:S(2)}) collective-permute-start(bf16[288,256]{1,0:T(8,128)(2,1)S(1)} %get-tuple-element.44._.refs_0_.refs_4_.refs_7_), channel_id=1, source_target_pairs={{0,2},{2,0},{1,3},{3,1},{4,6},{6,4},{5,7},{7,5},{8,10},{10,8},{9,1... | collective-permute-start | bytes 442376 | tf_op jit(solution)/shard_map/ppermute | solution.py:348
  5.7 5.7 %collective-permute-start.2 = (bf16[272,256]{1,0:T(8,128)(2,1)S(1)}, bf16[272,256]{1,0:T(8,128)(2,1)S(1)}, u32[]{:S(2)}, u32[]{:S(2)}) collective-permute-start(bf16[272,256]{1,0:T(8,128)(2,1)S(1)} %get-tuple-element.45), channel_id=1, source_target_pairs={{0,4},{4,0},{8,12},{12,8},{1,9},{5,13},{9,1},{13,5},{2,6},{6,2},{1... | collective-permute-start | bytes 417800 | tf_op jit(solution)/shard_map/ppermute | solution.py:336
  7.3 7.1 %collective-permute-start.5 = (bf16[384,256]{1,0:T(8,128)(2,1)S(1)}, bf16[384,256]{1,0:T(8,128)(2,1)S(1)}, u32[]{:S(2)}, u32[]{:S(2)}) collective-permute-start(bf16[384,256]{1,0:T(8,128)(2,1)S(1)} %get-tuple-element.53.refs_0_), channel_id=1, source_target_pairs={{0,2},{2,0},{1,3},{3,1},{4,6},{6,4},{5,7},{7,5},{8,10},{10,8},{9,1... | collective-permute-start | bytes 589832 | tf_op jit(solution)/shard_map/ppermute | solution.py:348
  11.4 3.0 %collective-permute-start.3 = (bf16[288,256]{1,0:T(8,128)(2,1)S(1)}, bf16[288,256]{1,0:T(8,128)(2,1)S(1)}, u32[]{:S(2)}, u32[]{:S(2)}) collective-permute-start(bf16[288,256]{1,0:T(8,128)(2,1)S(1)} %collective-permute-done.refs_1_.refs_5_.refs_8_), channel_id=1, source_target_pairs={{0,1},{1,0},{2,3},{3,2},{4,5},{5,4},{6,7},{7,6},{8,9},{9,8},{10,11... | collective-permute-start | bytes 442376 | tf_op jit(solution)/shard_map/ppermute | solution.py:302
  11.6 3.4 %collective-permute-start.1 = (bf16[288,256]{1,0:T(8,128)(2,1)S(1)}, bf16[288,256]{1,0:T(8,128)(2,1)S(1)}, u32[]{:S(2)}, u32[]{:S(2)}) collective-permute-start(bf16[288,256]{1,0:T(8,128)(2,1)S(1)} %get-tuple-element.44._.refs_0_.refs_4_.refs_7_), channel_id=1, source_target_pairs={{0,1},{1,0},{2,3},{3,2},{4,5},{5,4},{6,7},{7,6},{8,9},{9,8},{10,11... | collective-permute-start | bytes 442376 | tf_op jit(solution)/shard_map/ppermute | solution.py:302
  11.9 3.3 %collective-permute-start.4 = (bf16[272,256]{1,0:T(8,128)(2,1)S(1)}, bf16[272,256]{1,0:T(8,128)(2,1)S(1)}, u32[]{:S(2)}, u32[]{:S(2)}) collective-permute-start(bf16[272,256]{1,0:T(8,128)(2,1)S(1)} %collective-permute-done.2.refs_4_.refs_7_), channel_id=1, source_target_pairs={{0,1},{1,0},{2,3},{3,2},{4,5},{5,4},{6,7},{7,6},{8,9},{9,8},{10,11... | collective-permute-start | bytes 417800 | tf_op jit(solution)/shard_map/ppermute | solution.py:302
  12.1 11.5 %collective-permute-start.12 = (bf16[384,256]{1,0:T(8,128)(2,1)S(1)}, bf16[384,256]{1,0:T(8,128)(2,1)S(1)}, u32[]{:S(2)}, u32[]{:S(2)}) collective-permute-start(bf16[384,256]{1,0:T(8,128)(2,1)S(1)} %get-tuple-element.64.refs_0_), channel_id=1, source_target_pairs={{0,3},{1,2},{2,1},{3,0},{4,7},{5,6},{6,5},{7,4},{8,11},{9,10},{10,... | collective-permute-start | bytes 589832 | tf_op jit(solution)/shard_map/ppermute | solution.py:358
  14.4 9.2 %collective-permute-start.11 = (bf16[384,256]{1,0:T(8,128)(2,1)S(1)}, bf16[384,256]{1,0:T(8,128)(2,1)S(1)}, u32[]{:S(2)}, u32[]{:S(2)}) collective-permute-start(bf16[384,256]{1,0:T(8,128)(2,1)S(1)} %get-tuple-element.64.refs_0_), channel_id=1, source_target_pairs={{0,1},{1,0},{2,3},{3,2},{4,5},{5,4},{6,7},{7,6},{8,9},{9,8},{10,11... | collective-permute-start | bytes 589832 | tf_op jit(solution)/shard_map/ppermute | solution.py:302
  14.4 9.2 %collective-permute-start.10 = (bf16[384,256]{1,0:T(8,128)(2,1)S(1)}, bf16[384,256]{1,0:T(8,128)(2,1)S(1)}, u32[]{:S(2)}, u32[]{:S(2)}) collective-permute-start(bf16[384,256]{1,0:T(8,128)(2,1)S(1)} %get-tuple-element.64.refs_0_), channel_id=1, source_target_pairs={{0,2},{2,0},{1,3},{3,1},{4,6},{6,4},{5,7},{7,5},{8,10},{10,8},{9,1... | collective-permute-start | bytes 589832 | tf_op jit(solution)/shard_map/ppermute | solution.py:348
  15.0 2.1 %collective-permute-start.6 = (bf16[384,256]{1,0:T(8,128)(2,1)S(1)}, bf16[384,256]{1,0:T(8,128)(2,1)S(1)}, u32[]{:S(2)}, u32[]{:S(2)}) collective-permute-start(bf16[384,256]{1,0:T(8,128)(2,1)S(1)} %get-tuple-element.53.refs_0_), channel_id=1, source_target_pairs={{0,1},{1,0},{2,3},{3,2},{4,5},{5,4},{6,7},{7,6},{8,9},{9,8},{10,11... | collective-permute-start | bytes 589832 | tf_op jit(solution)/shard_map/ppermute | solution.py:302
  15.2 1.9 %collective-permute-start.7 = (bf16[384,256]{1,0:T(8,128)(2,1)S(1)}, bf16[384,256]{1,0:T(8,128)(2,1)S(1)}, u32[]{:S(2)}, u32[]{:S(2)}) collective-permute-start(bf16[384,256]{1,0:T(8,128)(2,1)S(1)} %collective-permute-done.5.refs_8_.refs_1_), channel_id=1, source_target_pairs={{0,1},{1,0},{2,3},{3,2},{4,5},{5,4},{6,7},{7,6},{8,9},{9,8},{10,11... | collective-permute-start | bytes 589832 | tf_op jit(solution)/shard_map/ppermute | solution.py:302
  18.4 6.7 %collective-permute-start.8 = (bf16[128,256]{1,0:T(8,128)(2,1)S(1)}, bf16[128,256]{1,0:T(8,128)(2,1)S(1)}, u32[]{:S(2)}, u32[]{:S(2)}) collective-permute-start(bf16[128,256]{1,0:T(8,128)(2,1)S(1)} %get-tuple-element.59), channel_id=1, source_target_pairs={{0,8},{4,12},{8,0},{12,4},{1,9},{5,13},{9,1},{13,5},{2,10},{6,14},... | collective-permute-start | bytes 196616 | tf_op jit(solution)/shard_map/ppermute | solution.py:305
  20.2 5.1 %collective-permute-start.9 = (bf16[128,256]{1,0:T(8,128)(2,1)S(1)}, bf16[128,256]{1,0:T(8,128)(2,1)S(1)}, u32[]{:S(2)}, u32[]{:S(2)}) collective-permute-start(bf16[128,256]{1,0:T(8,128)(2,1)S(1)} %get-tuple-element.60), channel_id=1, source_target_pairs={{0,4},{4,0},{8,12},{12,8},{1,5},{5,1},{9,13},{13,9},{2,6},{6,2},{1... | collective-permute-start | bytes 196616 | tf_op jit(solution)/shard_map/ppermute | solution.py:305
  26.4 5.3 %collective-permute-start.13 = (bf16[128,256]{1,0:T(8,128)(2,1)S(1)}, bf16[128,256]{1,0:T(8,128)(2,1)S(1)}, u32[]{:S(2)}, u32[]{:S(2)}) collective-permute-start(bf16[128,256]{1,0:T(8,128)(2,1)S(1)} %get-tuple-element.67), channel_id=1, source_target_pairs={{0,8},{4,12},{8,0},{12,4},{1,9},{5,13},{9,1},{13,5},{2,10},{6,14},... | collective-permute-start | bytes 196616 | tf_op jit(solution)/shard_map/ppermute | solution.py:305
  27.6 4.8 %collective-permute-start.14 = (bf16[128,256]{1,0:T(8,128)(2,1)S(1)}, bf16[128,256]{1,0:T(8,128)(2,1)S(1)}, u32[]{:S(2)}, u32[]{:S(2)}) collective-permute-start(bf16[128,256]{1,0:T(8,128)(2,1)S(1)} %get-tuple-element.68), channel_id=1, source_target_pairs={{0,4},{4,0},{8,12},{12,8},{1,5},{5,1},{9,13},{13,9},{2,6},{6,2},{1... | collective-permute-start | bytes 196616 | tf_op jit(solution)/shard_map/ppermute | solution.py:305
  33.5 5.2 %collective-permute-start.15 = (bf16[128,256]{1,0:T(8,128)(2,1)S(1)}, bf16[128,256]{1,0:T(8,128)(2,1)S(1)}, u32[]{:S(2)}, u32[]{:S(2)}) collective-permute-start(bf16[128,256]{1,0:T(8,128)(2,1)S(1)} %get-tuple-element.73), channel_id=1, source_target_pairs={{0,8},{4,12},{8,0},{12,4},{1,9},{5,13},{9,1},{13,5},{2,10},{6,14},... | collective-permute-start | bytes 196616 | tf_op jit(solution)/shard_map/ppermute | solution.py:305
  35.0 4.4 %collective-permute-start.16 = (bf16[128,256]{1,0:T(8,128)(2,1)S(1)}, bf16[128,256]{1,0:T(8,128)(2,1)S(1)}, u32[]{:S(2)}, u32[]{:S(2)}) collective-permute-start(bf16[128,256]{1,0:T(8,128)(2,1)S(1)} %get-tuple-element.74), channel_id=1, source_target_pairs={{0,4},{4,0},{8,12},{12,8},{1,5},{5,1},{9,13},{13,9},{2,6},{6,2},{1... | collective-permute-start | bytes 196616 | tf_op jit(solution)/shard_map/ppermute | solution.py:305
